TPU v7x, 32 devices: a whole 2x2x4 slice. The times are simulated.
32 devices in a mesh: fsdp: 4 (over y, core), blk: 2 (over x), seq: 4 (over z).
Axes of the slice: x: 2, y: 2, z: 4, core: 2. Of those that a mesh axis runs over, the one named last changes fastest.
Arguments:
- tokens: float32 [4, 1024, 768], P('fsdp', ('blk', 'seq')), may hold values from -6 to 6
- counts: int32 [4, 8], P('fsdp'), may hold values from 1 to 128, 820 in all within a row
- norm_gain: bfloat16 [2, 768], replicated, may hold values from 0.5 to 1.5
- norm_bias: bfloat16 [2, 768], replicated, may hold values from -4 to 4
- vec_bias: bfloat16 [4, 768], replicated, may hold values from -4 to 4
- up_bias: bfloat16 [3072], replicated, may hold values from -6 to 6
- w_qkv: bfloat16 [768, 2304], P('fsdp'), may hold values from -0.3125 to 0.3125
- w_out: bfloat16 [768, 768], P('fsdp'), may hold values from -1.25 to 1.25
- w_up: bfloat16 [768, 3072], P('fsdp'), may hold values from -0.21875 to 0.21875
- w_down: bfloat16 [3072, 768], P('fsdp'), may hold values from -0.109375 to 0.109375
- grad_out: float32 [4, 1024, 768], P('fsdp', ('blk', 'seq')), may hold values from -6 to 6
Outputs:
- activations: float32 [4, 1024, 768], P('fsdp', ('blk', 'seq'))
- grad_tokens: float32 [4, 1024, 768], P('fsdp', ('blk', 'seq'))
- grad_norm_gain: float32 [2, 768], P(None, 'fsdp')
- grad_norm_bias: float32 [2, 768], P(None, 'fsdp')
- grad_vec_bias: float32 [4, 768], P(None, 'fsdp')
- grad_up_bias: float32 [3072], P('fsdp')
- grad_w_qkv: float32 [768, 2304], P('fsdp')
- grad_w_out: float32 [768, 768], P('fsdp')
- grad_w_up: float32 [768, 3072], P('fsdp')
- grad_w_down: float32 [3072, 768], P('fsdp')
Inputs may be any that keep to these rules, and one draw needn't show every extreme that they name: `counts`: row i lists, for the 8 devices that hold image i in order, how many of their 128 slots carry tokens; these come first. A row sums to 820 and holds 128 at least once.
All inputs are finite; a program needn't handle non-finite values.
Results may differ from a plain program's by a relative error of at most 0.02.
Values may be sent and summed in bfloat16 or wider, within the bound.
No kernel may reach another device: no remote copies, remote signals or barrier semaphores. Data moves between devices by JAX's collectives and lax.ppermute only.
A program may use at most 128 MiB of HBM per device.

v0:
```python
import functools

import jax
import jax.numpy as jnp
from jax import lax
from jax.experimental import pallas as pl
from jax.experimental.pallas import tpu as pltpu
from jax.sharding import PartitionSpec as P

HD = 64
EPSILON = 1e-06
MASKED = -1e30
SCALE = HD ** (-0.5)
BF = jnp.bfloat16
F32 = jnp.float32
VMEM_LIMIT = 44 * 1024 * 1024


def dot_nn(left_side, right_side):
    return lax.dot_general(
        left_side, right_side, (((1,), (0,)), ((), ())), preferred_element_type=F32
    )


def dot_nt(left_side, right_side):
    return lax.dot_general(
        left_side, right_side, (((1,), (1,)), ((), ())), preferred_element_type=F32
    )


def dot_tn(left_side, right_side):
    return lax.dot_general(
        left_side, right_side, (((0,), (0,)), ((), ())), preferred_element_type=F32
    )


def swap(array, axis, bits):
    return lax.ppermute(array, axis, [(i, i ^ bits) for i in range(lax.axis_size(axis))])


def from_all(array, axis):
    return [array] + [swap(array, axis, j) for j in range(1, lax.axis_size(axis))]


def doubled(array, axis):
    pieces = {0: array}
    bit = lax.axis_size(axis) // 2
    while bit:
        pieces.update({j | bit: swap(piece, axis, bit) for j, piece in list(pieces.items())})
        bit //= 2
    return [pieces[j] for j in range(lax.axis_size(axis))]


def piece_bias(place_ref, counts_ref, block, pieces, slot_rows):
    row = lax.broadcasted_iota(jnp.int32, (pieces * slot_rows, 1), 0)
    limit = jnp.zeros_like(row)
    for piece in range(pieces):
        held = (place_ref[0] ^ block) * pieces + (place_ref[1] ^ piece)
        end = counts_ref[0, held] + piece * slot_rows
        limit = jnp.where(row >= piece * slot_rows, end, limit)
    return jnp.where(row < limit, 0.0, MASKED)


def own_rows_valid(place_ref, counts_ref, seqs, rows):
    count = counts_ref[0, place_ref[0] * seqs + place_ref[1]]
    return lax.broadcasted_iota(jnp.int32, (rows, 1), 0) < count


def normalised(matrix_rows):
    centre = matrix_rows - jnp.mean(matrix_rows, axis=-1, keepdims=True)
    inverse = lax.rsqrt(jnp.mean(centre * centre, axis=-1, keepdims=True) + EPSILON)
    return centre * inverse, inverse


def norm_back(upstream, unit_rows, inverse, gain_row):
    scaled = upstream * gain_row
    return inverse * (
        scaled
        - jnp.mean(scaled, axis=-1, keepdims=True)
        - unit_rows * jnp.mean(scaled * unit_rows, axis=-1, keepdims=True)
    )


def row_of(ref, index):
    return ref[...].astype(F32)[index : index + 1]


def fetches(pieces, own, first, size, target, sems):
    return [
        pltpu.make_async_copy(
            piece.at[pl.ds(first, size)],
            target.at[pl.ds(pl.multiple_of((own ^ j) * size, 16), size)],
            sems.at[j],
        )
        for j, piece in enumerate(pieces)
    ]


def prepare_kernel(
    seqs, place_ref, counts_ref, tokens_ref, grad_ref, gain_ref, shift_ref, normed_ref, outcome_ref
):
    unit = normalised(tokens_ref[...])[0]
    normed_ref[...] = (unit * row_of(gain_ref, 0) + row_of(shift_ref, 0)).astype(BF)
    valid = own_rows_valid(place_ref, counts_ref, seqs, grad_ref.shape[0])
    outcome_ref[...] = jnp.where(valid, grad_ref[...], 0.0).astype(BF)


def attend_kernel(blocks, heads, pieces, slot_rows, place_ref, counts_ref, q_ref, *refs):
    kv_refs, out_refs, log_ref = refs[:blocks], refs[blocks:-1], refs[-1]
    width = heads * HD
    biases = [piece_bias(place_ref, counts_ref, m, pieces, slot_rows) for m in range(blocks)]
    for head in range(heads):
        low, high = head * HD, (head + 1) * HD
        query = q_ref[:, low:high] * SCALE
        scores = [dot_nt(kv[:, low:high], query) + bias for kv, bias in zip(kv_refs, biases)]
        top = functools.reduce(
            jnp.maximum, [jnp.max(block, axis=0, keepdims=True) for block in scores]
        )
        powers = [jnp.exp(block - top) for block in scores]
        total = sum(jnp.sum(block, axis=0, keepdims=True) for block in powers)
        inverse = 1.0 / total
        result = sum(
            dot_tn((block * inverse).astype(BF), kv[:, width + low : width + high])
            for block, kv in zip(powers, kv_refs)
        ).astype(BF)
        for k, out_ref in enumerate(out_refs):
            out_ref[:, low:high] = result[k * slot_rows : (k + 1) * slot_rows]
        log_ref[head : head + 1, :] = top + jnp.log(total)


def attend_back_kernel(blocks, heads, pieces, slot_rows, place_ref, counts_ref, q_ref, log_ref, *refs):
    d_refs, refs = refs[:pieces], refs[pieces:]
    kv_refs, dq_ref, dkv_refs = refs[:blocks], refs[blocks], refs[blocks + 1 :]
    width = heads * HD
    biases = [piece_bias(place_ref, counts_ref, m, pieces, slot_rows) for m in range(blocks)]
    for head in range(heads):
        low, high = head * HD, (head + 1) * HD
        query = q_ref[:, low:high] * SCALE
        d_out = jnp.concatenate([d_ref[:, low:high] for d_ref in d_refs])
        log_row = log_ref[head : head + 1, :]
        softs, d_softs, delta = [], [], 0.0
        for kv, bias in zip(kv_refs, biases):
            soft = jnp.exp(dot_nt(kv[:, low:high], query) + bias - log_row)
            d_soft = dot_nt(kv[:, width + low : width + high], d_out)
            delta = delta + jnp.sum(soft * d_soft, axis=0, keepdims=True)
            softs.append(soft)
            d_softs.append(d_soft)
        d_query = 0.0
        for kv, dkv, soft, d_soft in zip(kv_refs, dkv_refs, softs, d_softs):
            d_scores = (soft * (d_soft - delta)).astype(BF)
            d_query = d_query + dot_tn(d_scores, kv[:, low:high])
            dkv[:, low:high] = dot_nn(d_scores, query).astype(dkv.dtype)
            dkv[:, width + low : width + high] = dot_nn(soft.astype(BF), d_out).astype(dkv.dtype)
        dq_ref[:, low:high] = (d_query * SCALE).astype(BF)


def project_kernel(owners, seqs, place_ref, *refs):
    pieces, att_refs = refs[:owners], refs[owners : owners + seqs]
    tokens_ref, vec_ref, gain_ref, shift_ref, middle_ref, normed_ref, w_ref, sems = refs[owners + seqs :]
    own_rows, head_width = w_ref.shape[0] // owners, w_ref.shape[0] // seqs
    copies = fetches(pieces, place_ref[2], 0, own_rows, w_ref, sems)
    for copy in copies:
        copy.start()
    middle = tokens_ref[...] + row_of(vec_ref, 2)
    for copy in copies:
        copy.wait()
    for k, att_ref in enumerate(att_refs):
        first = pl.multiple_of((place_ref[1] ^ k) * head_width, 16)
        middle = middle + dot_nn(att_ref[...], w_ref[pl.ds(first, head_width), :])
    middle_ref[...] = middle
    unit = normalised(middle)[0]
    normed_ref[...] = (unit * row_of(gain_ref, 1) + row_of(shift_ref, 1)).astype(BF)


def hidden_kernel(owners, blocks, own_rows, hidden_rows, place_ref, *refs):
    pieces, refs = refs[:owners], refs[owners:]
    normed_refs, outcome_refs, refs = refs[:blocks], refs[blocks : 2 * blocks], refs[2 * blocks :]
    shift_ref, hidden_ref, d_up_ref, sums_ref = refs[:4]
    d_normed_refs, out_refs = refs[4 : 4 + blocks], refs[4 + blocks : 4 + 2 * blocks]
    up_ref, down_ref, sems = refs[4 + 2 * blocks :]
    parts, width = up_ref.shape[0], up_ref.shape[1]
    own = place_ref[2]
    waits = []
    for part in range(parts):
        waits += fetches(
            pieces, own, (1 + part) * own_rows, own_rows, up_ref.at[part], sems.at[part]
        )
    waits += fetches(pieces, own, (1 + parts) * own_rows, hidden_rows, down_ref, sems.at[parts])
    for copy in waits:
        copy.start()
    normed = jnp.concatenate([ref[...] for ref in normed_refs])
    outcome = jnp.concatenate([ref[...] for ref in outcome_refs])
    for copy in waits:
        copy.wait()
    size = min(384, parts * width)
    d_normed, result = 0.0, 0.0
    for first in range(0, parts * width, size):
        part, column = first // width, first % width
        up_weights = up_ref[part, :, column : column + size]
        down_weights = down_ref[first : first + size, :]
        up_proj = dot_nn(normed, up_weights) + shift_ref[:, first : first + size]
        chance = 0.5 * (1.0 + lax.erf(up_proj * (0.5**0.5)))
        hidden = (up_proj * chance).astype(BF)
        slope = chance + up_proj * (jnp.exp(-0.5 * up_proj * up_proj) * 0.3989422804014327)
        d_up = (dot_nt(outcome, down_weights) * slope).astype(BF)
        hidden_ref[:, first : first + size] = hidden
        d_up_ref[:, first : first + size] = d_up
        sums_ref[:, first : first + size] = jnp.sum(d_up.astype(F32), axis=0, keepdims=True)
        d_normed = d_normed + dot_nt(d_up, up_weights)
        result = result + dot_nn(hidden, down_weights)
    rows = normed_refs[0].shape[0]
    for m in range(blocks):
        d_normed_refs[m][...] = d_normed[m * rows : (m + 1) * rows].astype(d_normed_refs[m].dtype)
        out_refs[m][...] = result[m * rows : (m + 1) * rows].astype(out_refs[m].dtype)


def middle_kernel(owners, seqs, blocks, place_ref, counts_ref, *refs):
    pieces, refs = refs[:owners], refs[owners:]
    d_normed_refs, refs = refs[:blocks], refs[blocks:]
    middle_in_ref, grad_ref, gain_ref, d_middle_ref, d_branch_ref, sums_ref = refs[:6]
    head_refs, (w_ref, sems) = refs[6 : 6 + seqs], refs[6 + seqs :]
    own_rows, head_width = w_ref.shape[0] // owners, w_ref.shape[0] // seqs
    copies = fetches(pieces, place_ref[2], 0, own_rows, w_ref, sems)
    for copy in copies:
        copy.start()
    valid = own_rows_valid(place_ref, counts_ref, seqs, grad_ref.shape[0])
    grad_rows = jnp.where(valid, grad_ref[...], 0.0)
    unit, inverse = normalised(middle_in_ref[...])
    upstream = sum(ref[...].astype(F32) for ref in d_normed_refs)
    d_middle = grad_rows + norm_back(upstream, unit, inverse, row_of(gain_ref, 1))
    d_branch = d_middle.astype(BF)
    d_middle_ref[...] = d_middle
    d_branch_ref[...] = d_branch
    for copy in copies:
        copy.wait()
    for k, head_ref in enumerate(head_refs):
        first = pl.multiple_of((place_ref[1] ^ k) * head_width, 16)
        head_ref[...] = dot_nt(d_branch, w_ref[pl.ds(first, head_width), :]).astype(BF)
    rows = (
        upstream * unit,
        upstream,
        d_branch.astype(F32),
        grad_rows.astype(BF).astype(F32),
    )
    for index, one in enumerate(rows):
        sums_ref[index : index + 1, :] = jnp.sum(one, axis=0, keepdims=True)


def grads_kernel(owners, seqs, blocks, own_rows, hidden_rows, place_ref, *refs):
    normed_refs, outcome_refs, refs = refs[:blocks], refs[blocks : 2 * blocks], refs[2 * blocks :]
    hidden_ref, d_up_ref, sent_ref, kept_ref = refs
    width = outcome_refs[0].shape[1]
    parts = d_up_ref.shape[1] // width
    bit = place_ref[2] & 1
    normed = jnp.concatenate([ref[...] for ref in normed_refs])
    outcome = jnp.concatenate([ref[...] for ref in outcome_refs])
    chunk, up_chunk = hidden_rows // seqs, own_rows // seqs
    for owner in range(owners):
        down = dot_tn(hidden_ref[:, owner * hidden_rows : (owner + 1) * hidden_rows], outcome)
        rows_in = normed[:, owner * own_rows : (owner + 1) * own_rows]
        ups = [
            dot_tn(rows_in, d_up_ref[:, part * width : (part + 1) * width]) for part in range(parts)
        ]

        def store(ref, owner=owner, down=down, ups=ups):
            for k in range(seqs):
                ref[owner // 2, k, 0:chunk, :] = down[k * chunk : (k + 1) * chunk].astype(BF)
                for part, up in enumerate(ups):
                    first = chunk + part * up_chunk
                    ref[owner // 2, k, first : first + up_chunk, :] = up[
                        k * up_chunk : (k + 1) * up_chunk
                    ].astype(BF)

        @pl.when(bit == owner % 2)
        def keep():
            store(kept_ref)

        @pl.when(bit != owner % 2)
        def send():
            store(sent_ref)


def first_back_kernel(pieces, *refs):
    part_refs, (tokens_ref, d_middle_ref, gain_ref, out_ref) = refs[:pieces], refs[pieces:]
    upstream = sum(ref[...].astype(F32) for ref in part_refs)
    unit, inverse = normalised(tokens_ref[...])
    out_ref[...] = d_middle_ref[...] + norm_back(upstream, unit, inverse, row_of(gain_ref, 0))


def place_kernel(seqs, blocks, layouts, place_ref, *refs):
    pieces = refs[: blocks * seqs]
    outs = refs[blocks * seqs : -2]
    held, sems = refs[-2:]
    blk, seq = place_ref[0], place_ref[1]
    copies = [
        pltpu.make_async_copy(
            pieces[m * seqs + k],
            held.at[jnp.bitwise_xor(blk, m), jnp.bitwise_xor(seq, k)],
            sems.at[m * seqs + k],
        )
        for m in range(blocks)
        for k in range(seqs)
    ]
    for copy in copies:
        copy.start()
    for copy in copies:
        copy.wait()
    for out, spots in zip(outs, layouts):
        for b in range(blocks):
            for k in range(seqs):
                for top, rows, first, size, row, column in spots(b, k):
                    piece = held[b, k, top : top + rows, first : first + size]
                    out[row : row + rows, column : column + size] = piece.astype(F32)


def run(kernel, label, outs, scalars, remote, arrays, scratch=(), flops=0, powers=0):
    moved = sum(one.size * one.dtype.itemsize for one in (*remote, *arrays))
    moved += sum(one.size * one.dtype.itemsize for one in outs)
    return pl.pallas_call(
        kernel,
        out_shape=tuple(outs),
        in_specs=[pl.BlockSpec(memory_space=pltpu.SMEM)] * len(scalars)
        + [pl.BlockSpec(memory_space=pl.ANY)] * len(remote)
        + [pl.BlockSpec(memory_space=pltpu.VMEM)] * len(arrays),
        out_specs=(pl.BlockSpec(memory_space=pltpu.VMEM),) * len(outs),
        scratch_shapes=list(scratch),
        compiler_params=pltpu.CompilerParams(vmem_limit_bytes=VMEM_LIMIT),
        cost_estimate=pl.CostEstimate(flops=flops, bytes_accessed=moved, transcendentals=powers),
        name=label,
    )(*scalars, *remote, *arrays)


def shape(dims, kind):
    return jax.ShapeDtypeStruct(tuple(dims), kind)


def after(value, *others):
    return lax.optimization_barrier((value, others))[0]


def pick(pairs, axis, index):
    return sum(
        lax.dynamic_index_in_dim(one, index, axis, keepdims=False).astype(F32) for one in pairs
    )


def owner_sums(kept, arrived, own):
    terms, sent = (kept, arrived), None
    bit = 2
    while bit < lax.axis_size("fsdp"):
        terms = tuple(one.reshape(one.shape[0] // 2, 2, *one.shape[1:]) for one in terms)
        high = (own // bit) % 2
        sent = pick(terms, 1, 1 - high).astype(BF)
        terms = (pick(terms, 1, high), swap(sent, "fsdp", bit))
        bit *= 2
    return tuple(one[0] for one in terms), sent


def chunk_sums(terms, axis, index):
    total = pick(terms, 0, index)
    for j in range(1, lax.axis_size(axis)):
        total = total + swap(pick(terms, 0, index ^ j).astype(BF), axis, j).astype(F32)
    return total


def sum_parts(parts, axis):
    return [parts[0]] + [swap(parts[j], axis, j) for j in range(1, len(parts))]


def tree_sum(pieces):
    pieces = [piece.astype(F32) for piece in pieces]
    while len(pieces) > 1:
        pieces = [pieces[i] + pieces[i + 1] for i in range(0, len(pieces), 2)]
    return pieces[0]


def in_order(pieces, index):
    result = []
    for place in range(len(pieces)):
        chosen = pieces[place]
        for other in range(1, len(pieces)):
            chosen = jnp.where(index == other, pieces[place ^ other], chosen)
        result.append(chosen)
    return result


def padded(rows, count, width):
    return jnp.pad(rows, ((0, 0), (0, count - rows.shape[1]), (0, width - rows.shape[2])))


def shards(
    tokens, counts, norm_gain, norm_bias, vec_bias, up_bias, w_qkv, w_out, w_up, w_down, grad_out
):
    owners, blocks, seqs = (lax.axis_size(name) for name in ("fsdp", "blk", "seq"))
    own, blk, seq = (lax.axis_index(name) for name in ("fsdp", "blk", "seq"))
    place = jnp.stack([blk, seq, own]).astype(jnp.int32)
    rows, width = tokens.shape[1:]
    head_width = width // seqs
    own_rows = width // owners
    hidden_rows = w_down.shape[0] // blocks
    hidden_width = hidden_rows * owners
    parts = hidden_width // width
    inputs, grad_in = tokens[0], grad_out[0]
    vmem, dma = pltpu.VMEM, pltpu.SemaphoreType.DMA

    normed1, d_outcome = run(
        functools.partial(prepare_kernel, seqs),
        "prepare",
        [shape((rows, width), BF)] * 2,
        [place, counts],
        [],
        [inputs, grad_in, norm_gain, norm_bias],
    )
    normed1_pieces = from_all(normed1, "seq")
    qkv_late = after(w_qkv, normed1)
    qkv_mine = jnp.concatenate(
        [
            lax.dynamic_slice_in_dim(qkv_late, part * width + seq * head_width, head_width, axis=1)
            for part in range(3)
        ],
        axis=1,
    )
    qkv_pieces = doubled(qkv_mine, "fsdp")
    qkv_full = jnp.concatenate(in_order(qkv_pieces, own))

    up_late, down_late, out_late = after((w_up, w_down, w_out), qkv_mine)
    up_columns = [
        lax.dynamic_slice_in_dim(up_late, (i * blocks + blk) * hidden_rows, hidden_rows, axis=1)
        for i in range(owners)
    ]
    in_part = owners // parts
    weights_mine = jnp.concatenate(
        [out_late]
        + [
            jnp.concatenate(up_columns[part * in_part : (part + 1) * in_part], axis=1)
            for part in range(parts)
        ]
        + [lax.dynamic_slice_in_dim(down_late, blk * hidden_rows, hidden_rows, axis=0)]
    )
    weights = doubled(after(weights_mine, qkv_pieces[owners // 2]), "fsdp")
    outcome_pieces = from_all(after(d_outcome, weights_mine), "blk")
    gain_row, shift_row = norm_gain[0].astype(F32), norm_bias[0].astype(F32)
    biases = vec_bias.astype(F32)
    qkv_shift = jnp.concatenate(
        [
            lax.dynamic_slice_in_dim(biases[0], seq * head_width, head_width),
            jnp.zeros((head_width,), F32),
            lax.dynamic_slice_in_dim(biases[1], seq * head_width, head_width),
        ]
    )
    up_shift = (
        jnp.concatenate(
            [
                lax.dynamic_slice_in_dim(up_bias, (i * blocks + blk) * hidden_rows, hidden_rows)
                for i in range(owners)
            ]
        )
        .astype(F32)
        .reshape(1, hidden_width)
    )

    normed1_all = jnp.concatenate(normed1_pieces)
    key_value = (
        dot_nn(normed1_all, qkv_full[:, head_width:]) + qkv_shift[head_width:]
    ).astype(BF)
    kv_blocks = from_all(key_value, "blk")
    queries = (
        dot_nn(after(normed1_all, key_value), qkv_full[:, :head_width]) + qkv_shift[:head_width]
    ).astype(BF)
    block_rows, heads = seqs * rows, head_width // HD
    powers = block_rows * block_rows * blocks * heads
    *att_out, log_total = run(
        functools.partial(attend_kernel, blocks, heads, seqs, rows),
        "attend",
        [shape((rows, head_width), BF)] * seqs + [shape((heads, block_rows), F32)],
        [place, counts],
        [],
        [queries, *kv_blocks],
        flops=4 * HD * powers,
        powers=powers,
    )
    att_pieces = sum_parts(att_out, "seq")
    middle, normed2 = run(
        functools.partial(project_kernel, owners, seqs),
        "project",
        [shape((rows, width), F32), shape((rows, width), BF)],
        [place],
        weights,
        [*att_pieces, inputs, vec_bias, norm_gain, norm_bias],
        [vmem((width, width), BF), dma((owners,))],
        flops=2 * rows * width * width,
    )

    normed_pieces = from_all(normed2, "blk")
    all_rows = blocks * rows
    row_shapes = [shape((rows, width), F32)] + [shape((rows, width), BF)] * (blocks - 1)
    hidden, d_up, up_sums, *rest = run(
        functools.partial(hidden_kernel, owners, blocks, own_rows, hidden_rows),
        "hidden",
        [shape((all_rows, hidden_width), BF)] * 2
        + [shape((1, hidden_width), F32)]
        + row_shapes * 2,
        [place],
        weights,
        [*normed_pieces, *outcome_pieces, up_shift],
        [
            vmem((parts, width, width), BF),
            vmem((hidden_width, width), BF),
            dma((parts + 1, owners)),
        ],
        flops=8 * all_rows * width * hidden_width,
        powers=2 * all_rows * hidden_width,
    )
    d_normed_parts, result_parts = rest[:blocks], rest[blocks:]
    d_normed_pieces = sum_parts(d_normed_parts, "blk")
    chunk, up_chunk = hidden_rows // seqs, own_rows // seqs
    chunk_rows = chunk + parts * up_chunk
    sent, kept = run(
        functools.partial(grads_kernel, owners, seqs, blocks, own_rows, hidden_rows),
        "grads",
        [shape((owners // 2, seqs, chunk_rows, width), BF)] * 2,
        [place],
        [],
        [*normed_pieces, *outcome_pieces, hidden, d_up],
        flops=4 * all_rows * width * hidden_width,
    )
    arrived = swap(sent, "fsdp", 1)
    d_middle, d_branch, middle_sums, *d_heads = run(
        functools.partial(middle_kernel, owners, seqs, blocks),
        "middle",
        [shape((rows, width), F32), shape((rows, width), BF), shape((4, width), F32)]
        + [shape((rows, head_width), BF)] * seqs,
        [place, counts],
        weights,
        [*after(tuple(d_normed_pieces), sent), middle, grad_in, norm_gain],
        [vmem((width, width), BF), dma((owners,))],
        flops=2 * rows * width * width,
    )
    d_att_pieces = sum_parts(d_heads, "seq")
    own_terms, feed_sent = owner_sums(kept, arrived, own)

    att_late, branch_late = after((tuple(att_pieces), d_branch), *d_heads)
    token_att = jnp.concatenate(in_order(att_late, seq), axis=1)
    early = jnp.concatenate(
        [
            padded(
                middle_sums.reshape(4, owners, own_rows).transpose(1, 0, 2), 4, width
            ),
            padded(
                jnp.where(
                    (jnp.arange(blocks) == blk)[None, :, None],
                    up_sums.reshape(owners, 1, hidden_rows),
                    0.0,
                ).reshape(owners, 1, blocks * hidden_rows),
                12,
                width,
            ),
        ],
        axis=1,
    ).astype(BF)
    out_grads = jnp.concatenate(
        [dot_tn(token_att, branch_late).astype(BF).reshape(owners, own_rows, width), early], axis=1
    )
    out_sums = lax.psum(
        lax.psum_scatter(
            out_grads.reshape(owners * (own_rows + 16), width),
            "fsdp",
            scatter_dimension=0,
            tiled=True,
        ),
        ("blk", "seq"),
    ).astype(F32)

    d_query, d_kv, *d_kv_sent = run(
        functools.partial(attend_back_kernel, blocks, heads, seqs, rows),
        "attend_back",
        [shape((block_rows, head_width), BF), shape((block_rows, 2 * head_width), F32)]
        + [shape((block_rows, 2 * head_width), BF)] * (blocks - 1),
        [after(place, feed_sent), counts],
        [],
        [queries, log_total, *d_att_pieces, *kv_blocks],
        flops=10 * HD * powers,
        powers=powers,
    )
    for m in range(1, blocks):
        d_kv = d_kv + swap(d_kv_sent[m - 1], "blk", m).astype(F32)
    d_kv = after(d_kv.astype(BF), own_terms)
    d_projected = jnp.concatenate([d_query, d_kv], axis=1)
    d_normed1_all = dot_nt(d_projected, qkv_full).astype(BF)
    d_normed1_pieces = sum_parts(
        [d_normed1_all[k * rows : (k + 1) * rows] for k in range(seqs)], "seq"
    )
    feed_sums = chunk_sums(own_terms, "seq", seq).astype(BF)

    normed1_late, result_late = after((normed1_all, tuple(result_parts[1:])), d_normed1_all)
    qkv_grads = dot_tn(normed1_late, d_projected)
    column_sums = jnp.sum(d_projected.astype(F32), axis=0)
    unit_grads = (qkv_grads - shift_row[:, None] * column_sums[None, :]) / gain_row[:, None]
    qkv_float = qkv_full.astype(F32)
    is_seq = (jnp.arange(seqs) == seq)[:, None]
    late = jnp.stack(
        [
            jnp.sum(qkv_float * unit_grads, axis=1),
            jnp.sum(qkv_float * column_sums[None, :], axis=1),
            jnp.where(is_seq, column_sums[None, :head_width], 0.0).reshape(-1),
            jnp.where(is_seq, column_sums[None, 2 * head_width :], 0.0).reshape(-1),
        ]
    )
    late = padded(late.reshape(4, owners, own_rows).transpose(1, 0, 2), 16, 3 * head_width)
    qkv_grads = jnp.concatenate(
        [qkv_grads.astype(BF).reshape(owners, own_rows, 3 * head_width), late.astype(BF)], axis=1
    ).reshape(owners // 2, 2, own_rows + 16, 3 * head_width)
    qkv_arrived = swap(
        lax.dynamic_index_in_dim(qkv_grads, 1 - own % 2, 1, keepdims=False), "fsdp", 1
    )
    qkv_terms, _ = owner_sums(
        lax.dynamic_index_in_dim(qkv_grads, own % 2, 1, keepdims=False), qkv_arrived, own
    )
    qkv_own = sum(one.astype(F32) for one in qkv_terms)
    blk_rows = own_rows // blocks

    def qkv_part(index):
        return jnp.concatenate(
            [lax.dynamic_slice_in_dim(qkv_own, index * blk_rows, blk_rows), qkv_own[own_rows:]]
        )

    qkv_sums = tree_sum(
        [qkv_part(blk).astype(BF)]
        + [swap(qkv_part(blk ^ m).astype(BF), "blk", m) for m in range(1, blocks)]
    ).astype(BF)

    (grad_tokens,) = run(
        functools.partial(first_back_kernel, seqs),
        "first_back",
        [shape((rows, width), F32)],
        [],
        [],
        [*d_normed1_pieces, inputs, d_middle, norm_gain],
    )
    outcome = result_parts[0]
    for m in range(1, blocks):
        outcome = outcome + swap(result_late[m - 1], "blk", m).astype(F32)
    valid = lax.broadcasted_iota(jnp.int32, (rows, 1), 0) < counts[0, blk * seqs + seq]
    activations = jnp.where(valid, middle + outcome + biases[3], 0.0)

    feed_seq = from_all(feed_sums, "seq")
    feed_all = [from_all(one, "blk") for one in feed_seq]
    qkv_seq = from_all(qkv_sums, "seq")
    qkv_all = [from_all(one, "blk") for one in qkv_seq]
    held = pltpu.VMEM((blocks, seqs, chunk_rows, width), BF)
    grad_down, grad_up = run(
        functools.partial(
            place_kernel,
            seqs,
            blocks,
            [
                lambda b, k: [(0, chunk, 0, width, b * hidden_rows + k * chunk, 0)],
                lambda b, k: [
                    (
                        chunk + (i * hidden_rows // width) * up_chunk,
                        up_chunk,
                        i * hidden_rows % width,
                        hidden_rows,
                        k * up_chunk,
                        (i * blocks + b) * hidden_rows,
                    )
                    for i in range(owners)
                ],
            ],
        ),
        "place_feed",
        [shape((blocks * hidden_rows, width), F32), shape((own_rows, blocks * hidden_width), F32)],
        [after(place, qkv_seq)],
        [feed_all[k][m] for m in range(blocks) for k in range(seqs)],
        [],
        [held, dma((blocks * seqs,))],
    )
    (grad_qkv,) = run(
        functools.partial(
            place_kernel,
            seqs,
            blocks,
            [
                lambda b, k: [
                    (
                        0,
                        blk_rows,
                        i * head_width,
                        head_width,
                        b * blk_rows,
                        i * width + k * head_width,
                    )
                    for i in range(3)
                ]
            ],
        ),
        "place_qkv",
        [shape((own_rows, 3 * width), F32)],
        [place],
        [qkv_all[k][m] for m in range(blocks) for k in range(seqs)],
        [],
        [
            pltpu.VMEM((blocks, seqs, blk_rows + 16, 3 * head_width), BF),
            dma((blocks * seqs,)),
        ],
    )
    late_sums = tree_sum([one[blk_rows : blk_rows + 4, :own_rows] for one in qkv_seq])
    early_sums = out_sums[own_rows : own_rows + 4, :own_rows]
    return (
        activations[None],
        grad_tokens[None],
        jnp.stack([late_sums[0], early_sums[0]]),
        jnp.stack([late_sums[1], early_sums[1]]),
        jnp.stack([late_sums[2], late_sums[3], early_sums[2], early_sums[3]]),
        out_sums[own_rows + 4, : blocks * hidden_rows],
        grad_qkv,
        out_sums[:own_rows],
        grad_up,
        grad_down,
    )


def solution(mesh):
    rows = P("fsdp", ("blk", "seq"), None)
    split = P("fsdp", None)
    return jax.shard_map(
        shards,
        mesh=mesh,
        in_specs=(rows, split, P(), P(), P(), P(), split, split, split, split, rows),
        out_specs=(
            rows,
            rows,
            P(None, "fsdp"),
            P(None, "fsdp"),
            P(None, "fsdp"),
            P("fsdp"),
            split,
            split,
            split,
            split,
        ),
        check_vma=False,
    )
```

profile of v0, /device:TPU:0, one launch (start us, length us, event | category | flops | bytes accessed | tf_op | source)
XLA Modules:
  0.0 341.5 jit_solution(8825318685843501419)
XLA Ops:
  14.6 3.0 collective-permute-start
  18.9 6.1 %collective-permute-done = bf16[192,576]{0,1:T(8,128)(2,1)} collective-permute-done((bf16[192,576]{0,1:T(8,128)(2,1)}, bf16[192,576]{0,1:T(8,128)(2,1)}, u32[]{:S(2)}, u32[]{:S(2)}) %collective-permute-start) | collective-permute-done | bytes 221216 | tf_op jit(solution)/shard_map/ppermute | solution.py:38
  26.7 3.6 %collective-permute-start.6 = (bf16[128,768]{1,0:T(8,128)(2,1)S(1)}, bf16[128,768]{1,0:T(8,128)(2,1)S(1)}, u32[]{:S(2)}, u32[]{:S(2)}) collective-permute-start(bf16[128,768]{1,0:T(8,128)(2,1)S(1)} %get-tuple-element.58), channel_id=1, source_target_pairs={{0,3},{1,2},{2,1},{3,0},{4,7},{5,6},{6,5},{7,4},{8,11},{9,10},{10,... | collective-permute-start | bytes 589832 | tf_op jit(solution)/shard_map/ppermute | solution.py:38
  31.2 10.5 %collective-permute-done.4 = bf16[128,768]{1,0:T(8,128)(2,1)} collective-permute-done((bf16[128,768]{1,0:T(8,128)(2,1)S(1)}, bf16[128,768]{1,0:T(8,128)(2,1)}, u32[]{:S(2)}, u32[]{:S(2)}) %collective-permute-start.4) | collective-permute-done | bytes 196640 | tf_op jit(solution)/shard_map/ppermute | solution.py:38
  41.8 16.7 %collective-permute-done.2.refs_2_ = bf16[960,768]{1,0:T(8,128)(2,1)} collective-permute-done((bf16[960,768]{1,0:T(8,128)(2,1)S(1)}, bf16[960,768]{1,0:T(8,128)(2,1)}, u32[]{:S(2)}, u32[]{:S(2)}) %collective-permute-start.2) | collective-permute-done | bytes 1474592 | tf_op jit(solution)/shard_map/ppermute | solution.py:38
  66.8 9.2 %collective-permute-done.9.refs_1_.refs_5_ = bf16[512,384]{1,0:T(8,128)(2,1)S(1)} collective-permute-done((bf16[512,384]{1,0:T(8,128)(2,1)S(1)}, bf16[512,384]{1,0:T(8,128)(2,1)S(1)}, u32[]{:S(2)}, u32[]{:S(2)}) %collective-permute-start.9) | collective-permute-done | bytes 393248 | tf_op jit(solution)/shard_map/ppermute | solution.py:38
  76.0 3.8 %attend.1 = (bf16[128,192]{1,0:T(8,128)(2,1)S(1)}, bf16[128,192]{1,0:T(8,128)(2,1)S(1)}, bf16[128,192]{1,0:T(8,128)(2,1)S(1)}, bf16[128,192]{1,0:T(8,128)(2,1)S(1)}, f32[3,512]{1,0:T(4,128)S(1)}) custom-call(s32[3]{0:T(128)S(1)} %pad_add_fusion.place_ref, s32[1,8]{1,0:T(1,128)S(1)} %copy-done.29, bf16[512,192]{1,0:T(8,128)(2,1)S(1)} %fusion.8.q_ref, ...), custom_call_target="tpu_custom_call" | custom-call | flops 402653184 | bytes 1185792 | tf_op jit(solution)/shard_map/attend/pallas_call | solution.py:319
  81.4 2.6 collective-permute-start.11
  90.2 2.5 project.1
  94.9 4.2 %collective-permute-done.13.refs_5_.refs_1_ = bf16[128,768]{1,0:T(8,128)(2,1)S(1)} collective-permute-done((bf16[128,768]{1,0:T(8,128)(2,1)S(1)}, bf16[128,768]{1,0:T(8,128)(2,1)S(1)}, u32[]{:S(2)}, u32[]{:S(2)}) %collective-permute-start.13) | collective-permute-done | bytes 196640 | tf_op jit(solution)/shard_map/ppermute | solution.py:38
  99.1 6.2 %hidden.1 = (bf16[256,1536]{1,0:T(8,128)(2,1)S(1)}, bf16[256,1536]{1,0:T(8,128)(2,1)S(1)}, f32[1,1536]{1,0:T(1,128)S(1)}, f32[128,768]{1,0:T(8,128)S(1)}, bf16[1...) custom-call(s32[3]{0:T(128)S(1)} %pad_add_fusion.place_ref, ...), custom_call_target="tpu_custom_call" | custom-call | flops 2415919104 | bytes 9449472 | tf_op jit(solution)/shard_map/hidden/pallas_call | solution.py:319
  106.7 4.6 %grads.1 = (bf16[2,4,192,768]{3,2,1,0:T(8,128)(2,1)}, bf16[2,4,192,768]{3,2,1,0:T(8,128)(2,1)S(1)}) custom-call(s32[3]{0:T(128)S(1)} %pad_add_fusion.place_ref, bf16[128,768]{1,0:T(8,128)(2,1)S(1)} %get-tuple-element.70.refs_4_.refs_0_, bf16[128,768]{1,0:T(8,128)(2,1)S(1)} %collective-permute-done.13.refs_5_.refs_1_, bf16[128,768]{1,0:T(8,128)(2,1)S(1)} %copy-done.37, ...), custom_call_target="tpu_custom_call" | custom-call | flops 1207959552 | bytes 7077888 | tf_op jit(solution)/shard_map/grads/pallas_call | solution.py:319
  116.8 4.7 %collective-permute-done.16.refs_5_ = bf16[128,768]{1,0:T(8,128)(2,1)S(1)} collective-permute-done((bf16[128,768]{1,0:T(8,128)(2,1)}, bf16[128,768]{1,0:T(8,128)(2,1)S(1)}, u32[]{:S(2)}, u32[]{:S(2)}) %collective-permute-start.16) | collective-permute-done | bytes 196640 | tf_op jit(solution)/shard_map/ppermute | solution.py:38
  126.3 2.9 middle.1
  133.1 2.6 collective-permute-start.19
  138.3 4.8 %convert_add_fusion = (f32[1,4,192,768]{3,2,1,0:T(8,128)}, bf16[1,4,192,768]{3,2,1,0:T(8,128)(2,1)}) fusion(bf16[2,4,192,768]{3,2,1,0:T(8,128)(2,1)} %collective-permute-done.15, s32[]{:T(128)S(6)} %select_n.287, bf16[2,4,192,768]{3,2,1,0:T(8,128)(2,1)} %copy-done.7, s32[]{:T(128)S(6)} %select_n.283), kind=kLoop, calls=%fused_computation.6 | loop fusion | flops 4128768 | bytes 8257544 | tf_op jit(solution)/shard_map/add | solution.py:342
  143.1 5.6 %attend_back.1 = (bf16[512,192]{1,0:T(8,128)(2,1)S(1)}, f32[512,384]{1,0:T(8,128)S(1)}, bf16[512,384]{1,0:T(8,128)(2,1)S(1)}) custom-call(s32[3]{0:T(128)S(1)} %pad_add_fusion.place_ref, s32[1,8]{1,0:T(1,128)S(1)} %copy-done.29, bf16[512,192]{1,0:T(8,128)(2,1)S(1)} %copy-done.42, f32[3,512]{1,0:T(4,128)S(1)} %get-tuple-element.80.log_ref, ...), custom_call_target="tpu_custom_call" | custom-call | flops 1006632960 | bytes 2562048 | tf_op jit(solution)/shard_map/attend_back/pallas_call | solution.py:319
  151.8 6.9 %collective-permute-done.20 = bf16[512,384]{1,0:T(8,128)(2,1)S(1)} collective-permute-done((bf16[512,384]{1,0:T(8,128)(2,1)S(1)}, bf16[512,384]{1,0:T(8,128)(2,1)S(1)}, u32[]{:S(2)}, u32[]{:S(2)}) %collective-permute-start.20) | collective-permute-done | bytes 393248 | tf_op jit(solution)/shard_map/ppermute | solution.py:38
  169.0 3.1 collective-permute-start.22
  173.7 3.3 collective-permute-done.24.refs_3_
  179.3 6.3 %collective-permute-done.23.refs_2_ = bf16[128,768]{1,0:T(8,128)(2,1)S(1)} collective-permute-done((bf16[128,768]{1,0:T(8,128)(2,1)S(1)}, bf16[128,768]{1,0:T(8,128)(2,1)S(1)}, u32[]{:S(2)}, u32[]{:S(2)}) %collective-permute-start.23) | collective-permute-done | bytes 196640 | tf_op jit(solution)/shard_map/ppermute | solution.py:38
  191.1 14.8 %collective-permute-done.26 = bf16[1,208,576]{2,1,0:T(8,128)(2,1)S(1)} collective-permute-done((bf16[1,208,576]{2,1,0:T(8,128)(2,1)S(1)}, bf16[1,208,576]{2,1,0:T(8,128)(2,1)S(1)}, u32[]{:S(2)}, u32[]{:S(2)}) %collective-permute-start.26) | collective-permute-done | bytes 239648 | tf_op jit(solution)/shard_map/ppermute | solution.py:38
  211.6 2.4 collective-permute-start.38
  214.0 44.3 %all-reduce.6.cloned.1.call-done = bf16[208,768]{1,0:T(8,128)(2,1)} async-done(((bf16[208,768]{1,0:T(8,128)(2,1)}), bf16[208,768]{1,0:T(8,128)(2,1)}) %all-reduce.6.cloned.1.call-update) | async-done | bytes 319504 | tf_op jit(solution)/shard_map/psum | solution.py:564
  262.6 2.4 collective-permute-start.30
  268.4 2.4 collective-permute-start.41
  271.1 13.6 %collective-permute-start.39 = (bf16[192,768]{1,0:T(8,128)(2,1)S(1)}, bf16[192,768]{1,0:T(8,128)(2,1)S(1)}, u32[]{:S(2)}, u32[]{:S(2)}) collective-permute-start(bf16[192,768]{1,0:T(8,128)(2,1)S(1)} %fusion.12.refs_0_), channel_id=1, source_target_pairs={{0,1},{1,0},{2,3},{3,2},{4,5},{5,4},{6,7},{7,6},{8,9},{9,8},{10,11... | collective-permute-start | bytes 884744 | tf_op jit(solution)/shard_map/ppermute | solution.py:38
  285.3 4.8 %collective-permute-done.29.refs_2_ = bf16[112,576]{1,0:T(8,128)(2,1)S(1)} collective-permute-done((bf16[112,576]{1,0:T(8,128)(2,1)S(1)}, bf16[112,576]{1,0:T(8,128)(2,1)S(1)}, u32[]{:S(2)}, u32[]{:S(2)}) %collective-permute-start.29) | collective-permute-done | bytes 129056 | tf_op jit(solution)/shard_map/ppermute | solution.py:38
  292.2 4.5 %collective-permute-done.31.refs_4_ = bf16[112,576]{1,0:T(8,128)(2,1)S(1)} collective-permute-done((bf16[112,576]{1,0:T(8,128)(2,1)S(1)}, bf16[112,576]{1,0:T(8,128)(2,1)S(1)}, u32[]{:S(2)}, u32[]{:S(2)}) %collective-permute-start.31) | collective-permute-done | bytes 129056 | tf_op jit(solution)/shard_map/ppermute | solution.py:38
  306.0 21.6 %collective-permute-done.32.refs_5_ = bf16[112,576]{1,0:T(8,128)(2,1)S(1)} collective-permute-done((bf16[112,576]{1,0:T(8,128)(2,1)S(1)}, bf16[112,576]{1,0:T(8,128)(2,1)S(1)}, u32[]{:S(2)}, u32[]{:S(2)}) %collective-permute-start.32) | collective-permute-done | bytes 129056 | tf_op jit(solution)/shard_map/ppermute | solution.py:38
  327.5 3.5 %place_qkv.1 = f32[192,2304]{1,0:T(8,128)} custom-call(s32[3]{0:T(128)S(1)} %pad_add_fusion.place_ref, bf16[112,576]{1,0:T(8,128)(2,1)S(1)} %add_convert_fusion.5.refs_0_, bf16[112,576]{1,0:T(8,128)(2,1)S(1)} %collective-permute-done.28.refs_1_, bf16[112,576]{1,0:T(8,128)(2,1)S(1)} %collective-permute-done.29.refs_2_, ...), custom_call_target="tpu_custom_call" | custom-call | bytes 2801664 | tf_op jit(solution)/shard_map/place_qkv/pallas_call | solution.py:319
  331.1 3.5 %place_feed.1 = (f32[768,768]{1,0:T(8,128)}, f32[192,3072]{1,0:T(8,128)}) custom-call(s32[3]{0:T(128)S(1)} %pad_add_fusion.place_ref, bf16[192,768]{1,0:T(8,128)(2,1)S(1)} %fusion.12.refs_0_, bf16[192,768]{1,0:T(8,128)(2,1)S(1)} %collective-permute-done.39.refs_1_, bf16[192,768]{1,0:T(8,128)(2,1)S(1)} %collective-permute-done.40.refs_2_, ...), custom_call_target="tpu_custom_call" | custom-call | bytes 7077888 | tf_op jit(solution)/shard_map/place_feed/pallas_call | solution.py:319
  (264 shorter events, 95.5 us)
Async XLA Ops:
  7.2 172.0 %reduce-scatter.2.cloned.1.call-start = ((), (), s32[]{:S(2)}) async-start(), calls=%async_computation.1 | async-start | bytes 1597440 | tf_op jit(solution)/shard_map/reduce_scatter | solution.py:565
  24.9 33.6 %collective-permute-start.2 = (bf16[960,768]{1,0:T(8,128)(2,1)S(1)}, bf16[960,768]{1,0:T(8,128)(2,1)}, u32[]{:S(2)}, u32[]{:S(2)}) collective-permute-start(bf16[960,768]{1,0:T(8,128)(2,1)S(1)} %pad_maximum_fusion.refs_0_), channel_id=1, source_target_pairs={{0,16},{8,24},{16,0},{24,8},{1,17},{9,25},{17,1},{25,9},{2,18},{10... | collective-permute-start | bytes 4423688 | tf_op jit(solution)/shard_map/ppermute | solution.py:38
  26.7 34.3 %collective-permute-start.6 = (bf16[128,768]{1,0:T(8,128)(2,1)S(1)}, bf16[128,768]{1,0:T(8,128)(2,1)S(1)}, u32[]{:S(2)}, u32[]{:S(2)}) collective-permute-start(bf16[128,768]{1,0:T(8,128)(2,1)S(1)} %get-tuple-element.58), channel_id=1, source_target_pairs={{0,3},{1,2},{2,1},{3,0},{4,7},{5,6},{6,5},{7,4},{8,11},{9,10},{10,... | collective-permute-start | bytes 589832 | tf_op jit(solution)/shard_map/ppermute | solution.py:38
  30.3 29.2 %collective-permute-start.5 = (bf16[128,768]{1,0:T(8,128)(2,1)S(1)}, bf16[128,768]{1,0:T(8,128)(2,1)}, u32[]{:S(2)}, u32[]{:S(2)}) collective-permute-start(bf16[128,768]{1,0:T(8,128)(2,1)S(1)} %get-tuple-element.58), channel_id=1, source_target_pairs={{0,2},{1,3},{2,0},{3,1},{4,6},{5,7},{6,4},{7,5},{8,10},{9,11},{10,... | collective-permute-start | bytes 589832 | tf_op jit(solution)/shard_map/ppermute | solution.py:38
  30.3 11.5 %collective-permute-start.4 = (bf16[128,768]{1,0:T(8,128)(2,1)S(1)}, bf16[128,768]{1,0:T(8,128)(2,1)}, u32[]{:S(2)}, u32[]{:S(2)}) collective-permute-start(bf16[128,768]{1,0:T(8,128)(2,1)S(1)} %get-tuple-element.58), channel_id=1, source_target_pairs={{0,1},{1,0},{2,3},{3,2},{4,5},{5,4},{6,7},{7,6},{8,9},{9,8},{10,11... | collective-permute-start | bytes 589832 | tf_op jit(solution)/shard_map/ppermute | solution.py:38
  31.0 30.0 %collective-permute-start.8 = (bf16[192,576]{0,1:T(8,128)(2,1)}, bf16[192,576]{0,1:T(8,128)(2,1)}, u32[]{:S(2)}, u32[]{:S(2)}) collective-permute-start(bf16[192,576]{0,1:T(8,128)(2,1)} %pad_maximum_fusion.3), channel_id=1, source_target_pairs={{0,8},{8,0},{16,24},{24,16},{1,9},{9,1},{17,25},{25,17},{2,10},{10... | collective-permute-start | bytes 663560 | tf_op jit(solution)/shard_map/ppermute | solution.py:38
  41.8 48.3 %collective-permute-start.1 = (bf16[960,768]{1,0:T(8,128)(2,1)S(1)}, bf16[960,768]{1,0:T(8,128)(2,1)S(1)}, u32[]{:S(2)}, u32[]{:S(2)}) collective-permute-start(bf16[960,768]{1,0:T(8,128)(2,1)S(1)} %pad_maximum_fusion.refs_0_), channel_id=1, source_target_pairs={{0,8},{8,0},{16,24},{24,16},{1,9},{9,1},{17,25},{25,17},{2,10},{10... | collective-permute-start | bytes 4423688 | tf_op jit(solution)/shard_map/ppermute | solution.py:38
  58.5 31.6 %collective-permute-start.3 = (bf16[960,768]{1,0:T(8,128)(2,1)}, bf16[960,768]{1,0:T(8,128)(2,1)S(1)}, u32[]{:S(2)}, u32[]{:S(2)}) collective-permute-start(bf16[960,768]{1,0:T(8,128)(2,1)} %collective-permute-done.2.refs_2_), channel_id=1, source_target_pairs={{0,8},{8,0},{16,24},{24,16},{1,9},{9,1},{17,25},{25,17},{2,10},{10... | collective-permute-start | bytes 4423688 | tf_op jit(solution)/shard_map/ppermute | solution.py:38
  112.7 25.5 %collective-permute-start.15 = (bf16[2,4,192,768]{3,2,1,0:T(8,128)(2,1)}, bf16[2,4,192,768]{3,2,1,0:T(8,128)(2,1)}, u32[]{:S(2)}, u32[]{:S(2)}) collective-permute-start(bf16[2,4,192,768]{3,2,1,0:T(8,128)(2,1)} %get-tuple-element.78), channel_id=1, source_target_pairs={{0,8},{8,0},{16,24},{24,16},{1,9},{9,1},{17,25},{25,17},{2,10},{10... | collective-permute-start | bytes 7077896 | tf_op jit(solution)/shard_map/ppermute | solution.py:38
  131.3 11.8 %collective-permute-start.17 = (bf16[128,192]{1,0:T(8,128)(2,1)}, bf16[128,192]{1,0:T(8,128)(2,1)S(1)}, u32[]{:S(2)}, u32[]{:S(2)}) collective-permute-start(bf16[128,192]{1,0:T(8,128)(2,1)} %get-tuple-element.86), channel_id=1, source_target_pairs={{0,1},{1,0},{2,3},{3,2},{4,5},{5,4},{6,7},{7,6},{8,9},{9,8},{10,11... | collective-permute-start | bytes 147464 | tf_op jit(solution)/shard_map/ppermute | solution.py:38
  131.3 11.8 %collective-permute-start.18 = (bf16[128,192]{1,0:T(8,128)(2,1)}, bf16[128,192]{1,0:T(8,128)(2,1)S(1)}, u32[]{:S(2)}, u32[]{:S(2)}) collective-permute-start(bf16[128,192]{1,0:T(8,128)(2,1)} %get-tuple-element.87), channel_id=1, source_target_pairs={{0,2},{1,3},{2,0},{3,1},{4,6},{5,7},{6,4},{7,5},{8,10},{9,11},{10,... | collective-permute-start | bytes 147464 | tf_op jit(solution)/shard_map/ppermute | solution.py:38
  151.5 106.8 %all-reduce.6.cloned.1.call-start = ((), (), s32[]{:S(2)}) async-start(), calls=%async_computation.2 | async-start | bytes 638976 | tf_op jit(solution)/shard_map/psum | solution.py:564
  165.9 20.9 %collective-permute-start.25 = (bf16[2,208,576]{2,1,0:T(8,128)(2,1)}, bf16[2,208,576]{2,1,0:T(8,128)(2,1)}, u32[]{:S(2)}, u32[]{:S(2)}) collective-permute-start(bf16[2,208,576]{2,1,0:T(8,128)(2,1)} %fusion.14), channel_id=1, source_target_pairs={{0,8},{8,0},{16,24},{24,16},{1,9},{9,1},{17,25},{25,17},{2,10},{10... | collective-permute-start | bytes 1437704 | tf_op jit(solution)/shard_map/ppermute | solution.py:38
  169.0 16.6 %collective-permute-start.23 = (bf16[128,768]{1,0:T(8,128)(2,1)S(1)}, bf16[128,768]{1,0:T(8,128)(2,1)S(1)}, u32[]{:S(2)}, u32[]{:S(2)}) collective-permute-start(bf16[128,768]{1,0:T(8,128)(2,1)S(1)} %get-tuple-element.126), channel_id=1, source_target_pairs={{0,2},{1,3},{2,0},{3,1},{4,6},{5,7},{6,4},{7,5},{8,10},{9,11},{10,... | collective-permute-start | bytes 589832 | tf_op jit(solution)/shard_map/ppermute | solution.py:38
  169.0 16.6 %collective-permute-start.22 = (bf16[128,768]{1,0:T(8,128)(2,1)S(1)}, bf16[128,768]{1,0:T(8,128)(2,1)S(1)}, u32[]{:S(2)}, u32[]{:S(2)}) collective-permute-start(bf16[128,768]{1,0:T(8,128)(2,1)S(1)} %get-tuple-element.127), channel_id=1, source_target_pairs={{0,1},{1,0},{2,3},{3,2},{4,5},{5,4},{6,7},{7,6},{8,9},{9,8},{10,11... | collective-permute-start | bytes 589832 | tf_op jit(solution)/shard_map/ppermute | solution.py:38
  172.2 36.4 %collective-permute-start.35 = (bf16[1,4,192,768]{3,2,1,0:T(8,128)(2,1)}, bf16[1,4,192,768]{3,2,1,0:T(8,128)(2,1)}, u32[]{:S(2)}, u32[]{:S(2)}) collective-permute-start(bf16[1,4,192,768]{3,2,1,0:T(8,128)(2,1)} %get-tuple-element.109), channel_id=1, source_target_pairs={{0,16},{8,24},{16,0},{24,8},{1,17},{9,25},{17,1},{25,9},{2,18},{10... | collective-permute-start | bytes 3538952 | tf_op jit(solution)/shard_map/ppermute | solution.py:38
  177.1 12.3 %collective-permute-start.21 = (bf16[128,768]{1,0:T(8,128)(2,1)S(1)}, bf16[128,768]{1,0:T(8,128)(2,1)}, u32[]{:S(2)}, u32[]{:S(2)}) collective-permute-start(bf16[128,768]{1,0:T(8,128)(2,1)S(1)} %copy-done.35), channel_id=1, source_target_pairs={{0,4},{4,0},{1,5},{5,1},{2,6},{6,2},{3,7},{7,3},{8,12},{12,8},{9,1... | collective-permute-start | bytes 589832 | tf_op jit(solution)/shard_map/ppermute | solution.py:38
  187.8 18.1 %collective-permute-start.26 = (bf16[1,208,576]{2,1,0:T(8,128)(2,1)S(1)}, bf16[1,208,576]{2,1,0:T(8,128)(2,1)S(1)}, u32[]{:S(2)}, u32[]{:S(2)}) collective-permute-start(bf16[1,208,576]{2,1,0:T(8,128)(2,1)S(1)} %fusion.15), channel_id=1, source_target_pairs={{0,16},{8,24},{16,0},{24,8},{1,17},{9,25},{17,1},{25,9},{2,18},{10... | collective-permute-start | bytes 718856 | tf_op jit(solution)/shard_map/ppermute | solution.py:38
  207.1 55.4 %collective-permute-start.27 = (bf16[112,576]{1,0:T(8,128)(2,1)S(1)}, bf16[112,576]{1,0:T(8,128)(2,1)S(1)}, u32[]{:S(2)}, u32[]{:S(2)}) collective-permute-start(bf16[112,576]{1,0:T(8,128)(2,1)S(1)} %pad_maximum_fusion.6), channel_id=1, source_target_pairs={{0,4},{4,0},{1,5},{5,1},{2,6},{6,2},{3,7},{7,3},{8,12},{12,8},{9,1... | collective-permute-start | bytes 387080 | tf_op jit(solution)/shard_map/ppermute | solution.py:38
  210.0 55.1 %collective-permute-start.36 = (bf16[192,768]{1,0:T(8,128)(2,1)S(1)}, bf16[192,768]{1,0:T(8,128)(2,1)S(1)}, u32[]{:S(2)}, u32[]{:S(2)}) collective-permute-start(bf16[192,768]{1,0:T(8,128)(2,1)S(1)} %get-tuple-element.110), channel_id=1, source_target_pairs={{0,1},{1,0},{2,3},{3,2},{4,5},{5,4},{6,7},{7,6},{8,9},{9,8},{10,11... | collective-permute-start | bytes 884744 | tf_op jit(solution)/shard_map/ppermute | solution.py:38
  211.6 55.5 %collective-permute-start.38 = (bf16[192,768]{1,0:T(8,128)(2,1)S(1)}, bf16[192,768]{1,0:T(8,128)(2,1)S(1)}, u32[]{:S(2)}, u32[]{:S(2)}) collective-permute-start(bf16[192,768]{1,0:T(8,128)(2,1)S(1)} %get-tuple-element.111), channel_id=1, source_target_pairs={{0,3},{1,2},{2,1},{3,0},{4,7},{5,6},{6,5},{7,4},{8,11},{9,10},{10,... | collective-permute-start | bytes 884744 | tf_op jit(solution)/shard_map/ppermute | solution.py:38
  213.9 53.1 %collective-permute-start.37 = (bf16[192,768]{1,0:T(8,128)(2,1)S(1)}, bf16[192,768]{1,0:T(8,128)(2,1)S(1)}, u32[]{:S(2)}, u32[]{:S(2)}) collective-permute-start(bf16[192,768]{1,0:T(8,128)(2,1)S(1)} %get-tuple-element.112), channel_id=1, source_target_pairs={{0,2},{1,3},{2,0},{3,1},{4,6},{5,7},{6,4},{7,5},{8,10},{9,11},{10,... | collective-permute-start | bytes 884744 | tf_op jit(solution)/shard_map/ppermute | solution.py:38
  265.0 25.1 %collective-permute-start.29 = (bf16[112,576]{1,0:T(8,128)(2,1)S(1)}, bf16[112,576]{1,0:T(8,128)(2,1)S(1)}, u32[]{:S(2)}, u32[]{:S(2)}) collective-permute-start(bf16[112,576]{1,0:T(8,128)(2,1)S(1)} %add_convert_fusion.5.refs_0_), channel_id=1, source_target_pairs={{0,2},{1,3},{2,0},{3,1},{4,6},{5,7},{6,4},{7,5},{8,10},{9,11},{10,... | collective-permute-start | bytes 387080 | tf_op jit(solution)/shard_map/ppermute | solution.py:38
  265.1 25.8 %collective-permute-start.28 = (bf16[112,576]{1,0:T(8,128)(2,1)S(1)}, bf16[112,576]{1,0:T(8,128)(2,1)S(1)}, u32[]{:S(2)}, u32[]{:S(2)}) collective-permute-start(bf16[112,576]{1,0:T(8,128)(2,1)S(1)} %add_convert_fusion.5.refs_0_), channel_id=1, source_target_pairs={{0,1},{1,0},{2,3},{3,2},{4,5},{5,4},{6,7},{7,6},{8,9},{9,8},{10,11... | collective-permute-start | bytes 387080 | tf_op jit(solution)/shard_map/ppermute | solution.py:38
  268.4 32.1 %collective-permute-start.41 = (bf16[192,768]{1,0:T(8,128)(2,1)S(1)}, bf16[192,768]{1,0:T(8,128)(2,1)S(1)}, u32[]{:S(2)}, u32[]{:S(2)}) collective-permute-start(bf16[192,768]{1,0:T(8,128)(2,1)S(1)} %fusion.12.refs_0_), channel_id=1, source_target_pairs={{0,3},{1,2},{2,1},{3,0},{4,7},{5,6},{6,5},{7,4},{8,11},{9,10},{10,... | collective-permute-start | bytes 884744 | tf_op jit(solution)/shard_map/ppermute | solution.py:38
  270.8 31.0 %collective-permute-start.40 = (bf16[192,768]{1,0:T(8,128)(2,1)S(1)}, bf16[192,768]{1,0:T(8,128)(2,1)S(1)}, u32[]{:S(2)}, u32[]{:S(2)}) collective-permute-start(bf16[192,768]{1,0:T(8,128)(2,1)S(1)} %fusion.12.refs_0_), channel_id=1, source_target_pairs={{0,2},{1,3},{2,0},{3,1},{4,6},{5,7},{6,4},{7,5},{8,10},{9,11},{10,... | collective-permute-start | bytes 884744 | tf_op jit(solution)/shard_map/ppermute | solution.py:38
  271.1 31.6 %collective-permute-start.39 = (bf16[192,768]{1,0:T(8,128)(2,1)S(1)}, bf16[192,768]{1,0:T(8,128)(2,1)S(1)}, u32[]{:S(2)}, u32[]{:S(2)}) collective-permute-start(bf16[192,768]{1,0:T(8,128)(2,1)S(1)} %fusion.12.refs_0_), channel_id=1, source_target_pairs={{0,1},{1,0},{2,3},{3,2},{4,5},{5,4},{6,7},{7,6},{8,9},{9,8},{10,11... | collective-permute-start | bytes 884744 | tf_op jit(solution)/shard_map/ppermute | solution.py:38
  299.8 31.3 %collective-permute-start.42 = (bf16[192,768]{1,0:T(8,128)(2,1)S(1)}, bf16[192,768]{1,0:T(8,128)(2,1)S(1)}, u32[]{:S(2)}, u32[]{:S(2)}) collective-permute-start(bf16[192,768]{1,0:T(8,128)(2,1)S(1)} %fusion.12.refs_0_), channel_id=1, source_target_pairs={{0,4},{4,0},{1,5},{5,1},{2,6},{6,2},{3,7},{7,3},{8,12},{12,8},{9,1... | collective-permute-start | bytes 884744 | tf_op jit(solution)/shard_map/ppermute | solution.py:38
  300.5 30.6 %collective-permute-start.45 = (bf16[192,768]{1,0:T(8,128)(2,1)S(1)}, bf16[192,768]{1,0:T(8,128)(2,1)S(1)}, u32[]{:S(2)}, u32[]{:S(2)}) collective-permute-start(bf16[192,768]{1,0:T(8,128)(2,1)S(1)} %collective-permute-done.41.refs_3_), channel_id=1, source_target_pairs={{0,4},{4,0},{1,5},{5,1},{2,6},{6,2},{3,7},{7,3},{8,12},{12,8},{9,1... | collective-permute-start | bytes 884744 | tf_op jit(solution)/shard_map/ppermute | solution.py:38
  301.8 29.3 %collective-permute-start.44 = (bf16[192,768]{1,0:T(8,128)(2,1)S(1)}, bf16[192,768]{1,0:T(8,128)(2,1)S(1)}, u32[]{:S(2)}, u32[]{:S(2)}) collective-permute-start(bf16[192,768]{1,0:T(8,128)(2,1)S(1)} %collective-permute-done.40.refs_2_), channel_id=1, source_target_pairs={{0,4},{4,0},{1,5},{5,1},{2,6},{6,2},{3,7},{7,3},{8,12},{12,8},{9,1... | collective-permute-start | bytes 884744 | tf_op jit(solution)/shard_map/ppermute | solution.py:38
  302.7 28.4 %collective-permute-start.43 = (bf16[192,768]{1,0:T(8,128)(2,1)S(1)}, bf16[192,768]{1,0:T(8,128)(2,1)S(1)}, u32[]{:S(2)}, u32[]{:S(2)}) collective-permute-start(bf16[192,768]{1,0:T(8,128)(2,1)S(1)} %collective-permute-done.39.refs_1_), channel_id=1, source_target_pairs={{0,4},{4,0},{1,5},{5,1},{2,6},{6,2},{3,7},{7,3},{8,12},{12,8},{9,1... | collective-permute-start | bytes 884744 | tf_op jit(solution)/shard_map/ppermute | solution.py:38
  303.8 23.7 %collective-permute-start.32 = (bf16[112,576]{1,0:T(8,128)(2,1)S(1)}, bf16[112,576]{1,0:T(8,128)(2,1)S(1)}, u32[]{:S(2)}, u32[]{:S(2)}) collective-permute-start(bf16[112,576]{1,0:T(8,128)(2,1)S(1)} %collective-permute-done.28.refs_1_), channel_id=1, source_target_pairs={{0,4},{4,0},{1,5},{5,1},{2,6},{6,2},{3,7},{7,3},{8,12},{12,8},{9,1... | collective-permute-start | bytes 387080 | tf_op jit(solution)/shard_map/ppermute | solution.py:38
  (70 other events, 499.6 us)
Sparse Core Ops, SparseCore 0:
  151.6 24.8 reduce-scatter.1
  180.2 77.9 all-reduce.5
where the time goes:
time: 343 us; the launch traced here: 341 us
  waiting for transfers between devices  166 us (48%)
  starting transfers between devices  69 us (20%)
  Pallas kernels  34.7 us (10%)
  local copies, waits for them, and re-layouts  27.7 us (8%)
  other arithmetic  22.7 us (7%)
  between operations  14.9 us (4%)
  matrix products  6.26 us (2%)
    ppermute x46, waiting for transfers between devices, swap(): lax.ppermute(array, axis, [(i, i ^ bits) for i in range(lax.axis_size(axi...  122 us
    ppermute x46, starting transfers between devices, swap(): lax.ppermute(array, axis, [(i, i ^ bits) for i in range(lax.axis_size(axi...  68.7 us
    psum x1, waiting for transfers between devices, shards(): lax.psum(lax.psum_scatter(out_grads.reshape(owners * (own_rows + 16), wid...  44.3 us
    pallas_call x10, Pallas kernels, run(): pl.pallas_call(kernel, out_shape=tuple(outs), in_specs=[pl.BlockSpec(memo...  34.7 us
    unnamed x112, local copies, waits for them, and re-layouts  17.2 us
  transfers between devices with their start and end apart: 48, of which 20 were waited for; matrix products, arithmetic and copies ran while one was open for 11% of the time, Pallas kernels for 4%

commit v1 on v0

--- a/solution.py
+++ b/solution.py
@@ -97,12 +97,66 @@
 
 
 def prepare_kernel(
-    seqs, place_ref, counts_ref, tokens_ref, grad_ref, gain_ref, shift_ref, normed_ref, outcome_ref
+    seqs,
+    place_ref,
+    counts_ref,
+    tokens_ref,
+    grad_ref,
+    gain_ref,
+    shift_ref,
+    qkv_ref,
+    normed_ref,
+    outcome_ref,
+    mine_ref,
 ):
+    width = tokens_ref.shape[1]
+    size = width // seqs
+    for part in range(3):
+        chosen = qkv_ref[:, part * width : part * width + size]
+        for k in range(1, seqs):
+            first = part * width + k * size
+            chosen = jnp.where(place_ref[1] == k, qkv_ref[:, first : first + size], chosen)
+        mine_ref[:, part * size : (part + 1) * size] = chosen
     unit = normalised(tokens_ref[...])[0]
     normed_ref[...] = (unit * row_of(gain_ref, 0) + row_of(shift_ref, 0)).astype(BF)
     valid = own_rows_valid(place_ref, counts_ref, seqs, grad_ref.shape[0])
     outcome_ref[...] = jnp.where(valid, grad_ref[...], 0.0).astype(BF)
+
+
+def pack_kernel(owners, blocks, parts, place_ref, up_ref, down_ref, out_ref, sems):
+    rows, width = up_ref.shape[0], down_ref.shape[1]
+    size = down_ref.shape[0] // blocks
+    copies = []
+    for i in range(owners):
+        first = pl.multiple_of((i * blocks + place_ref[0]) * size, 128)
+        part, column = divmod(i * size, width)
+        copies.append((up_ref.at[:, pl.ds(first, size)],
+                       out_ref.at[pl.ds(part * rows, rows), pl.ds(column, size)]))
+    first = pl.multiple_of(place_ref[0] * size, 16)
+    copies.append((down_ref.at[pl.ds(first, size)], out_ref.at[pl.ds(parts * rows, size)]))
+    copies = [
+        pltpu.make_async_copy(source, target, sems.at[i])
+        for i, (source, target) in enumerate(copies)
+    ]
+    for copy in copies:
+        copy.start()
+    for copy in copies:
+        copy.wait()
+
+
+def qkv_kernel(owners, seqs, place_ref, *refs):
+    pieces, normed_refs, refs = refs[:owners], refs[owners : owners + seqs], refs[owners + seqs :]
+    shift_ref, kv_ref, q_ref, w_ref, sems = refs
+    own_rows, size = pieces[0].shape[0], q_ref.shape[1]
+    copies = fetches(pieces, place_ref[2], 0, own_rows, w_ref, sems)
+    for copy in copies:
+        copy.start()
+    normed = jnp.concatenate([ref[...] for ref in normed_refs])
+    for copy in copies:
+        copy.wait()
+    result = (dot_nn(normed, w_ref[...]) + shift_ref[...]).astype(BF)
+    q_ref[...] = result[:, :size]
+    kv_ref[...] = result[:, size:]
 
 
 def attend_kernel(blocks, heads, pieces, slot_rows, place_ref, counts_ref, q_ref, *refs):
@@ -183,9 +237,9 @@
     waits = []
     for part in range(parts):
         waits += fetches(
-            pieces, own, (1 + part) * own_rows, own_rows, up_ref.at[part], sems.at[part]
+            pieces, own, part * own_rows, own_rows, up_ref.at[part], sems.at[part]
         )
-    waits += fetches(pieces, own, (1 + parts) * own_rows, hidden_rows, down_ref, sems.at[parts])
+    waits += fetches(pieces, own, parts * own_rows, hidden_rows, down_ref, sems.at[parts])
     for copy in waits:
         copy.start()
     normed = jnp.concatenate([ref[...] for ref in normed_refs])
@@ -280,6 +334,134 @@
             store(sent_ref)
 
 
+def step_kernel(bit, place_ref, kept_ref, arrived_ref, sent_ref, next_ref):
+    high = (place_ref[2] // bit) & 1
+    for i in range(sent_ref.shape[0]):
+        for ref, index in ((sent_ref, 2 * i + 1 - high), (next_ref, 2 * i + high)):
+            ref[i] = (kept_ref[index].astype(F32) + arrived_ref[index].astype(F32)).astype(BF)
+
+
+def chunk_kernel(seqs, place_ref, kept_ref, arrived_ref, *out_refs):
+    for j in range(seqs):
+        index = place_ref[1] ^ j
+        total = kept_ref[0, index].astype(F32) + arrived_ref[0, index].astype(F32)
+        out_refs[j][...] = total.astype(BF)
+
+
+def add_kernel(*refs):
+    refs[-1][...] = sum(ref[...].astype(F32) for ref in refs[:-1]).astype(BF)
+
+
+def project_back_kernel(blocks, seqs, *refs):
+    q_ref, kv_refs, w_ref, refs = refs[0], refs[1 : 1 + blocks], refs[1 + blocks], refs[2 + blocks :]
+    normed_refs, (gain_ref, shift_ref), refs = refs[:seqs], refs[seqs : seqs + 2], refs[seqs + 2 :]
+    projected_ref, columns_ref, sums_ref, part_refs = refs[0], refs[1], refs[2], refs[3:]
+    d_kv = sum(ref[...].astype(F32) for ref in kv_refs).astype(BF)
+    d_projected = jnp.concatenate([q_ref[...], d_kv], axis=1)
+    projected_ref[...] = d_projected
+    columns_ref[...] = jnp.sum(d_projected.astype(F32), axis=0, keepdims=True)
+    rows = normed_refs[0].shape[0]
+    gain, shift = row_of(gain_ref, 0), row_of(shift_ref, 0)
+    with_normed, plain = 0.0, 0.0
+    for k in range(seqs):
+        part = dot_nt(d_projected[k * rows : (k + 1) * rows], w_ref[...])
+        part_refs[k][...] = part.astype(BF)
+        with_normed = with_normed + jnp.sum(
+            part * (normed_refs[k][...].astype(F32) - shift), axis=0, keepdims=True
+        )
+        plain = plain + jnp.sum(part, axis=0, keepdims=True)
+    sums_ref[0:1, :] = with_normed / gain
+    sums_ref[1:2, :] = plain
+
+
+def last_grads_kernel(owners, seqs, blocks, place_ref, *refs):
+    normed_refs, att_refs, refs = refs[:seqs], refs[seqs : 2 * seqs], refs[2 * seqs :]
+    (projected_ref, branch_ref, columns_ref, first_ref, middle_ref, up_ref) = refs[:6]
+    sent_ref, kept_ref, att_ref = refs[6:]
+    width, size = branch_ref.shape[1], att_refs[0].shape[1]
+    own_rows, hidden_rows = width // owners, up_ref.shape[1] // owners
+    third = 3 * size
+    bit = place_ref[2] & 1
+    for k in range(seqs):
+        att_ref[place_ref[1] ^ k] = att_refs[k][...]
+    normed = jnp.concatenate([ref[...] for ref in normed_refs])
+    projected, branch = projected_ref[...], branch_ref[...]
+    for owner in range(owners):
+        first = owner * own_rows
+        group, column = divmod(first, size)
+        qkv = dot_tn(normed[:, first : first + own_rows], projected).astype(BF)
+        out = dot_tn(att_ref[group][:, column : column + own_rows], branch).astype(BF)
+        is_group = place_ref[1] == group
+        bias = [
+            jnp.where(is_group, columns_ref[:, start : start + own_rows], 0.0)
+            for start in (column, 2 * size + column)
+        ]
+        lines = [
+            first_ref[0:1, first : first + own_rows],
+            first_ref[1:2, first : first + own_rows],
+            *bias,
+        ] + [middle_ref[i : i + 1, first : first + own_rows] for i in range(4)]
+        lines = jnp.concatenate(lines).astype(BF)
+        up_line = up_ref[:, owner * hidden_rows : (owner + 1) * hidden_rows]
+        up_line = jnp.concatenate(
+            [jnp.where(place_ref[0] == b, up_line, 0.0) for b in range(blocks)], axis=1
+        ).astype(BF)
+
+        def store(ref, owner=owner, qkv=qkv, out=out, lines=lines, up_line=up_line):
+            ref[owner // 2, 0:own_rows, 0:third] = qkv
+            ref[owner // 2, 0:own_rows, third:] = out
+            ref[owner // 2, own_rows:, :] = jnp.zeros((16, third + width), BF)
+            ref[owner // 2, own_rows : own_rows + 8, 0:own_rows] = lines
+            ref[owner // 2, own_rows + 8 : own_rows + 9, 0 : up_line.shape[1]] = up_line
+
+        @pl.when(bit == owner % 2)
+        def keep():
+            store(kept_ref)
+
+        @pl.when(bit != owner % 2)
+        def send():
+            store(sent_ref)
+
+
+def block_kernel(blocks, place_ref, kept_ref, arrived_ref, *out_refs):
+    total = kept_ref[0].astype(F32) + arrived_ref[0].astype(F32)
+    own_rows = total.shape[0] - 16
+    size = own_rows // blocks
+    for m in range(blocks):
+        chosen = total[:size]
+        for j in range(1, blocks):
+            chosen = jnp.where(place_ref[0] ^ m == j, total[j * size : (j + 1) * size], chosen)
+        out_refs[m][0:size, :] = chosen.astype(BF)
+        out_refs[m][size:, :] = total[own_rows:].astype(BF)
+
+
+def seq_kernel(blocks, seqs, place_ref, *refs):
+    in_refs, main_ref, out_refs = refs[:blocks], refs[blocks], refs[blocks + 1 :]
+    terms = [ref[...].astype(F32) for ref in in_refs]
+    while len(terms) > 1:
+        terms = [terms[i] + terms[i + 1] for i in range(0, len(terms), 2)]
+    total = terms[0]
+    size = total.shape[0] - 16
+    width = main_ref.shape[1]
+    head = width // seqs
+    third = 3 * head
+    main_ref[...] = total[:, :width].astype(BF)
+    for j in range(seqs):
+        chosen = total[:size, third : third + head]
+        for k in range(1, seqs):
+            first = third + k * head
+            chosen = jnp.where(place_ref[1] ^ j == k, total[:size, first : first + head], chosen)
+        out_refs[j][...] = chosen.astype(BF)
+
+
+def join_kernel(seqs, main_ref, *refs):
+    out_ref = refs[seqs]
+    size, head = refs[0].shape
+    out_ref[...] = main_ref[...]
+    total = sum(ref[...].astype(F32) for ref in refs[:seqs])
+    out_ref[0:size, 3 * head :] = total.astype(BF)
+
+
 def first_back_kernel(pieces, *refs):
     part_refs, (tokens_ref, d_middle_ref, gain_ref, out_ref) = refs[:pieces], refs[pieces:]
     upstream = sum(ref[...].astype(F32) for ref in part_refs)
@@ -313,54 +495,46 @@
                     out[row : row + rows, column : column + size] = piece.astype(F32)
 
 
-def run(kernel, label, outs, scalars, remote, arrays, scratch=(), flops=0, powers=0):
-    moved = sum(one.size * one.dtype.itemsize for one in (*remote, *arrays))
-    moved += sum(one.size * one.dtype.itemsize for one in outs)
+def run(kernel, label, outs, scalars, remote, arrays, scratch=(), waits=(), in_hbm=False):
+    inputs = len(scalars) + len(remote) + len(arrays)
+
+    def without_waits(*refs):
+        kernel(*refs[:inputs], *refs[inputs + len(waits) :])
+
     return pl.pallas_call(
-        kernel,
+        without_waits,
         out_shape=tuple(outs),
         in_specs=[pl.BlockSpec(memory_space=pltpu.SMEM)] * len(scalars)
-        + [pl.BlockSpec(memory_space=pl.ANY)] * len(remote)
-        + [pl.BlockSpec(memory_space=pltpu.VMEM)] * len(arrays),
-        out_specs=(pl.BlockSpec(memory_space=pltpu.VMEM),) * len(outs),
+        + [pl.BlockSpec(memory_space=pltpu.HBM)] * len(remote)
+        + [pl.BlockSpec(memory_space=pltpu.VMEM)] * len(arrays)
+        + [pl.BlockSpec(memory_space=pltpu.HBM)] * len(waits),
+        out_specs=(pl.BlockSpec(memory_space=pltpu.HBM if in_hbm else pltpu.VMEM),) * len(outs),
         scratch_shapes=list(scratch),
         compiler_params=pltpu.CompilerParams(vmem_limit_bytes=VMEM_LIMIT),
-        cost_estimate=pl.CostEstimate(flops=flops, bytes_accessed=moved, transcendentals=powers),
+        cost_estimate=pl.CostEstimate(flops=1, bytes_accessed=1, transcendentals=0),
         name=label,
-    )(*scalars, *remote, *arrays)
+    )(*scalars, *remote, *arrays, *waits)
 
 
 def shape(dims, kind):
     return jax.ShapeDtypeStruct(tuple(dims), kind)
 
 
-def after(value, *others):
-    return lax.optimization_barrier((value, others))[0]
-
-
-def pick(pairs, axis, index):
-    return sum(
-        lax.dynamic_index_in_dim(one, index, axis, keepdims=False).astype(F32) for one in pairs
-    )
-
-
-def owner_sums(kept, arrived, own):
-    terms, sent = (kept, arrived), None
-    bit = 2
+def owner_sums(kept, arrived, place, label):
+    sent, bit = None, 2
     while bit < lax.axis_size("fsdp"):
-        terms = tuple(one.reshape(one.shape[0] // 2, 2, *one.shape[1:]) for one in terms)
-        high = (own // bit) % 2
-        sent = pick(terms, 1, 1 - high).astype(BF)
-        terms = (pick(terms, 1, high), swap(sent, "fsdp", bit))
+        half = (kept.shape[0] // 2, *kept.shape[1:])
+        sent, kept = run(
+            functools.partial(step_kernel, bit),
+            label,
+            [shape(half, BF)] * 2,
+            [place],
+            [],
+            [kept, arrived],
+        )
+        arrived = swap(sent, "fsdp", bit)
         bit *= 2
-    return tuple(one[0] for one in terms), sent
-
-
-def chunk_sums(terms, axis, index):
-    total = pick(terms, 0, index)
-    for j in range(1, lax.axis_size(axis)):
-        total = total + swap(pick(terms, 0, index ^ j).astype(BF), axis, j).astype(F32)
-    return total
+    return kept, arrived, sent
 
 
 def sum_parts(parts, axis):
@@ -372,20 +546,6 @@
     while len(pieces) > 1:
         pieces = [pieces[i] + pieces[i + 1] for i in range(0, len(pieces), 2)]
     return pieces[0]
-
-
-def in_order(pieces, index):
-    result = []
-    for place in range(len(pieces)):
-        chosen = pieces[place]
-        for other in range(1, len(pieces)):
-            chosen = jnp.where(index == other, pieces[place ^ other], chosen)
-        result.append(chosen)
-    return result
-
-
-def padded(rows, count, width):
-    return jnp.pad(rows, ((0, 0), (0, count - rows.shape[1]), (0, width - rows.shape[2])))
 
 
 def shards(
@@ -396,50 +556,55 @@
     place = jnp.stack([blk, seq, own]).astype(jnp.int32)
     rows, width = tokens.shape[1:]
     head_width = width // seqs
+    heads, third = head_width // HD, 3 * head_width
     own_rows = width // owners
     hidden_rows = w_down.shape[0] // blocks
     hidden_width = hidden_rows * owners
     parts = hidden_width // width
+    block_rows, all_rows = seqs * rows, blocks * rows
     inputs, grad_in = tokens[0], grad_out[0]
     vmem, dma = pltpu.VMEM, pltpu.SemaphoreType.DMA
 
-    normed1, d_outcome = run(
+    normed1, d_outcome, qkv_mine = run(
         functools.partial(prepare_kernel, seqs),
         "prepare",
-        [shape((rows, width), BF)] * 2,
+        [shape((rows, width), BF)] * 2 + [shape((own_rows, third), BF)],
         [place, counts],
         [],
-        [inputs, grad_in, norm_gain, norm_bias],
+        [inputs, grad_in, norm_gain, norm_bias, w_qkv],
     )
     normed1_pieces = from_all(normed1, "seq")
-    qkv_late = after(w_qkv, normed1)
-    qkv_mine = jnp.concatenate(
-        [
-            lax.dynamic_slice_in_dim(qkv_late, part * width + seq * head_width, head_width, axis=1)
-            for part in range(3)
-        ],
-        axis=1,
-    )
     qkv_pieces = doubled(qkv_mine, "fsdp")
-    qkv_full = jnp.concatenate(in_order(qkv_pieces, own))
-
-    up_late, down_late, out_late = after((w_up, w_down, w_out), qkv_mine)
-    up_columns = [
-        lax.dynamic_slice_in_dim(up_late, (i * blocks + blk) * hidden_rows, hidden_rows, axis=1)
-        for i in range(owners)
-    ]
-    in_part = owners // parts
-    weights_mine = jnp.concatenate(
-        [out_late]
-        + [
-            jnp.concatenate(up_columns[part * in_part : (part + 1) * in_part], axis=1)
-            for part in range(parts)
+    out_pieces = doubled(w_out, "fsdp")
+    outcome_pieces = from_all(d_outcome, "blk")
+
+    packed = shape((parts * own_rows + hidden_rows, width), BF)
+    if hidden_rows % 128 == 0:
+        (weights_mine,) = run(
+            functools.partial(pack_kernel, owners, blocks, parts),
+            "pack",
+            [packed],
+            [place],
+            [w_up, w_down],
+            [],
+            [dma((owners + 1,))],
+            waits=[qkv_pieces[owners // 2], out_pieces[owners // 2]],
+            in_hbm=True,
+        )
+    else:
+        columns = [
+            lax.dynamic_slice_in_dim(w_up, (i * blocks + blk) * hidden_rows, hidden_rows, axis=1)
+            for i in range(owners)
         ]
-        + [lax.dynamic_slice_in_dim(down_late, blk * hidden_rows, hidden_rows, axis=0)]
-    )
-    weights = doubled(after(weights_mine, qkv_pieces[owners // 2]), "fsdp")
-    outcome_pieces = from_all(after(d_outcome, weights_mine), "blk")
-    gain_row, shift_row = norm_gain[0].astype(F32), norm_bias[0].astype(F32)
+        in_part = owners // parts
+        weights_mine = jnp.concatenate(
+            [
+                jnp.concatenate(columns[part * in_part : (part + 1) * in_part], axis=1)
+                for part in range(parts)
+            ]
+            + [lax.dynamic_slice_in_dim(w_down, blk * hidden_rows, hidden_rows, axis=0)]
+        )
+    weights = doubled(weights_mine, "fsdp")
     biases = vec_bias.astype(F32)
     qkv_shift = jnp.concatenate(
         [
@@ -447,28 +612,27 @@
             jnp.zeros((head_width,), F32),
             lax.dynamic_slice_in_dim(biases[1], seq * head_width, head_width),
         ]
-    )
+    ).reshape(1, third)
     up_shift = (
-        jnp.concatenate(
-            [
-                lax.dynamic_slice_in_dim(up_bias, (i * blocks + blk) * hidden_rows, hidden_rows)
-                for i in range(owners)
-            ]
-        )
+        lax.dynamic_index_in_dim(up_bias.reshape(owners, blocks, hidden_rows), blk, 1, False)
         .astype(F32)
         .reshape(1, hidden_width)
     )
 
-    normed1_all = jnp.concatenate(normed1_pieces)
-    key_value = (
-        dot_nn(normed1_all, qkv_full[:, head_width:]) + qkv_shift[head_width:]
-    ).astype(BF)
+    key_value, queries, qkv_full = run(
+        functools.partial(qkv_kernel, owners, seqs),
+        "project_in",
+        [
+            shape((block_rows, 2 * head_width), BF),
+            shape((block_rows, head_width), BF),
+            shape((width, third), BF),
+        ],
+        [place],
+        qkv_pieces,
+        [*normed1_pieces, qkv_shift],
+        [dma((owners,))],
+    )
     kv_blocks = from_all(key_value, "blk")
-    queries = (
-        dot_nn(after(normed1_all, key_value), qkv_full[:, :head_width]) + qkv_shift[:head_width]
-    ).astype(BF)
-    block_rows, heads = seqs * rows, head_width // HD
-    powers = block_rows * block_rows * blocks * heads
     *att_out, log_total = run(
         functools.partial(attend_kernel, blocks, heads, seqs, rows),
         "attend",
@@ -476,23 +640,19 @@
         [place, counts],
         [],
         [queries, *kv_blocks],
-        flops=4 * HD * powers,
-        powers=powers,
     )
     att_pieces = sum_parts(att_out, "seq")
     middle, normed2 = run(
         functools.partial(project_kernel, owners, seqs),
-        "project",
+        "project_out",
         [shape((rows, width), F32), shape((rows, width), BF)],
         [place],
-        weights,
+        out_pieces,
         [*att_pieces, inputs, vec_bias, norm_gain, norm_bias],
         [vmem((width, width), BF), dma((owners,))],
-        flops=2 * rows * width * width,
     )
 
     normed_pieces = from_all(normed2, "blk")
-    all_rows = blocks * rows
     row_shapes = [shape((rows, width), F32)] + [shape((rows, width), BF)] * (blocks - 1)
     hidden, d_up, up_sums, *rest = run(
         functools.partial(hidden_kernel, owners, blocks, own_rows, hidden_rows),
@@ -508,127 +668,120 @@
             vmem((hidden_width, width), BF),
             dma((parts + 1, owners)),
         ],
-        flops=8 * all_rows * width * hidden_width,
-        powers=2 * all_rows * hidden_width,
-    )
-    d_normed_parts, result_parts = rest[:blocks], rest[blocks:]
-    d_normed_pieces = sum_parts(d_normed_parts, "blk")
+    )
+    d_normed_pieces = sum_parts(rest[:blocks], "blk")
     chunk, up_chunk = hidden_rows // seqs, own_rows // seqs
     chunk_rows = chunk + parts * up_chunk
     sent, kept = run(
         functools.partial(grads_kernel, owners, seqs, blocks, own_rows, hidden_rows),
-        "grads",
+        "feed_grads",
         [shape((owners // 2, seqs, chunk_rows, width), BF)] * 2,
         [place],
         [],
         [*normed_pieces, *outcome_pieces, hidden, d_up],
-        flops=4 * all_rows * width * hidden_width,
-    )
-    arrived = swap(sent, "fsdp", 1)
+    )
     d_middle, d_branch, middle_sums, *d_heads = run(
         functools.partial(middle_kernel, owners, seqs, blocks),
         "middle",
         [shape((rows, width), F32), shape((rows, width), BF), shape((4, width), F32)]
         + [shape((rows, head_width), BF)] * seqs,
         [place, counts],
-        weights,
-        [*after(tuple(d_normed_pieces), sent), middle, grad_in, norm_gain],
+        out_pieces,
+        [*d_normed_pieces, middle, grad_in, norm_gain],
         [vmem((width, width), BF), dma((owners,))],
-        flops=2 * rows * width * width,
+        waits=[sent],
     )
     d_att_pieces = sum_parts(d_heads, "seq")
-    own_terms, feed_sent = owner_sums(kept, arrived, own)
-
-    att_late, branch_late = after((tuple(att_pieces), d_branch), *d_heads)
-    token_att = jnp.concatenate(in_order(att_late, seq), axis=1)
-    early = jnp.concatenate(
-        [
-            padded(
-                middle_sums.reshape(4, owners, own_rows).transpose(1, 0, 2), 4, width
-            ),
-            padded(
-                jnp.where(
-                    (jnp.arange(blocks) == blk)[None, :, None],
-                    up_sums.reshape(owners, 1, hidden_rows),
-                    0.0,
-                ).reshape(owners, 1, blocks * hidden_rows),
-                12,
-                width,
-            ),
-        ],
-        axis=1,
-    ).astype(BF)
-    out_grads = jnp.concatenate(
-        [dot_tn(token_att, branch_late).astype(BF).reshape(owners, own_rows, width), early], axis=1
-    )
-    out_sums = lax.psum(
-        lax.psum_scatter(
-            out_grads.reshape(owners * (own_rows + 16), width),
-            "fsdp",
-            scatter_dimension=0,
-            tiled=True,
-        ),
-        ("blk", "seq"),
-    ).astype(F32)
-
-    d_query, d_kv, *d_kv_sent = run(
+    kept, arrived, sent = owner_sums(kept, swap(sent, "fsdp", 1), place, "feed_step")
+
+    d_query, *d_kv = run(
         functools.partial(attend_back_kernel, blocks, heads, seqs, rows),
         "attend_back",
         [shape((block_rows, head_width), BF), shape((block_rows, 2 * head_width), F32)]
         + [shape((block_rows, 2 * head_width), BF)] * (blocks - 1),
-        [after(place, feed_sent), counts],
+        [place, counts],
         [],
         [queries, log_total, *d_att_pieces, *kv_blocks],
-        flops=10 * HD * powers,
-        powers=powers,
-    )
-    for m in range(1, blocks):
-        d_kv = d_kv + swap(d_kv_sent[m - 1], "blk", m).astype(F32)
-    d_kv = after(d_kv.astype(BF), own_terms)
-    d_projected = jnp.concatenate([d_query, d_kv], axis=1)
-    d_normed1_all = dot_nt(d_projected, qkv_full).astype(BF)
-    d_normed1_pieces = sum_parts(
-        [d_normed1_all[k * rows : (k + 1) * rows] for k in range(seqs)], "seq"
-    )
-    feed_sums = chunk_sums(own_terms, "seq", seq).astype(BF)
-
-    normed1_late, result_late = after((normed1_all, tuple(result_parts[1:])), d_normed1_all)
-    qkv_grads = dot_tn(normed1_late, d_projected)
-    column_sums = jnp.sum(d_projected.astype(F32), axis=0)
-    unit_grads = (qkv_grads - shift_row[:, None] * column_sums[None, :]) / gain_row[:, None]
-    qkv_float = qkv_full.astype(F32)
-    is_seq = (jnp.arange(seqs) == seq)[:, None]
-    late = jnp.stack(
+        waits=[sent],
+    )
+    d_projected, column_sums, first_sums, *d_normed1 = run(
+        functools.partial(project_back_kernel, blocks, seqs),
+        "project_back",
         [
-            jnp.sum(qkv_float * unit_grads, axis=1),
-            jnp.sum(qkv_float * column_sums[None, :], axis=1),
-            jnp.where(is_seq, column_sums[None, :head_width], 0.0).reshape(-1),
-            jnp.where(is_seq, column_sums[None, 2 * head_width :], 0.0).reshape(-1),
+            shape((block_rows, third), BF),
+            shape((1, third), F32),
+            shape((2, width), F32),
         ]
-    )
-    late = padded(late.reshape(4, owners, own_rows).transpose(1, 0, 2), 16, 3 * head_width)
-    qkv_grads = jnp.concatenate(
-        [qkv_grads.astype(BF).reshape(owners, own_rows, 3 * head_width), late.astype(BF)], axis=1
-    ).reshape(owners // 2, 2, own_rows + 16, 3 * head_width)
-    qkv_arrived = swap(
-        lax.dynamic_index_in_dim(qkv_grads, 1 - own % 2, 1, keepdims=False), "fsdp", 1
-    )
-    qkv_terms, _ = owner_sums(
-        lax.dynamic_index_in_dim(qkv_grads, own % 2, 1, keepdims=False), qkv_arrived, own
-    )
-    qkv_own = sum(one.astype(F32) for one in qkv_terms)
+        + [shape((rows, width), BF)] * seqs,
+        [],
+        [],
+        [d_query, *sum_parts(d_kv, "blk"), qkv_full, *normed1_pieces, norm_gain, norm_bias],
+    )
+    d_normed1_pieces = sum_parts(d_normed1, "seq")
+    feed_chunks = run(
+        functools.partial(chunk_kernel, seqs),
+        "feed_chunks",
+        [shape((chunk_rows, width), BF)] * seqs,
+        [place],
+        [],
+        [kept, arrived],
+    )
+    (feed_sums,) = run(
+        add_kernel,
+        "feed_sums",
+        [shape((chunk_rows, width), BF)],
+        [],
+        [],
+        sum_parts(feed_chunks, "seq"),
+    )
+    feed_seq = from_all(feed_sums, "seq")
+
+    sent, kept = run(
+        functools.partial(last_grads_kernel, owners, seqs, blocks),
+        "last_grads",
+        [shape((owners // 2, own_rows + 16, third + width), BF)] * 2,
+        [place],
+        [],
+        [
+            *normed1_pieces,
+            *att_pieces,
+            d_projected,
+            d_branch,
+            column_sums,
+            first_sums,
+            middle_sums,
+            up_sums,
+        ],
+        [vmem((seqs, rows, head_width), BF)],
+        waits=[feed_chunks[0]],
+    )
+    kept, arrived, _ = owner_sums(kept, swap(sent, "fsdp", 1), place, "last_step")
     blk_rows = own_rows // blocks
-
-    def qkv_part(index):
-        return jnp.concatenate(
-            [lax.dynamic_slice_in_dim(qkv_own, index * blk_rows, blk_rows), qkv_own[own_rows:]]
-        )
-
-    qkv_sums = tree_sum(
-        [qkv_part(blk).astype(BF)]
-        + [swap(qkv_part(blk ^ m).astype(BF), "blk", m) for m in range(1, blocks)]
-    ).astype(BF)
-
+    last_blocks = run(
+        functools.partial(block_kernel, blocks),
+        "last_blocks",
+        [shape((blk_rows + 16, third + width), BF)] * blocks,
+        [place],
+        [],
+        [kept, arrived],
+    )
+    last_main, *out_chunks = run(
+        functools.partial(seq_kernel, blocks, seqs),
+        "last_chunks",
+        [shape((blk_rows + 16, width), BF)] + [shape((blk_rows, head_width), BF)] * seqs,
+        [place],
+        [],
+        sum_parts(last_blocks, "blk"),
+    )
+    (last_sums,) = run(
+        functools.partial(join_kernel, seqs),
+        "last_sums",
+        [shape((blk_rows + 16, width), BF)],
+        [],
+        [],
+        [last_main, *sum_parts(out_chunks, "seq")],
+    )
+    last_seq = from_all(last_sums, "seq")
     (grad_tokens,) = run(
         functools.partial(first_back_kernel, seqs),
         "first_back",
@@ -636,18 +789,14 @@
         [],
         [],
         [*d_normed1_pieces, inputs, d_middle, norm_gain],
-    )
-    outcome = result_parts[0]
-    for m in range(1, blocks):
-        outcome = outcome + swap(result_late[m - 1], "blk", m).astype(F32)
+        waits=[feed_sums],
+    )
+    outcome = sum(one.astype(F32) for one in sum_parts(rest[blocks:], "blk"))
     valid = lax.broadcasted_iota(jnp.int32, (rows, 1), 0) < counts[0, blk * seqs + seq]
     activations = jnp.where(valid, middle + outcome + biases[3], 0.0)
 
-    feed_seq = from_all(feed_sums, "seq")
     feed_all = [from_all(one, "blk") for one in feed_seq]
-    qkv_seq = from_all(qkv_sums, "seq")
-    qkv_all = [from_all(one, "blk") for one in qkv_seq]
-    held = pltpu.VMEM((blocks, seqs, chunk_rows, width), BF)
+    last_all = [from_all(one, "blk") for one in last_seq]
     grad_down, grad_up = run(
         functools.partial(
             place_kernel,
@@ -670,12 +819,13 @@
         ),
         "place_feed",
         [shape((blocks * hidden_rows, width), F32), shape((own_rows, blocks * hidden_width), F32)],
-        [after(place, qkv_seq)],
+        [place],
         [feed_all[k][m] for m in range(blocks) for k in range(seqs)],
         [],
-        [held, dma((blocks * seqs,))],
-    )
-    (grad_qkv,) = run(
+        [vmem((blocks, seqs, chunk_rows, width), BF), dma((blocks * seqs,))],
+        waits=last_seq[1:],
+    )
+    grad_qkv, grad_w_out = run(
         functools.partial(
             place_kernel,
             seqs,
@@ -691,30 +841,28 @@
                         i * width + k * head_width,
                     )
                     for i in range(3)
-                ]
+                ],
+                lambda b, k: [(0, blk_rows, third, head_width, b * blk_rows, k * head_width)],
             ],
         ),
-        "place_qkv",
-        [shape((own_rows, 3 * width), F32)],
-        [place],
-        [qkv_all[k][m] for m in range(blocks) for k in range(seqs)],
-        [],
-        [
-            pltpu.VMEM((blocks, seqs, blk_rows + 16, 3 * head_width), BF),
-            dma((blocks * seqs,)),
-        ],
-    )
-    late_sums = tree_sum([one[blk_rows : blk_rows + 4, :own_rows] for one in qkv_seq])
-    early_sums = out_sums[own_rows : own_rows + 4, :own_rows]
+        "place_last",
+        [shape((own_rows, 3 * width), F32), shape((own_rows, width), F32)],
+        [place],
+        [last_all[k][m] for m in range(blocks) for k in range(seqs)],
+        [],
+        [vmem((blocks, seqs, blk_rows + 16, width), BF), dma((blocks * seqs,))],
+    )
+    small = tree_sum([one[blk_rows:] for one in last_seq])
+    lines = small[:8, :own_rows]
     return (
         activations[None],
         grad_tokens[None],
-        jnp.stack([late_sums[0], early_sums[0]]),
-        jnp.stack([late_sums[1], early_sums[1]]),
-        jnp.stack([late_sums[2], late_sums[3], early_sums[2], early_sums[3]]),
-        out_sums[own_rows + 4, : blocks * hidden_rows],
+        jnp.stack([lines[0], lines[4]]),
+        jnp.stack([lines[1], lines[5]]),
+        jnp.stack([lines[2], lines[3], lines[6], lines[7]]),
+        small[8, : blocks * hidden_rows],
         grad_qkv,
-        out_sums[:own_rows],
+        grad_w_out,
         grad_up,
         grad_down,
     )

time: 343 us -> 297 us (0.87)
  other arithmetic: 22.7 us -> 4.38 us
  Pallas kernels: 34.7 us -> 49.5 us
  local copies, waits for them, and re-layouts: 27.7 us -> 13.4 us
  between operations: 14.9 us -> 1.29 us
  waiting for transfers between devices: 166 us -> 158 us
  matrix products: 6.26 us -> 0 us
    psum x1 -> x0, waiting for transfers between devices: 44.3 us -> none  [shards(): lax.psum(lax.psum_scatter(out_grads.reshape(owners * (own_rows + 16), wid...]
    ppermute x46 -> x52, waiting for transfers between devices: 122 us -> 158 us  [swap(): lax.ppermute(array, axis, [(i, i ^ bits) for i in range(lax.axis_size(axi...]
    pallas_call x10 -> x21, Pallas kernels: 34.7 us -> 49.5 us  [run(): pl.pallas_call(without_waits, out_shape=tuple(outs), in_specs=[pl.BlockSp...]
    dot_general x5 -> x0, matrix products: 6.26 us -> none  [the longest x2 3.55 us: dot_tn(): lax.dot_general(left_side, right_side, (((0,), (0,)), ((), ())), preferre...]
    add x2 -> x0, other arithmetic: 5.83 us -> none  [the longest x1 4.77 us: pick(): sum((lax.dynamic_index_in_dim(one, index, axis, keepdims=False).astype(F3...]
    unnamed x112 -> x84, local copies, waits for them, and re-layouts: 17.2 us -> 12.1 us
    convert_element_type x9 -> x1, other arithmetic: 4.92 us -> 0.01 us  [shards(): up_shift = lax.dynamic_index_in_dim(up_bias.reshape(owners, blocks, hidde...]
    slice x8 -> x3, local copies, waits for them, and re-layouts: 4.58 us -> 0.62 us  [the longest x1 0.6 us: shards(): small[8, :blocks * hidden_rows]]
  transfers between devices with their start and end apart: 48 -> 52, of which waited for: 20 -> 24; matrix products, arithmetic and copies ran while one was open for 11% -> 2% of each run, Pallas kernels for 4% -> 9%
where the time goes in v1:
time: 297 us; the launch traced here: 294 us
  waiting for transfers between devices  158 us (53%)
  starting transfers between devices  67.8 us (23%)
  Pallas kernels  49.5 us (17%)
  local copies, waits for them, and re-layouts  13.4 us (5%)
  other arithmetic  4.38 us (1%)
    ppermute x52, waiting for transfers between devices, swap(): lax.ppermute(array, axis, [(i, i ^ bits) for i in range(lax.axis_size(axi...  158 us
    ppermute x52, starting transfers between devices, swap(): lax.ppermute(array, axis, [(i, i ^ bits) for i in range(lax.axis_size(axi...  67.8 us
    pallas_call x21, Pallas kernels, run(): pl.pallas_call(without_waits, out_shape=tuple(outs), in_specs=[pl.BlockSp...  49.5 us
    unnamed x84, local copies, waits for them, and re-layouts  12.1 us
  transfers between devices with their start and end apart: 52, of which 24 were waited for; matrix products, arithmetic and copies ran while one was open for 2% of the time, Pallas kernels for 9%

profile of v1, /device:TPU:0, one launch (start us, length us, event | category | flops | bytes accessed | tf_op | source)
XLA Modules:
  0.0 294.2 jit_solution(7897843488088157392)
XLA Ops:
  0.6 3.0 %collective-permute-start.1 = (bf16[192,768]{1,0:T(8,128)(2,1)}, bf16[192,768]{1,0:T(8,128)(2,1)S(1)}, u32[]{:S(2)}, u32[]{:S(2)}) collective-permute-start(bf16[192,768]{1,0:T(8,128)(2,1)} %refs_2_.3), channel_id=1, source_target_pairs={{0,16},{8,24},{16,0},{24,8},{1,17},{9,25},{17,1},{25,9},{2,18},{10... | collective-permute-start | bytes 884744 | tf_op jit(solution)/shard_map/ppermute | solution.py:38
  10.8 7.4 %collective-permute-done.4.refs_3_ = bf16[192,576]{1,0:T(8,128)(2,1)S(1)} collective-permute-done((bf16[192,576]{1,0:T(8,128)(2,1)S(1)}, bf16[192,576]{1,0:T(8,128)(2,1)S(1)}, u32[]{:S(2)}, u32[]{:S(2)}) %collective-permute-start.4) | collective-permute-done | bytes 221216 | tf_op jit(solution)/shard_map/ppermute | solution.py:38
  20.7 26.3 %collective-permute-done.14.refs_3_ = bf16[768,768]{1,0:T(8,128)(2,1)} collective-permute-done((bf16[768,768]{1,0:T(8,128)(2,1)S(1)}, bf16[768,768]{1,0:T(8,128)(2,1)}, u32[]{:S(2)}, u32[]{:S(2)}) %collective-permute-start.14) | collective-permute-done | bytes 1179680 | tf_op jit(solution)/shard_map/ppermute | solution.py:38
  51.7 6.7 %collective-permute-done.6.refs_6_.refs_5_.refs_2_ = bf16[128,768]{1,0:T(8,128)(2,1)S(1)} collective-permute-done((bf16[128,768]{1,0:T(8,128)(2,1)S(1)}, bf16[128,768]{1,0:T(8,128)(2,1)S(1)}, u32[]{:S(2)}, u32[]{:S(2)}) %collective-permute-start.6) | collective-permute-done | bytes 196640 | tf_op jit(solution)/shard_map/ppermute | solution.py:38
  61.1 5.2 %collective-permute-done.8.refs_8_.refs_7_.refs_4_ = bf16[128,768]{1,0:T(8,128)(2,1)S(1)} collective-permute-done((bf16[128,768]{1,0:T(8,128)(2,1)S(1)}, bf16[128,768]{1,0:T(8,128)(2,1)S(1)}, u32[]{:S(2)}, u32[]{:S(2)}) %collective-permute-start.8) | collective-permute-done | bytes 196640 | tf_op jit(solution)/shard_map/ppermute | solution.py:38
  73.6 7.2 %collective-permute-done.9.refs_4_.refs_9_ = bf16[512,384]{1,0:T(8,128)(2,1)S(1)} collective-permute-done((bf16[512,384]{1,0:T(8,128)(2,1)S(1)}, bf16[512,384]{1,0:T(8,128)(2,1)S(1)}, u32[]{:S(2)}, u32[]{:S(2)}) %collective-permute-start.9) | collective-permute-done | bytes 393248 | tf_op jit(solution)/shard_map/ppermute | solution.py:38
  81.5 3.9 %attend.1 = (bf16[128,192]{1,0:T(8,128)(2,1)S(1)}, bf16[128,192]{1,0:T(8,128)(2,1)S(1)}, bf16[128,192]{1,0:T(8,128)(2,1)S(1)}, bf16[128,192]{1,0:T(8,128)(2,1)S(1)}, f32[3,512]{1,0:T(4,128)S(1)}) custom-call(s32[3]{0:T(128)S(1)} %pad_add_fusion.refs_0_, s32[1,8]{1,0:T(1,128)S(1)} %copy-done.38, bf16[512,192]{1,0:T(8,128)(2,1)S(1)} %get-tuple-element.72.refs_2_, ...), custom_call_target="tpu_custom_call" | custom-call | flops 1 | bytes 1 | tf_op jit(solution)/shard_map/attend/pallas_call | solution.py:504
  85.4 5.3 %collective-permute-start.10 = (bf16[128,192]{1,0:T(8,128)(2,1)S(1)}, bf16[128,192]{1,0:T(8,128)(2,1)S(1)}, u32[]{:S(2)}, u32[]{:S(2)}) collective-permute-start(bf16[128,192]{1,0:T(8,128)(2,1)S(1)} %get-tuple-element.75), channel_id=1, source_target_pairs={{0,1},{1,0},{2,3},{3,2},{4,5},{5,4},{6,7},{7,6},{8,9},{9,8},{10,11... | collective-permute-start | bytes 147464 | tf_op jit(solution)/shard_map/ppermute | solution.py:38
  94.6 3.1 %collective-permute-done.11.refs_7_ = bf16[128,192]{1,0:T(8,128)(2,1)S(1)} collective-permute-done((bf16[128,192]{1,0:T(8,128)(2,1)S(1)}, bf16[128,192]{1,0:T(8,128)(2,1)S(1)}, u32[]{:S(2)}, u32[]{:S(2)}) %collective-permute-start.11) | collective-permute-done | bytes 49184 | tf_op jit(solution)/shard_map/ppermute | solution.py:38
  102.2 4.4 %collective-permute-done.16.refs_6_.refs_2_ = bf16[128,768]{1,0:T(8,128)(2,1)} collective-permute-done((bf16[128,768]{1,0:T(8,128)(2,1)}, bf16[128,768]{1,0:T(8,128)(2,1)}, u32[]{:S(2)}, u32[]{:S(2)}) %collective-permute-start.16) | collective-permute-done | bytes 196640 | tf_op jit(solution)/shard_map/ppermute | solution.py:38
  106.7 7.2 %hidden.1 = (bf16[256,1536]{1,0:T(8,128)(2,1)S(1)}, bf16[256,1536]{1,0:T(8,128)(2,1)S(1)}, f32[1,1536]{1,0:T(1,128)S(1)}, f32[128,768]{1,0:T(8,128)S(1)}, bf16[1...) custom-call(s32[3]{0:T(128)S(1)} %pad_add_fusion.refs_0_, ...), custom_call_target="tpu_custom_call" | custom-call | flops 1 | bytes 1 | tf_op jit(solution)/shard_map/hidden/pallas_call | solution.py:504
  114.7 3.9 %feed_grads.1 = (bf16[2,4,192,768]{3,2,1,0:T(8,128)(2,1)S(1)}, bf16[2,4,192,768]{3,2,1,0:T(8,128)(2,1)S(1)}) custom-call(s32[3]{0:T(128)S(1)} %pad_add_fusion.refs_0_, bf16[128,768]{1,0:T(8,128)(2,1)} %get-tuple-element.79.refs_5_.refs_1_, bf16[128,768]{1,0:T(8,128)(2,1)} %collective-permute-done.16.refs_6_.refs_2_, ...), custom_call_target="tpu_custom_call" | custom-call | flops 1 | bytes 1 | tf_op jit(solution)/shard_map/feed_grads/pallas_call | solution.py:504
  118.7 4.5 %collective-permute-done.23.refs_2_ = bf16[2,4,192,768]{3,2,1,0:T(8,128)(2,1)S(1)} collective-permute-done((bf16[2,4,192,768]{3,2,1,0:T(8,128)(2,1)S(1)}, bf16[2,4,192,768]{3,2,1,0:T(8,128)(2,1)S(1)}, u32[]{:S(2)}, u32[]{:S(2)}) %collective-permute-start.23) | collective-permute-done | bytes 2359328 | tf_op jit(solution)/shard_map/ppermute | solution.py:38
  126.4 5.0 %collective-permute-done.19.refs_7_ = bf16[128,768]{1,0:T(8,128)(2,1)S(1)} collective-permute-done((bf16[128,768]{1,0:T(8,128)(2,1)S(1)}, bf16[128,768]{1,0:T(8,128)(2,1)S(1)}, u32[]{:S(2)}, u32[]{:S(2)}) %collective-permute-start.19) | collective-permute-done | bytes 196640 | tf_op jit(solution)/shard_map/ppermute | solution.py:38
  138.7 3.9 %collective-permute-done.21.refs_6_ = bf16[128,192]{1,0:T(8,128)(2,1)S(1)} collective-permute-done((bf16[128,192]{1,0:T(8,128)(2,1)S(1)}, bf16[128,192]{1,0:T(8,128)(2,1)S(1)}, u32[]{:S(2)}, u32[]{:S(2)}) %collective-permute-start.21) | collective-permute-done | bytes 49184 | tf_op jit(solution)/shard_map/ppermute | solution.py:38
  142.6 5.6 %attend_back.1 = (bf16[512,192]{1,0:T(8,128)(2,1)S(1)}, f32[512,384]{1,0:T(8,128)S(1)}, bf16[512,384]{1,0:T(8,128)(2,1)S(1)}) custom-call(s32[3]{0:T(128)S(1)} %pad_add_fusion.refs_0_, s32[1,8]{1,0:T(1,128)S(1)} %copy-done.39, bf16[512,192]{1,0:T(8,128)(2,1)S(1)} %copy-done.15, f32[3,512]{1,0:T(4,128)S(1)} %get-tuple-element.83.refs_3_, ...), custom_call_target="tpu_custom_call" | custom-call | flops 1 | bytes 1 | tf_op jit(solution)/shard_map/attend_back/pallas_call | solution.py:504
  149.8 6.7 %collective-permute-done.24.refs_2_ = bf16[512,384]{1,0:T(8,128)(2,1)S(1)} collective-permute-done((bf16[512,384]{1,0:T(8,128)(2,1)S(1)}, bf16[512,384]{1,0:T(8,128)(2,1)S(1)}, u32[]{:S(2)}, u32[]{:S(2)}) %collective-permute-start.24) | collective-permute-done | bytes 393248 | tf_op jit(solution)/shard_map/ppermute | solution.py:38
  159.7 3.4 %last_grads.1 = (bf16[2,208,1344]{2,1,0:T(8,128)(2,1)S(1)}, bf16[2,208,1344]{2,1,0:T(8,128)(2,1)S(1)}) custom-call(s32[3]{0:T(128)S(1)} %pad_add_fusion.refs_0_, bf16[128,768]{1,0:T(8,128)(2,1)S(1)} %get-tuple-element.71.refs_5_.refs_4_.refs_1_, bf16[128,768]{1,0:T(8,128)(2,1)S(1)} %collective-permute-done.6.refs_6_.refs_5_.refs_2_, ...), custom_call_target="tpu_custom_call" | custom-call | flops 1 | bytes 1 | tf_op jit(solution)/shard_map/last_grads/pallas_call | solution.py:504
  163.2 2.8 collective-permute-done.32.refs_2_
  173.2 9.0 %collective-permute-done.33.refs_2_ = bf16[1,208,1344]{2,1,0:T(8,128)(2,1)S(1)} collective-permute-done((bf16[1,208,1344]{2,1,0:T(8,128)(2,1)S(1)}, bf16[1,208,1344]{2,1,0:T(8,128)(2,1)S(1)}, u32[]{:S(2)}, u32[]{:S(2)}) %collective-permute-start.33) | collective-permute-done | bytes 559136 | tf_op jit(solution)/shard_map/ppermute | solution.py:38
  187.5 6.9 %collective-permute-done.30.refs_2_ = bf16[192,768]{1,0:T(8,128)(2,1)S(1)} collective-permute-done((bf16[192,768]{1,0:T(8,128)(2,1)S(1)}, bf16[192,768]{1,0:T(8,128)(2,1)S(1)}, u32[]{:S(2)}, u32[]{:S(2)}) %collective-permute-start.30) | collective-permute-done | bytes 294944 | tf_op jit(solution)/shard_map/ppermute | solution.py:38
  194.5 5.5 %collective-permute-start.45 = (bf16[192,768]{1,0:T(8,128)(2,1)S(1)}, bf16[192,768]{1,0:T(8,128)(2,1)S(1)}, u32[]{:S(2)}, u32[]{:S(2)}) collective-permute-start(bf16[192,768]{1,0:T(8,128)(2,1)S(1)} %feed_sums.1.refs_7_.refs_1_), channel_id=1, source_target_pairs={{0,1},{1,0},{2,3},{3,2},{4,5},{5,4},{6,7},{7,6},{8,9},{9,8},{10,11... | collective-permute-start | bytes 884744 | tf_op jit(solution)/shard_map/ppermute | solution.py:38
  202.8 3.1 %collective-permute-start.27 = (bf16[128,768]{1,0:T(8,128)(2,1)}, bf16[128,768]{1,0:T(8,128)(2,1)S(1)}, u32[]{:S(2)}, u32[]{:S(2)}) collective-permute-start(bf16[128,768]{1,0:T(8,128)(2,1)} %get-tuple-element.102), channel_id=1, source_target_pairs={{0,3},{1,2},{2,1},{3,0},{4,7},{5,6},{6,5},{7,4},{8,11},{9,10},{10,... | collective-permute-start | bytes 589832 | tf_op jit(solution)/shard_map/ppermute | solution.py:38
  205.9 4.1 %collective-permute-done.35.refs_2_ = bf16[96,192]{1,0:T(8,128)(2,1)S(1)} collective-permute-done((bf16[96,192]{1,0:T(8,128)(2,1)S(1)}, bf16[96,192]{1,0:T(8,128)(2,1)S(1)}, u32[]{:S(2)}, u32[]{:S(2)}) %collective-permute-start.35) | collective-permute-done | bytes 36896 | tf_op jit(solution)/shard_map/ppermute | solution.py:38
  211.8 26.4 %collective-permute-done.36.refs_3_ = bf16[96,192]{1,0:T(8,128)(2,1)S(1)} collective-permute-done((bf16[96,192]{1,0:T(8,128)(2,1)}, bf16[96,192]{1,0:T(8,128)(2,1)S(1)}, u32[]{:S(2)}, u32[]{:S(2)}) %collective-permute-start.36) | collective-permute-done | bytes 36896 | tf_op jit(solution)/shard_map/ppermute | solution.py:38
  239.0 3.9 %collective-permute-start.40 = (bf16[112,768]{1,0:T(8,128)(2,1)S(1)}, bf16[112,768]{1,0:T(8,128)(2,1)S(1)}, u32[]{:S(2)}, u32[]{:S(2)}) collective-permute-start(bf16[112,768]{1,0:T(8,128)(2,1)S(1)} %last_sums.1.refs_1_), channel_id=1, source_target_pairs={{0,3},{1,2},{2,1},{3,0},{4,7},{5,6},{6,5},{7,4},{8,11},{9,10},{10,... | collective-permute-start | bytes 516104 | tf_op jit(solution)/shard_map/ppermute | solution.py:38
  246.9 9.0 %collective-permute-done.46.refs_3_ = bf16[192,768]{1,0:T(8,128)(2,1)S(1)} collective-permute-done((bf16[192,768]{1,0:T(8,128)(2,1)S(1)}, bf16[192,768]{1,0:T(8,128)(2,1)S(1)}, u32[]{:S(2)}, u32[]{:S(2)}) %collective-permute-start.46) | collective-permute-done | bytes 294944 | tf_op jit(solution)/shard_map/ppermute | solution.py:38
  259.4 5.5 %collective-permute-done.39.refs_3_.refs_10_ = bf16[112,768]{1,0:T(8,128)(2,1)S(1)} collective-permute-done((bf16[112,768]{1,0:T(8,128)(2,1)S(1)}, bf16[112,768]{1,0:T(8,128)(2,1)S(1)}, u32[]{:S(2)}, u32[]{:S(2)}) %collective-permute-start.39) | collective-permute-done | bytes 172064 | tf_op jit(solution)/shard_map/ppermute | solution.py:38
  270.4 4.8 %collective-permute-done.50.refs_7_ = bf16[192,768]{1,0:T(8,128)(2,1)S(1)} collective-permute-done((bf16[192,768]{1,0:T(8,128)(2,1)S(1)}, bf16[192,768]{1,0:T(8,128)(2,1)S(1)}, u32[]{:S(2)}, u32[]{:S(2)}) %collective-permute-start.50) | collective-permute-done | bytes 294944 | tf_op jit(solution)/shard_map/ppermute | solution.py:38
  276.8 4.8 %collective-permute-done.51.refs_8_ = bf16[192,768]{1,0:T(8,128)(2,1)S(1)} collective-permute-done((bf16[192,768]{1,0:T(8,128)(2,1)S(1)}, bf16[192,768]{1,0:T(8,128)(2,1)S(1)}, u32[]{:S(2)}, u32[]{:S(2)}) %collective-permute-start.51) | collective-permute-done | bytes 294944 | tf_op jit(solution)/shard_map/ppermute | solution.py:38
  281.6 3.5 %place_feed.1 = (f32[768,768]{1,0:T(8,128)}, f32[192,3072]{1,0:T(8,128)}) custom-call(s32[3]{0:T(128)S(1)} %pad_add_fusion.refs_0_, bf16[192,768]{1,0:T(8,128)(2,1)S(1)} %feed_sums.1.refs_7_.refs_1_, bf16[192,768]{1,0:T(8,128)(2,1)S(1)} %collective-permute-done.45.refs_2_, bf16[192,768]{1,0:T(8,128)(2,1)S(1)} %collective-permute-done.46.refs_3_, ...), custom_call_target="tpu_custom_call" | custom-call | flops 1 | bytes 1 | tf_op jit(solution)/shard_map/place_feed/pallas_call | solution.py:504
  290.0 4.0 %place_last.1 = (f32[192,2304]{1,0:T(8,128)}, f32[192,768]{1,0:T(8,128)}) custom-call(s32[3]{0:T(128)S(1)} %pad_add_fusion.refs_0_, bf16[112,768]{1,0:T(8,128)(2,1)S(1)} %last_sums.1.refs_1_, bf16[112,768]{1,0:T(8,128)(2,1)S(1)} %collective-permute-done.38.refs_2_.refs_9_, bf16[112,768]{1,0:T(8,128)(2,1)S(1)} %collective-permute-done.39.refs_3_.refs_10_, ...), custom_call_target="tpu_custom_call" | custom-call | flops 1 | bytes 1 | tf_op jit(solution)/shard_map/place_last/pallas_call | solution.py:504
  (198 shorter events, 86.7 us)
Async XLA Ops:
  0.6 17.6 %collective-permute-start.1 = (bf16[192,768]{1,0:T(8,128)(2,1)}, bf16[192,768]{1,0:T(8,128)(2,1)S(1)}, u32[]{:S(2)}, u32[]{:S(2)}) collective-permute-start(bf16[192,768]{1,0:T(8,128)(2,1)} %refs_2_.3), channel_id=1, source_target_pairs={{0,16},{8,24},{16,0},{24,8},{1,17},{9,25},{17,1},{25,9},{2,18},{10... | collective-permute-start | bytes 884744 | tf_op jit(solution)/shard_map/ppermute | solution.py:38
  20.3 26.7 %collective-permute-start.14 = (bf16[768,768]{1,0:T(8,128)(2,1)S(1)}, bf16[768,768]{1,0:T(8,128)(2,1)}, u32[]{:S(2)}, u32[]{:S(2)}) collective-permute-start(bf16[768,768]{1,0:T(8,128)(2,1)S(1)} %pack.1.refs_1_), channel_id=1, source_target_pairs={{0,16},{8,24},{16,0},{24,8},{1,17},{9,25},{17,1},{25,9},{2,18},{10... | collective-permute-start | bytes 3538952 | tf_op jit(solution)/shard_map/ppermute | solution.py:38
  20.7 86.0 %collective-permute-start.13 = (bf16[768,768]{1,0:T(8,128)(2,1)S(1)}, bf16[768,768]{1,0:T(8,128)(2,1)}, u32[]{:S(2)}, u32[]{:S(2)}) collective-permute-start(bf16[768,768]{1,0:T(8,128)(2,1)S(1)} %pack.1.refs_1_), channel_id=1, source_target_pairs={{0,8},{8,0},{16,24},{24,16},{1,9},{9,1},{17,25},{25,17},{2,10},{10... | collective-permute-start | bytes 3538952 | tf_op jit(solution)/shard_map/ppermute | solution.py:38
  47.0 59.7 %collective-permute-start.15 = (bf16[768,768]{1,0:T(8,128)(2,1)}, bf16[768,768]{1,0:T(8,128)(2,1)}, u32[]{:S(2)}, u32[]{:S(2)}) collective-permute-start(bf16[768,768]{1,0:T(8,128)(2,1)} %collective-permute-done.14.refs_3_), channel_id=1, source_target_pairs={{0,8},{8,0},{16,24},{24,16},{1,9},{9,1},{17,25},{25,17},{2,10},{10... | collective-permute-start | bytes 3538952 | tf_op jit(solution)/shard_map/ppermute | solution.py:38
  47.0 19.3 %collective-permute-start.3 = (bf16[192,576]{1,0:T(8,128)(2,1)S(1)}, bf16[192,576]{1,0:T(8,128)(2,1)S(1)}, u32[]{:S(2)}, u32[]{:S(2)}) collective-permute-start(bf16[192,576]{1,0:T(8,128)(2,1)S(1)} %get-tuple-element.70.refs_1_), channel_id=1, source_target_pairs={{0,8},{8,0},{16,24},{24,16},{1,9},{9,1},{17,25},{25,17},{2,10},{10... | collective-permute-start | bytes 663560 | tf_op jit(solution)/shard_map/ppermute | solution.py:38
  73.1 17.6 %collective-permute-start = (bf16[192,768]{1,0:T(8,128)(2,1)}, bf16[192,768]{1,0:T(8,128)(2,1)S(1)}, u32[]{:S(2)}, u32[]{:S(2)}) collective-permute-start(bf16[192,768]{1,0:T(8,128)(2,1)} %refs_2_.3), channel_id=1, source_target_pairs={{0,8},{8,0},{16,24},{24,16},{1,9},{9,1},{17,25},{25,17},{2,10},{10... | collective-permute-start | bytes 884744 | tf_op jit(solution)/shard_map/ppermute | solution.py:38
  73.1 17.7 %collective-permute-start.2 = (bf16[192,768]{1,0:T(8,128)(2,1)S(1)}, bf16[192,768]{1,0:T(8,128)(2,1)S(1)}, u32[]{:S(2)}, u32[]{:S(2)}) collective-permute-start(bf16[192,768]{1,0:T(8,128)(2,1)S(1)} %collective-permute-done.1.refs_3_.refs_4_), channel_id=1, source_target_pairs={{0,8},{8,0},{16,24},{24,16},{1,9},{9,1},{17,25},{25,17},{2,10},{10... | collective-permute-start | bytes 884744 | tf_op jit(solution)/shard_map/ppermute | solution.py:38
  124.4 34.4 %collective-permute-start.28 = (bf16[1,4,192,768]{3,2,1,0:T(8,128)(2,1)S(1)}, bf16[1,4,192,768]{3,2,1,0:T(8,128)(2,1)S(1)}, u32[]{:S(2)}, u32[]{:S(2)}) collective-permute-start(bf16[1,4,192,768]{3,2,1,0:T(8,128)(2,1)S(1)} %get-tuple-element.94.refs_10_), channel_id=1, source_target_pairs={{0,16},{8,24},{16,0},{24,8},{1,17},{9,25},{17,1},{25,9},{2,18},{10... | collective-permute-start | bytes 3538952 | tf_op jit(solution)/shard_map/ppermute | solution.py:38
  166.9 15.3 %collective-permute-start.33 = (bf16[1,208,1344]{2,1,0:T(8,128)(2,1)S(1)}, bf16[1,208,1344]{2,1,0:T(8,128)(2,1)S(1)}, u32[]{:S(2)}, u32[]{:S(2)}) collective-permute-start(bf16[1,208,1344]{2,1,0:T(8,128)(2,1)S(1)} %get-tuple-element.118), channel_id=1, source_target_pairs={{0,16},{8,24},{16,0},{24,8},{1,17},{9,25},{17,1},{25,9},{2,18},{10... | collective-permute-start | bytes 1677320 | tf_op jit(solution)/shard_map/ppermute | solution.py:38
  168.5 16.5 %collective-permute-start.29 = (bf16[192,768]{1,0:T(8,128)(2,1)S(1)}, bf16[192,768]{1,0:T(8,128)(2,1)S(1)}, u32[]{:S(2)}, u32[]{:S(2)}) collective-permute-start(bf16[192,768]{1,0:T(8,128)(2,1)S(1)} %get-tuple-element.106), channel_id=1, source_target_pairs={{0,1},{1,0},{2,3},{3,2},{4,5},{5,4},{6,7},{7,6},{8,9},{9,8},{10,11... | collective-permute-start | bytes 884744 | tf_op jit(solution)/shard_map/ppermute | solution.py:38
  170.9 23.5 %collective-permute-start.30 = (bf16[192,768]{1,0:T(8,128)(2,1)S(1)}, bf16[192,768]{1,0:T(8,128)(2,1)S(1)}, u32[]{:S(2)}, u32[]{:S(2)}) collective-permute-start(bf16[192,768]{1,0:T(8,128)(2,1)S(1)} %get-tuple-element.107), channel_id=1, source_target_pairs={{0,2},{1,3},{2,0},{3,1},{4,6},{5,7},{6,4},{7,5},{8,10},{9,11},{10,... | collective-permute-start | bytes 884744 | tf_op jit(solution)/shard_map/ppermute | solution.py:38
  171.9 22.5 %collective-permute-start.31 = (bf16[192,768]{1,0:T(8,128)(2,1)S(1)}, bf16[192,768]{1,0:T(8,128)(2,1)S(1)}, u32[]{:S(2)}, u32[]{:S(2)}) collective-permute-start(bf16[192,768]{1,0:T(8,128)(2,1)S(1)} %get-tuple-element.108), channel_id=1, source_target_pairs={{0,3},{1,2},{2,1},{3,0},{4,7},{5,6},{6,5},{7,4},{8,11},{9,10},{10,... | collective-permute-start | bytes 884744 | tf_op jit(solution)/shard_map/ppermute | solution.py:38
  183.0 17.1 %collective-permute-start.34 = (bf16[112,1344]{1,0:T(8,128)(2,1)S(1)}, bf16[112,1344]{1,0:T(8,128)(2,1)S(1)}, u32[]{:S(2)}, u32[]{:S(2)}) collective-permute-start(bf16[112,1344]{1,0:T(8,128)(2,1)S(1)} %get-tuple-element.120), channel_id=1, source_target_pairs={{0,4},{4,0},{1,5},{5,1},{2,6},{6,2},{3,7},{7,3},{8,12},{12,8},{9,1... | collective-permute-start | bytes 903176 | tf_op jit(solution)/shard_map/ppermute | solution.py:38
  184.6 18.2 %collective-permute-start.18 = (bf16[128,768]{1,0:T(8,128)(2,1)S(1)}, bf16[128,768]{1,0:T(8,128)(2,1)}, u32[]{:S(2)}, u32[]{:S(2)}) collective-permute-start(bf16[128,768]{1,0:T(8,128)(2,1)S(1)} %get-tuple-element.82), channel_id=1, source_target_pairs={{0,4},{4,0},{1,5},{5,1},{2,6},{6,2},{3,7},{7,3},{8,12},{12,8},{9,1... | collective-permute-start | bytes 589832 | tf_op jit(solution)/shard_map/ppermute | solution.py:38
  185.1 20.9 %collective-permute-start.25 = (bf16[128,768]{1,0:T(8,128)(2,1)S(1)}, bf16[128,768]{1,0:T(8,128)(2,1)S(1)}, u32[]{:S(2)}, u32[]{:S(2)}) collective-permute-start(bf16[128,768]{1,0:T(8,128)(2,1)S(1)} %get-tuple-element.100), channel_id=1, source_target_pairs={{0,1},{1,0},{2,3},{3,2},{4,5},{5,4},{6,7},{7,6},{8,9},{9,8},{10,11... | collective-permute-start | bytes 589832 | tf_op jit(solution)/shard_map/ppermute | solution.py:38
  194.5 49.5 %collective-permute-start.45 = (bf16[192,768]{1,0:T(8,128)(2,1)S(1)}, bf16[192,768]{1,0:T(8,128)(2,1)S(1)}, u32[]{:S(2)}, u32[]{:S(2)}) collective-permute-start(bf16[192,768]{1,0:T(8,128)(2,1)S(1)} %feed_sums.1.refs_7_.refs_1_), channel_id=1, source_target_pairs={{0,1},{1,0},{2,3},{3,2},{4,5},{5,4},{6,7},{7,6},{8,9},{9,8},{10,11... | collective-permute-start | bytes 884744 | tf_op jit(solution)/shard_map/ppermute | solution.py:38
  201.6 37.4 %collective-permute-start.26 = (bf16[128,768]{1,0:T(8,128)(2,1)}, bf16[128,768]{1,0:T(8,128)(2,1)S(1)}, u32[]{:S(2)}, u32[]{:S(2)}) collective-permute-start(bf16[128,768]{1,0:T(8,128)(2,1)} %get-tuple-element.101), channel_id=1, source_target_pairs={{0,2},{1,3},{2,0},{3,1},{4,6},{5,7},{6,4},{7,5},{8,10},{9,11},{10,... | collective-permute-start | bytes 589832 | tf_op jit(solution)/shard_map/ppermute | solution.py:38
  202.8 40.1 %collective-permute-start.27 = (bf16[128,768]{1,0:T(8,128)(2,1)}, bf16[128,768]{1,0:T(8,128)(2,1)S(1)}, u32[]{:S(2)}, u32[]{:S(2)}) collective-permute-start(bf16[128,768]{1,0:T(8,128)(2,1)} %get-tuple-element.102), channel_id=1, source_target_pairs={{0,3},{1,2},{2,1},{3,0},{4,7},{5,6},{6,5},{7,4},{8,11},{9,10},{10,... | collective-permute-start | bytes 589832 | tf_op jit(solution)/shard_map/ppermute | solution.py:38
  205.9 32.3 %collective-permute-start.36 = (bf16[96,192]{1,0:T(8,128)(2,1)}, bf16[96,192]{1,0:T(8,128)(2,1)S(1)}, u32[]{:S(2)}, u32[]{:S(2)}) collective-permute-start(bf16[96,192]{1,0:T(8,128)(2,1)} %get-tuple-element.124), channel_id=1, source_target_pairs={{0,2},{1,3},{2,0},{3,1},{4,6},{5,7},{6,4},{7,5},{8,10},{9,11},{10,... | collective-permute-start | bytes 110600 | tf_op jit(solution)/shard_map/ppermute | solution.py:38
  210.0 28.2 %collective-permute-start.37 = (bf16[96,192]{1,0:T(8,128)(2,1)}, bf16[96,192]{1,0:T(8,128)(2,1)S(1)}, u32[]{:S(2)}, u32[]{:S(2)}) collective-permute-start(bf16[96,192]{1,0:T(8,128)(2,1)} %get-tuple-element.125), channel_id=1, source_target_pairs={{0,3},{1,2},{2,1},{3,0},{4,7},{5,6},{6,5},{7,4},{8,11},{9,10},{10,... | collective-permute-start | bytes 110600 | tf_op jit(solution)/shard_map/ppermute | solution.py:38
  238.2 17.7 %collective-permute-start.46 = (bf16[192,768]{1,0:T(8,128)(2,1)S(1)}, bf16[192,768]{1,0:T(8,128)(2,1)S(1)}, u32[]{:S(2)}, u32[]{:S(2)}) collective-permute-start(bf16[192,768]{1,0:T(8,128)(2,1)S(1)} %feed_sums.1.refs_7_.refs_1_), channel_id=1, source_target_pairs={{0,2},{1,3},{2,0},{3,1},{4,6},{5,7},{6,4},{7,5},{8,10},{9,11},{10,... | collective-permute-start | bytes 884744 | tf_op jit(solution)/shard_map/ppermute | solution.py:38
  238.2 19.2 %collective-permute-start.47 = (bf16[192,768]{1,0:T(8,128)(2,1)S(1)}, bf16[192,768]{1,0:T(8,128)(2,1)S(1)}, u32[]{:S(2)}, u32[]{:S(2)}) collective-permute-start(bf16[192,768]{1,0:T(8,128)(2,1)S(1)} %feed_sums.1.refs_7_.refs_1_), channel_id=1, source_target_pairs={{0,3},{1,2},{2,1},{3,0},{4,7},{5,6},{6,5},{7,4},{8,11},{9,10},{10,... | collective-permute-start | bytes 884744 | tf_op jit(solution)/shard_map/ppermute | solution.py:38
  239.0 18.9 %collective-permute-start.40 = (bf16[112,768]{1,0:T(8,128)(2,1)S(1)}, bf16[112,768]{1,0:T(8,128)(2,1)S(1)}, u32[]{:S(2)}, u32[]{:S(2)}) collective-permute-start(bf16[112,768]{1,0:T(8,128)(2,1)S(1)} %last_sums.1.refs_1_), channel_id=1, source_target_pairs={{0,3},{1,2},{2,1},{3,0},{4,7},{5,6},{6,5},{7,4},{8,11},{9,10},{10,... | collective-permute-start | bytes 516104 | tf_op jit(solution)/shard_map/ppermute | solution.py:38
  242.9 22.0 %collective-permute-start.39 = (bf16[112,768]{1,0:T(8,128)(2,1)S(1)}, bf16[112,768]{1,0:T(8,128)(2,1)S(1)}, u32[]{:S(2)}, u32[]{:S(2)}) collective-permute-start(bf16[112,768]{1,0:T(8,128)(2,1)S(1)} %last_sums.1.refs_1_), channel_id=1, source_target_pairs={{0,2},{1,3},{2,0},{3,1},{4,6},{5,7},{6,4},{7,5},{8,10},{9,11},{10,... | collective-permute-start | bytes 516104 | tf_op jit(solution)/shard_map/ppermute | solution.py:38
  244.0 22.3 %collective-permute-start.38 = (bf16[112,768]{1,0:T(8,128)(2,1)S(1)}, bf16[112,768]{1,0:T(8,128)(2,1)S(1)}, u32[]{:S(2)}, u32[]{:S(2)}) collective-permute-start(bf16[112,768]{1,0:T(8,128)(2,1)S(1)} %last_sums.1.refs_1_), channel_id=1, source_target_pairs={{0,1},{1,0},{2,3},{3,2},{4,5},{5,4},{6,7},{7,6},{8,9},{9,8},{10,11... | collective-permute-start | bytes 516104 | tf_op jit(solution)/shard_map/ppermute | solution.py:38
  255.9 12.2 %collective-permute-start.48 = (bf16[192,768]{1,0:T(8,128)(2,1)S(1)}, bf16[192,768]{1,0:T(8,128)(2,1)S(1)}, u32[]{:S(2)}, u32[]{:S(2)}) collective-permute-start(bf16[192,768]{1,0:T(8,128)(2,1)S(1)} %feed_sums.1.refs_7_.refs_1_), channel_id=1, source_target_pairs={{0,4},{4,0},{1,5},{5,1},{2,6},{6,2},{3,7},{7,3},{8,12},{12,8},{9,1... | collective-permute-start | bytes 884744 | tf_op jit(solution)/shard_map/ppermute | solution.py:38
  257.9 17.3 %collective-permute-start.50 = (bf16[192,768]{1,0:T(8,128)(2,1)S(1)}, bf16[192,768]{1,0:T(8,128)(2,1)S(1)}, u32[]{:S(2)}, u32[]{:S(2)}) collective-permute-start(bf16[192,768]{1,0:T(8,128)(2,1)S(1)} %collective-permute-done.46.refs_3_), channel_id=1, source_target_pairs={{0,4},{4,0},{1,5},{5,1},{2,6},{6,2},{3,7},{7,3},{8,12},{12,8},{9,1... | collective-permute-start | bytes 884744 | tf_op jit(solution)/shard_map/ppermute | solution.py:38
  264.9 16.7 %collective-permute-start.51 = (bf16[192,768]{1,0:T(8,128)(2,1)S(1)}, bf16[192,768]{1,0:T(8,128)(2,1)S(1)}, u32[]{:S(2)}, u32[]{:S(2)}) collective-permute-start(bf16[192,768]{1,0:T(8,128)(2,1)S(1)} %collective-permute-done.47.refs_4_), channel_id=1, source_target_pairs={{0,4},{4,0},{1,5},{5,1},{2,6},{6,2},{3,7},{7,3},{8,12},{12,8},{9,1... | collective-permute-start | bytes 884744 | tf_op jit(solution)/shard_map/ppermute | solution.py:38
  266.4 19.9 %collective-permute-start.41 = (bf16[112,768]{1,0:T(8,128)(2,1)S(1)}, bf16[112,768]{1,0:T(8,128)(2,1)S(1)}, u32[]{:S(2)}, u32[]{:S(2)}) collective-permute-start(bf16[112,768]{1,0:T(8,128)(2,1)S(1)} %last_sums.1.refs_1_), channel_id=1, source_target_pairs={{0,4},{4,0},{1,5},{5,1},{2,6},{6,2},{3,7},{7,3},{8,12},{12,8},{9,1... | collective-permute-start | bytes 516104 | tf_op jit(solution)/shard_map/ppermute | solution.py:38
  268.2 18.2 %collective-permute-start.42 = (bf16[112,768]{1,0:T(8,128)(2,1)S(1)}, bf16[112,768]{1,0:T(8,128)(2,1)S(1)}, u32[]{:S(2)}, u32[]{:S(2)}) collective-permute-start(bf16[112,768]{1,0:T(8,128)(2,1)S(1)} %collective-permute-done.38.refs_2_.refs_9_), channel_id=1, source_target_pairs={{0,4},{4,0},{1,5},{5,1},{2,6},{6,2},{3,7},{7,3},{8,12},{12,8},{9,1... | collective-permute-start | bytes 516104 | tf_op jit(solution)/shard_map/ppermute | solution.py:38
  269.6 18.6 %collective-permute-start.43 = (bf16[112,768]{1,0:T(8,128)(2,1)S(1)}, bf16[112,768]{1,0:T(8,128)(2,1)S(1)}, u32[]{:S(2)}, u32[]{:S(2)}) collective-permute-start(bf16[112,768]{1,0:T(8,128)(2,1)S(1)} %collective-permute-done.39.refs_3_.refs_10_), channel_id=1, source_target_pairs={{0,4},{4,0},{1,5},{5,1},{2,6},{6,2},{3,7},{7,3},{8,12},{12,8},{9,1... | collective-permute-start | bytes 516104 | tf_op jit(solution)/shard_map/ppermute | solution.py:38
  275.3 14.8 %collective-permute-start.44 = (bf16[112,768]{1,0:T(8,128)(2,1)S(1)}, bf16[112,768]{1,0:T(8,128)(2,1)S(1)}, u32[]{:S(2)}, u32[]{:S(2)}) collective-permute-start(bf16[112,768]{1,0:T(8,128)(2,1)S(1)} %collective-permute-done.40.refs_4_.refs_11_), channel_id=1, source_target_pairs={{0,4},{4,0},{1,5},{5,1},{2,6},{6,2},{3,7},{7,3},{8,12},{12,8},{9,1... | collective-permute-start | bytes 516104 | tf_op jit(solution)/shard_map/ppermute | solution.py:38
  (62 other events, 661.1 us)

commit v2 on v1

--- a/solution.py
+++ b/solution.py
@@ -42,11 +42,13 @@
     return [array] + [swap(array, axis, j) for j in range(1, lax.axis_size(axis))]
 
 
-def doubled(array, axis):
+def doubled(array, axis, waits=()):
     pieces = {0: array}
     bit = lax.axis_size(axis) // 2
     while bit:
         pieces.update({j | bit: swap(piece, axis, bit) for j, piece in list(pieces.items())})
+        if waits and bit == lax.axis_size(axis) // 2:
+            pieces[bit] = gate(pieces[bit], waits)
         bit //= 2
     return [pieces[j] for j in range(lax.axis_size(axis))]
 
@@ -100,16 +102,15 @@
     seqs,
     place_ref,
     counts_ref,
-    tokens_ref,
     grad_ref,
-    gain_ref,
-    shift_ref,
     qkv_ref,
-    normed_ref,
+    w_out_ref,
     outcome_ref,
     mine_ref,
+    out_ref,
 ):
-    width = tokens_ref.shape[1]
+    out_ref[...] = w_out_ref[...]
+    width = grad_ref.shape[1]
     size = width // seqs
     for part in range(3):
         chosen = qkv_ref[:, part * width : part * width + size]
@@ -117,10 +118,13 @@
             first = part * width + k * size
             chosen = jnp.where(place_ref[1] == k, qkv_ref[:, first : first + size], chosen)
         mine_ref[:, part * size : (part + 1) * size] = chosen
+    valid = own_rows_valid(place_ref, counts_ref, seqs, grad_ref.shape[0])
+    outcome_ref[...] = jnp.where(valid, grad_ref[...], 0.0).astype(BF)
+
+
+def first_norm_kernel(tokens_ref, gain_ref, shift_ref, normed_ref):
     unit = normalised(tokens_ref[...])[0]
     normed_ref[...] = (unit * row_of(gain_ref, 0) + row_of(shift_ref, 0)).astype(BF)
-    valid = own_rows_valid(place_ref, counts_ref, seqs, grad_ref.shape[0])
-    outcome_ref[...] = jnp.where(valid, grad_ref[...], 0.0).astype(BF)
 
 
 def pack_kernel(owners, blocks, parts, place_ref, up_ref, down_ref, out_ref, sems):
@@ -352,6 +356,28 @@
     refs[-1][...] = sum(ref[...].astype(F32) for ref in refs[:-1]).astype(BF)
 
 
+def out_chunks_kernel(blocks, seqs, place_ref, *refs):
+    total = sum(ref[...].astype(F32) for ref in refs[:blocks])
+    size = total.shape[1] // seqs
+    for j in range(seqs):
+        chosen = total[:, :size]
+        for k in range(1, seqs):
+            columns = total[:, k * size : (k + 1) * size]
+            chosen = jnp.where(place_ref[1] ^ j == k, columns, chosen)
+        refs[blocks + j][...] = chosen.astype(BF)
+
+
+def join_kernel(blocks, seqs, *refs):
+    in_refs, part_refs, out_ref = refs[:blocks], refs[blocks : blocks + seqs], refs[-1]
+    terms = [ref[...].astype(F32) for ref in in_refs]
+    while len(terms) > 1:
+        terms = [terms[i] + terms[i + 1] for i in range(0, len(terms), 2)]
+    out_ref[...] = terms[0].astype(BF)
+    total = sum(ref[...].astype(F32) for ref in part_refs)
+    size, columns = total.shape
+    out_ref[0:size, 3 * columns :] = total.astype(BF)
+
+
 def project_back_kernel(blocks, seqs, *refs):
     q_ref, kv_refs, w_ref, refs = refs[0], refs[1 : 1 + blocks], refs[1 + blocks], refs[2 + blocks :]
     normed_refs, (gain_ref, shift_ref), refs = refs[:seqs], refs[seqs : seqs + 2], refs[seqs + 2 :]
@@ -374,23 +400,46 @@
     sums_ref[1:2, :] = plain
 
 
-def last_grads_kernel(owners, seqs, blocks, place_ref, *refs):
-    normed_refs, att_refs, refs = refs[:seqs], refs[seqs : 2 * seqs], refs[2 * seqs :]
-    (projected_ref, branch_ref, columns_ref, first_ref, middle_ref, up_ref) = refs[:6]
-    sent_ref, kept_ref, att_ref = refs[6:]
-    width, size = branch_ref.shape[1], att_refs[0].shape[1]
-    own_rows, hidden_rows = width // owners, up_ref.shape[1] // owners
-    third = 3 * size
-    bit = place_ref[2] & 1
+def by_core(bit, owner, refs, store):
+    sent_ref, kept_ref = refs
+
+    @pl.when(bit == owner % 2)
+    def keep():
+        store(kept_ref)
+
+    @pl.when(bit != owner % 2)
+    def send():
+        store(sent_ref)
+
+
+def out_grads_kernel(owners, seqs, place_ref, *refs):
+    att_refs, branch_ref, (sent_ref, kept_ref, att_ref) = refs[:seqs], refs[seqs], refs[seqs + 1 :]
+    size = att_refs[0].shape[1]
+    own_rows = branch_ref.shape[1] // owners
     for k in range(seqs):
         att_ref[place_ref[1] ^ k] = att_refs[k][...]
+    for owner in range(owners):
+        group, column = divmod(owner * own_rows, size)
+        out = dot_tn(att_ref[group][:, column : column + own_rows], branch_ref[...]).astype(BF)
+
+        def store(ref, owner=owner, out=out):
+            ref[owner // 2] = out
+
+        by_core(place_ref[2] & 1, owner, (sent_ref, kept_ref), store)
+
+
+def last_grads_kernel(owners, seqs, blocks, place_ref, *refs):
+    normed_refs, refs = refs[:seqs], refs[seqs:]
+    (projected_ref, columns_ref, first_ref, middle_ref, up_ref, sent_ref, kept_ref) = refs
+    width, third = first_ref.shape[1], projected_ref.shape[1]
+    size = third // 3
+    own_rows, hidden_rows = width // owners, up_ref.shape[1] // owners
     normed = jnp.concatenate([ref[...] for ref in normed_refs])
-    projected, branch = projected_ref[...], branch_ref[...]
+    projected = projected_ref[...]
     for owner in range(owners):
         first = owner * own_rows
         group, column = divmod(first, size)
         qkv = dot_tn(normed[:, first : first + own_rows], projected).astype(BF)
-        out = dot_tn(att_ref[group][:, column : column + own_rows], branch).astype(BF)
         is_group = place_ref[1] == group
         bias = [
             jnp.where(is_group, columns_ref[:, start : start + own_rows], 0.0)
@@ -407,64 +456,32 @@
             [jnp.where(place_ref[0] == b, up_line, 0.0) for b in range(blocks)], axis=1
         ).astype(BF)
 
-        def store(ref, owner=owner, qkv=qkv, out=out, lines=lines, up_line=up_line):
+        def store(ref, owner=owner, qkv=qkv, lines=lines, up_line=up_line):
             ref[owner // 2, 0:own_rows, 0:third] = qkv
-            ref[owner // 2, 0:own_rows, third:] = out
-            ref[owner // 2, own_rows:, :] = jnp.zeros((16, third + width), BF)
+            ref[owner // 2, 0:own_rows, third:] = jnp.zeros((own_rows, width - third), BF)
+            ref[owner // 2, own_rows:, :] = jnp.zeros((16, width), BF)
             ref[owner // 2, own_rows : own_rows + 8, 0:own_rows] = lines
             ref[owner // 2, own_rows + 8 : own_rows + 9, 0 : up_line.shape[1]] = up_line
 
-        @pl.when(bit == owner % 2)
-        def keep():
-            store(kept_ref)
-
-        @pl.when(bit != owner % 2)
-        def send():
-            store(sent_ref)
-
-
-def block_kernel(blocks, place_ref, kept_ref, arrived_ref, *out_refs):
+        by_core(place_ref[2] & 1, owner, (sent_ref, kept_ref), store)
+
+
+def block_kernel(blocks, tail, place_ref, kept_ref, arrived_ref, *out_refs):
     total = kept_ref[0].astype(F32) + arrived_ref[0].astype(F32)
-    own_rows = total.shape[0] - 16
+    own_rows = total.shape[0] - tail
     size = own_rows // blocks
     for m in range(blocks):
         chosen = total[:size]
         for j in range(1, blocks):
             chosen = jnp.where(place_ref[0] ^ m == j, total[j * size : (j + 1) * size], chosen)
         out_refs[m][0:size, :] = chosen.astype(BF)
-        out_refs[m][size:, :] = total[own_rows:].astype(BF)
-
-
-def seq_kernel(blocks, seqs, place_ref, *refs):
-    in_refs, main_ref, out_refs = refs[:blocks], refs[blocks], refs[blocks + 1 :]
-    terms = [ref[...].astype(F32) for ref in in_refs]
-    while len(terms) > 1:
-        terms = [terms[i] + terms[i + 1] for i in range(0, len(terms), 2)]
-    total = terms[0]
-    size = total.shape[0] - 16
-    width = main_ref.shape[1]
-    head = width // seqs
-    third = 3 * head
-    main_ref[...] = total[:, :width].astype(BF)
-    for j in range(seqs):
-        chosen = total[:size, third : third + head]
-        for k in range(1, seqs):
-            first = third + k * head
-            chosen = jnp.where(place_ref[1] ^ j == k, total[:size, first : first + head], chosen)
-        out_refs[j][...] = chosen.astype(BF)
-
-
-def join_kernel(seqs, main_ref, *refs):
-    out_ref = refs[seqs]
-    size, head = refs[0].shape
-    out_ref[...] = main_ref[...]
-    total = sum(ref[...].astype(F32) for ref in refs[:seqs])
-    out_ref[0:size, 3 * head :] = total.astype(BF)
+        if tail:
+            out_refs[m][size:, :] = total[own_rows:].astype(BF)
 
 
 def first_back_kernel(pieces, *refs):
     part_refs, (tokens_ref, d_middle_ref, gain_ref, out_ref) = refs[:pieces], refs[pieces:]
-    upstream = sum(ref[...].astype(F32) for ref in part_refs)
+    upstream = sum(ref[:, : out_ref.shape[1]].astype(F32) for ref in part_refs)
     unit, inverse = normalised(tokens_ref[...])
     out_ref[...] = d_middle_ref[...] + norm_back(upstream, unit, inverse, row_of(gain_ref, 0))
 
@@ -495,7 +512,7 @@
                     out[row : row + rows, column : column + size] = piece.astype(F32)
 
 
-def run(kernel, label, outs, scalars, remote, arrays, scratch=(), waits=(), in_hbm=False):
+def run(kernel, label, outs, scalars, remote, arrays, scratch=(), waits=(), in_hbm=False, cost=1.0):
     inputs = len(scalars) + len(remote) + len(arrays)
 
     def without_waits(*refs):
@@ -511,7 +528,9 @@
         out_specs=(pl.BlockSpec(memory_space=pltpu.HBM if in_hbm else pltpu.VMEM),) * len(outs),
         scratch_shapes=list(scratch),
         compiler_params=pltpu.CompilerParams(vmem_limit_bytes=VMEM_LIMIT),
-        cost_estimate=pl.CostEstimate(flops=1, bytes_accessed=1, transcendentals=0),
+        cost_estimate=pl.CostEstimate(
+            flops=1, bytes_accessed=int(cost * 1.2e6), transcendentals=0
+        ),
         name=label,
     )(*scalars, *remote, *arrays, *waits)
 
@@ -520,7 +539,22 @@
     return jax.ShapeDtypeStruct(tuple(dims), kind)
 
 
-def owner_sums(kept, arrived, place, label):
+def gate(array, waits):
+    def nothing(*refs):
+        pass
+
+    return pl.pallas_call(
+        nothing,
+        out_shape=shape(array.shape, array.dtype),
+        in_specs=[pl.BlockSpec(memory_space=pltpu.HBM)] * (1 + len(waits)),
+        out_specs=pl.BlockSpec(memory_space=pltpu.HBM),
+        input_output_aliases={0: 0},
+        cost_estimate=pl.CostEstimate(flops=1, bytes_accessed=1, transcendentals=0),
+        name="gate",
+    )(array, *waits)
+
+
+def owner_sums(kept, arrived, place, label, waits=()):
     sent, bit = None, 2
     while bit < lax.axis_size("fsdp"):
         half = (kept.shape[0] // 2, *kept.shape[1:])
@@ -531,6 +565,7 @@
             [place],
             [],
             [kept, arrived],
+            waits=waits,
         )
         arrived = swap(sent, "fsdp", bit)
         bit *= 2
@@ -565,19 +600,60 @@
     inputs, grad_in = tokens[0], grad_out[0]
     vmem, dma = pltpu.VMEM, pltpu.SemaphoreType.DMA
 
-    normed1, d_outcome, qkv_mine = run(
+    (normed1,) = run(
+        first_norm_kernel,
+        "first_norm",
+        [shape((rows, width), BF)],
+        [],
+        [],
+        [inputs, norm_gain, norm_bias],
+    )
+    normed1_pieces = from_all(normed1, "seq")
+    d_outcome, qkv_mine, out_mine = run(
         functools.partial(prepare_kernel, seqs),
         "prepare",
-        [shape((rows, width), BF)] * 2 + [shape((own_rows, third), BF)],
+        [
+            shape((rows, width), BF),
+            shape((own_rows, third), BF),
+            shape((own_rows, width), BF),
+        ],
         [place, counts],
         [],
-        [inputs, grad_in, norm_gain, norm_bias, w_qkv],
-    )
-    normed1_pieces = from_all(normed1, "seq")
+        [grad_in, w_qkv, w_out],
+        waits=[normed1],
+    )
     qkv_pieces = doubled(qkv_mine, "fsdp")
-    out_pieces = doubled(w_out, "fsdp")
+    out_pieces = doubled(out_mine, "fsdp")
     outcome_pieces = from_all(d_outcome, "blk")
 
+    biases = vec_bias.astype(F32)
+    qkv_shift = jnp.concatenate(
+        [
+            lax.dynamic_slice_in_dim(biases[0], seq * head_width, head_width),
+            jnp.zeros((head_width,), F32),
+            lax.dynamic_slice_in_dim(biases[1], seq * head_width, head_width),
+        ]
+    ).reshape(1, third)
+    up_shift = (
+        lax.dynamic_index_in_dim(up_bias.reshape(owners, blocks, hidden_rows), blk, 1, False)
+        .astype(F32)
+        .reshape(1, hidden_width)
+    )
+
+    key_value, queries, qkv_full = run(
+        functools.partial(qkv_kernel, owners, seqs),
+        "project_in",
+        [
+            shape((block_rows, 2 * head_width), BF),
+            shape((block_rows, head_width), BF),
+            shape((width, third), BF),
+        ],
+        [place],
+        qkv_pieces,
+        [*normed1_pieces, qkv_shift],
+        [dma((owners,))],
+        waits=[*outcome_pieces[1:], out_pieces[owners // 2]],
+    )
     packed = shape((parts * own_rows + hidden_rows, width), BF)
     if hidden_rows % 128 == 0:
         (weights_mine,) = run(
@@ -588,7 +664,7 @@
             [w_up, w_down],
             [],
             [dma((owners + 1,))],
-            waits=[qkv_pieces[owners // 2], out_pieces[owners // 2]],
+            waits=[key_value],
             in_hbm=True,
         )
     else:
@@ -604,34 +680,7 @@
             ]
             + [lax.dynamic_slice_in_dim(w_down, blk * hidden_rows, hidden_rows, axis=0)]
         )
-    weights = doubled(weights_mine, "fsdp")
-    biases = vec_bias.astype(F32)
-    qkv_shift = jnp.concatenate(
-        [
-            lax.dynamic_slice_in_dim(biases[0], seq * head_width, head_width),
-            jnp.zeros((head_width,), F32),
-            lax.dynamic_slice_in_dim(biases[1], seq * head_width, head_width),
-        ]
-    ).reshape(1, third)
-    up_shift = (
-        lax.dynamic_index_in_dim(up_bias.reshape(owners, blocks, hidden_rows), blk, 1, False)
-        .astype(F32)
-        .reshape(1, hidden_width)
-    )
-
-    key_value, queries, qkv_full = run(
-        functools.partial(qkv_kernel, owners, seqs),
-        "project_in",
-        [
-            shape((block_rows, 2 * head_width), BF),
-            shape((block_rows, head_width), BF),
-            shape((width, third), BF),
-        ],
-        [place],
-        qkv_pieces,
-        [*normed1_pieces, qkv_shift],
-        [dma((owners,))],
-    )
+
     kv_blocks = from_all(key_value, "blk")
     *att_out, log_total = run(
         functools.partial(attend_kernel, blocks, heads, seqs, rows),
@@ -640,8 +689,11 @@
         [place, counts],
         [],
         [queries, *kv_blocks],
+        waits=out_pieces[1:],
+        cost=1.3,
     )
     att_pieces = sum_parts(att_out, "seq")
+    weights = doubled(weights_mine, "fsdp", att_pieces[1:])
     middle, normed2 = run(
         functools.partial(project_kernel, owners, seqs),
         "project_out",
@@ -668,6 +720,7 @@
             vmem((hidden_width, width), BF),
             dma((parts + 1, owners)),
         ],
+        cost=2.3,
     )
     d_normed_pieces = sum_parts(rest[:blocks], "blk")
     chunk, up_chunk = hidden_rows // seqs, own_rows // seqs
@@ -679,6 +732,7 @@
         [place],
         [],
         [*normed_pieces, *outcome_pieces, hidden, d_up],
+        cost=1.3,
     )
     d_middle, d_branch, middle_sums, *d_heads = run(
         functools.partial(middle_kernel, owners, seqs, blocks),
@@ -692,8 +746,9 @@
         waits=[sent],
     )
     d_att_pieces = sum_parts(d_heads, "seq")
-    kept, arrived, sent = owner_sums(kept, swap(sent, "fsdp", 1), place, "feed_step")
-
+    kept, arrived, feed_sent = owner_sums(
+        kept, swap(gate(sent, [d_branch]), "fsdp", 1), place, "feed_step"
+    )
     d_query, *d_kv = run(
         functools.partial(attend_back_kernel, blocks, heads, seqs, rows),
         "attend_back",
@@ -702,8 +757,23 @@
         [place, counts],
         [],
         [queries, log_total, *d_att_pieces, *kv_blocks],
-        waits=[sent],
-    )
+        waits=[feed_sent],
+        cost=1.9,
+    )
+    out_sent, out_kept = run(
+        functools.partial(out_grads_kernel, owners, seqs),
+        "out_grads",
+        [shape((owners // 2, own_rows, width), BF)] * 2,
+        [place],
+        [],
+        [*att_pieces, d_branch],
+        [vmem((seqs, rows, head_width), BF)],
+        waits=[d_query],
+    )
+    out_kept, out_arrived, out_step = owner_sums(
+        out_kept, swap(out_sent, "fsdp", 1), place, "out_step"
+    )
+    blk_rows = own_rows // blocks
     d_projected, column_sums, first_sums, *d_normed1 = run(
         functools.partial(project_back_kernel, blocks, seqs),
         "project_back",
@@ -718,6 +788,24 @@
         [d_query, *sum_parts(d_kv, "blk"), qkv_full, *normed1_pieces, norm_gain, norm_bias],
     )
     d_normed1_pieces = sum_parts(d_normed1, "seq")
+    (grad_tokens,) = run(
+        functools.partial(first_back_kernel, seqs),
+        "first_back",
+        [shape((rows, width), F32)],
+        [],
+        [],
+        [*d_normed1_pieces, inputs, d_middle, norm_gain],
+    )
+
+    out_blocks = run(
+        functools.partial(block_kernel, blocks, 0),
+        "out_blocks",
+        [shape((blk_rows, width), BF)] * blocks,
+        [place],
+        [],
+        [out_kept, out_arrived],
+        waits=[grad_tokens],
+    )
     feed_chunks = run(
         functools.partial(chunk_kernel, seqs),
         "feed_chunks",
@@ -734,63 +822,46 @@
         [],
         sum_parts(feed_chunks, "seq"),
     )
-    feed_seq = from_all(feed_sums, "seq")
-
-    sent, kept = run(
+
+    sent, last_kept = run(
         functools.partial(last_grads_kernel, owners, seqs, blocks),
         "last_grads",
-        [shape((owners // 2, own_rows + 16, third + width), BF)] * 2,
-        [place],
-        [],
-        [
-            *normed1_pieces,
-            *att_pieces,
-            d_projected,
-            d_branch,
-            column_sums,
-            first_sums,
-            middle_sums,
-            up_sums,
-        ],
-        [vmem((seqs, rows, head_width), BF)],
-        waits=[feed_chunks[0]],
-    )
-    kept, arrived, _ = owner_sums(kept, swap(sent, "fsdp", 1), place, "last_step")
-    blk_rows = own_rows // blocks
+        [shape((owners // 2, own_rows + 16, width), BF)] * 2,
+        [place],
+        [],
+        [*normed1_pieces, d_projected, column_sums, first_sums, middle_sums, up_sums],
+        waits=[out_step],
+    )
+    last_kept, last_arrived, _ = owner_sums(
+        last_kept, swap(sent, "fsdp", 1), place, "last_step", waits=feed_chunks[:1]
+    )
     last_blocks = run(
-        functools.partial(block_kernel, blocks),
+        functools.partial(block_kernel, blocks, 16),
         "last_blocks",
-        [shape((blk_rows + 16, third + width), BF)] * blocks,
-        [place],
-        [],
-        [kept, arrived],
-    )
-    last_main, *out_chunks = run(
-        functools.partial(seq_kernel, blocks, seqs),
-        "last_chunks",
-        [shape((blk_rows + 16, width), BF)] + [shape((blk_rows, head_width), BF)] * seqs,
-        [place],
-        [],
-        sum_parts(last_blocks, "blk"),
+        [shape((blk_rows + 16, width), BF)] * blocks,
+        [place],
+        [],
+        [last_kept, last_arrived],
+        waits=[feed_sums],
+    )
+    out_chunks = run(
+        functools.partial(out_chunks_kernel, blocks, seqs),
+        "out_chunks",
+        [shape((blk_rows, head_width), BF)] * seqs,
+        [place],
+        [],
+        sum_parts(out_blocks, "blk"),
     )
     (last_sums,) = run(
-        functools.partial(join_kernel, seqs),
+        functools.partial(join_kernel, blocks, seqs),
         "last_sums",
         [shape((blk_rows + 16, width), BF)],
         [],
         [],
-        [last_main, *sum_parts(out_chunks, "seq")],
-    )
-    last_seq = from_all(last_sums, "seq")
-    (grad_tokens,) = run(
-        functools.partial(first_back_kernel, seqs),
-        "first_back",
-        [shape((rows, width), F32)],
-        [],
-        [],
-        [*d_normed1_pieces, inputs, d_middle, norm_gain],
-        waits=[feed_sums],
-    )
+        [*sum_parts(last_blocks, "blk"), *sum_parts(out_chunks, "seq")],
+    )
+    feed_seq = from_all(feed_sums, "seq")
+    last_seq = from_all(gate(last_sums, [feed_seq[1]]), "seq")
     outcome = sum(one.astype(F32) for one in sum_parts(rest[blocks:], "blk"))
     valid = lax.broadcasted_iota(jnp.int32, (rows, 1), 0) < counts[0, blk * seqs + seq]
     activations = jnp.where(valid, middle + outcome + biases[3], 0.0)
@@ -851,6 +922,7 @@
         [last_all[k][m] for m in range(blocks) for k in range(seqs)],
         [],
         [vmem((blocks, seqs, blk_rows + 16, width), BF), dma((blocks * seqs,))],
+        waits=[grad_down],
     )
     small = tree_sum([one[blk_rows:] for one in last_seq])
     lines = small[:8, :own_rows]

time: 297 us -> 280 us (0.943)
  waiting for transfers between devices: 158 us -> 120 us
  local copies, waits for them, and re-layouts: 13.4 us -> 34.5 us
    ppermute x52 -> x55, waiting for transfers between devices: 158 us -> 120 us  [swap(): lax.ppermute(array, axis, [(i, i ^ bits) for i in range(lax.axis_size(axi...]
    unnamed x84 -> x160, local copies, waits for them, and re-layouts: 12.1 us -> 31.2 us
    ppermute x52 -> x55, starting transfers between devices: 67.8 us -> 70.6 us  [swap(): lax.ppermute(array, axis, [(i, i ^ bits) for i in range(lax.axis_size(axi...]
    pallas_call x21 -> x25, Pallas kernels: 49.5 us -> 49 us  [run(): pl.pallas_call(without_waits, out_shape=tuple(outs), in_specs=[pl.BlockSp...]
  transfers between devices with their start and end apart: 52 -> 55, of which waited for: 24 -> 24; matrix products, arithmetic and copies ran while one was open for 2% -> 2% of each run, Pallas kernels for 9% -> 11%
where the time goes in v2:
time: 280 us; the launch traced here: 279 us
  waiting for transfers between devices  120 us (43%)
  starting transfers between devices  70.6 us (25%)
  Pallas kernels  49 us (18%)
  local copies, waits for them, and re-layouts  34.5 us (12%)
  other arithmetic  3.45 us (1%)
    ppermute x55, waiting for transfers between devices, swap(): lax.ppermute(array, axis, [(i, i ^ bits) for i in range(lax.axis_size(axi...  120 us
    ppermute x55, starting transfers between devices, swap(): lax.ppermute(array, axis, [(i, i ^ bits) for i in range(lax.axis_size(axi...  70.6 us
    pallas_call x25, Pallas kernels, run(): pl.pallas_call(without_waits, out_shape=tuple(outs), in_specs=[pl.BlockSp...  49 us
    unnamed x160, local copies, waits for them, and re-layouts  31.2 us
  transfers between devices with their start and end apart: 55, of which 24 were waited for; matrix products, arithmetic and copies ran while one was open for 2% of the time, Pallas kernels for 11%

profile of v2, /device:TPU:0, one launch (start us, length us, event | category | flops | bytes accessed | tf_op | source)
XLA Modules:
  0.0 279.3 jit_solution(11610701007162954579)
XLA Ops:
  8.6 2.6 collective-permute-start.4
  12.8 2.6 collective-permute-start.7
  15.9 6.4 %collective-permute-done.6.refs_6_.refs_5_.refs_2_ = bf16[128,768]{1,0:T(8,128)(2,1)S(1)} collective-permute-done((bf16[128,768]{1,0:T(8,128)(2,1)S(1)}, bf16[128,768]{1,0:T(8,128)(2,1)S(1)}, u32[]{:S(2)}, u32[]{:S(2)}) %collective-permute-start.6) | collective-permute-done | bytes 196640 | tf_op jit(solution)/shard_map/ppermute | solution.py:38
  22.3 2.5 collective-permute-start.8
  26.4 3.9 %collective-permute-done.8.refs_8_.refs_7_.refs_4_ = bf16[128,768]{1,0:T(8,128)(2,1)S(1)} collective-permute-done((bf16[128,768]{1,0:T(8,128)(2,1)S(1)}, bf16[128,768]{1,0:T(8,128)(2,1)S(1)}, u32[]{:S(2)}, u32[]{:S(2)}) %collective-permute-start.8) | collective-permute-done | bytes 196640 | tf_op jit(solution)/shard_map/ppermute | solution.py:38
  30.7 2.8 project_in.1
  42.0 5.8 %collective-permute-done.10.refs_4_.refs_9_ = bf16[512,384]{1,0:T(8,128)(2,1)S(1)} collective-permute-done((bf16[512,384]{1,0:T(8,128)(2,1)S(1)}, bf16[512,384]{1,0:T(8,128)(2,1)S(1)}, u32[]{:S(2)}, u32[]{:S(2)}) %collective-permute-start.10) | collective-permute-done | bytes 393248 | tf_op jit(solution)/shard_map/ppermute | solution.py:38
  47.8 3.9 %attend.1 = (bf16[128,192]{1,0:T(8,128)(2,1)S(1)}, bf16[128,192]{1,0:T(8,128)(2,1)S(1)}, bf16[128,192]{1,0:T(8,128)(2,1)S(1)}, bf16[128,192]{1,0:T(8,128)(2,1)S(1)}, f32[3,512]{1,0:T(4,128)S(1)}) custom-call(s32[3]{0:T(128)S(1)} %pad_add_fusion.refs_0_, s32[1,8]{1,0:T(1,128)S(1)} %copy-done.74, bf16[512,192]{1,0:T(8,128)(2,1)S(1)} %get-tuple-element.78.refs_2_, ...), custom_call_target="tpu_custom_call" | custom-call | flops 1 | bytes 1560000 | tf_op jit(solution)/shard_map/attend/pallas_call | solution.py:521
  52.9 4.5 %collective-permute-start.11 = (bf16[128,192]{1,0:T(8,128)(2,1)S(1)}, bf16[128,192]{1,0:T(8,128)(2,1)S(1)}, u32[]{:S(2)}, u32[]{:S(2)}) collective-permute-start(bf16[128,192]{1,0:T(8,128)(2,1)S(1)} %get-tuple-element.81), channel_id=1, source_target_pairs={{0,1},{1,0},{2,3},{3,2},{4,5},{5,4},{6,7},{7,6},{8,9},{9,8},{10,11... | collective-permute-start | bytes 147464 | tf_op jit(solution)/shard_map/ppermute | solution.py:38
  59.9 4.3 %collective-permute-done.12.refs_7_.refs_2_.refs_3_ = bf16[128,192]{1,0:T(8,128)(2,1)S(1)} collective-permute-done((bf16[128,192]{1,0:T(8,128)(2,1)S(1)}, bf16[128,192]{1,0:T(8,128)(2,1)S(1)}, u32[]{:S(2)}, u32[]{:S(2)}) %collective-permute-start.12) | collective-permute-done | bytes 49184 | tf_op jit(solution)/shard_map/ppermute | solution.py:38
  79.6 4.3 %collective-permute-done.17.refs_6_.refs_2_ = bf16[128,768]{1,0:T(8,128)(2,1)} collective-permute-done((bf16[128,768]{1,0:T(8,128)(2,1)}, bf16[128,768]{1,0:T(8,128)(2,1)}, u32[]{:S(2)}, u32[]{:S(2)}) %collective-permute-start.17) | collective-permute-done | bytes 196640 | tf_op jit(solution)/shard_map/ppermute | solution.py:38
  85.8 6.8 %hidden.1 = (bf16[256,1536]{1,0:T(8,128)(2,1)S(1)}, bf16[256,1536]{1,0:T(8,128)(2,1)S(1)}, f32[1,1536]{1,0:T(1,128)S(1)}, f32[128,768]{1,0:T(8,128)S(1)}, bf16[1...) custom-call(s32[3]{0:T(128)S(1)} %pad_add_fusion.refs_0_, ...), custom_call_target="tpu_custom_call" | custom-call | flops 1 | bytes 2760000 | tf_op jit(solution)/shard_map/hidden/pallas_call | solution.py:521
  95.1 3.8 %feed_grads.1 = (bf16[2,4,192,768]{3,2,1,0:T(8,128)(2,1)S(1)}, bf16[2,4,192,768]{3,2,1,0:T(8,128)(2,1)S(1)}) custom-call(s32[3]{0:T(128)S(1)} %pad_add_fusion.refs_0_, bf16[128,768]{1,0:T(8,128)(2,1)} %get-tuple-element.85.refs_5_.refs_1_, bf16[128,768]{1,0:T(8,128)(2,1)} %collective-permute-done.17.refs_6_.refs_2_, bf16[128,768]{1,0:T(8,128)(2,1)S(1)} %copy-done.45, ...), custom_call_target="tpu_custom_call" | custom-call | flops 1 | bytes 1560000 | tf_op jit(solution)/shard_map/feed_grads/pallas_call | solution.py:521
  103.7 4.7 %collective-permute-done.23.refs_2_ = bf16[2,4,192,768]{3,2,1,0:T(8,128)(2,1)S(1)} collective-permute-done((bf16[2,4,192,768]{3,2,1,0:T(8,128)(2,1)}, bf16[2,4,192,768]{3,2,1,0:T(8,128)(2,1)S(1)}, u32[]{:S(2)}, u32[]{:S(2)}) %collective-permute-start.23) | collective-permute-done | bytes 2359328 | tf_op jit(solution)/shard_map/ppermute | solution.py:38
  111.2 2.7 collective-permute-start.20
  116.2 5.3 %collective-permute-done.21.refs_6_ = bf16[128,192]{1,0:T(8,128)(2,1)S(1)} collective-permute-done((bf16[128,192]{1,0:T(8,128)(2,1)S(1)}, bf16[128,192]{1,0:T(8,128)(2,1)S(1)}, u32[]{:S(2)}, u32[]{:S(2)}) %collective-permute-start.21) | collective-permute-done | bytes 49184 | tf_op jit(solution)/shard_map/ppermute | solution.py:38
  121.7 5.6 %attend_back.1 = (bf16[512,192]{1,0:T(8,128)(2,1)S(1)}, f32[512,384]{1,0:T(8,128)S(1)}, bf16[512,384]{1,0:T(8,128)(2,1)S(1)}) custom-call(s32[3]{0:T(128)S(1)} %pad_add_fusion.refs_0_, s32[1,8]{1,0:T(1,128)S(1)} %copy-done.75, bf16[512,192]{1,0:T(8,128)(2,1)S(1)} %copy-done.39, f32[3,512]{1,0:T(4,128)S(1)} %copy-done.72, ...), custom_call_target="tpu_custom_call" | custom-call | flops 1 | bytes 2280000 | tf_op jit(solution)/shard_map/attend_back/pallas_call | solution.py:521
  130.4 10.3 %collective-permute-done.24.refs_2_ = bf16[512,384]{1,0:T(8,128)(2,1)S(1)} collective-permute-done((bf16[512,384]{1,0:T(8,128)(2,1)S(1)}, bf16[512,384]{1,0:T(8,128)(2,1)S(1)}, u32[]{:S(2)}, u32[]{:S(2)}) %collective-permute-start.24) | collective-permute-done | bytes 393248 | tf_op jit(solution)/shard_map/ppermute | solution.py:38
  143.0 2.6 last_grads.1
  152.5 4.0 %collective-permute-done.25.refs_1_ = bf16[128,768]{1,0:T(8,128)(2,1)S(1)} collective-permute-done((bf16[128,768]{1,0:T(8,128)(2,1)S(1)}, bf16[128,768]{1,0:T(8,128)(2,1)S(1)}, u32[]{:S(2)}, u32[]{:S(2)}) %collective-permute-start.25) | collective-permute-done | bytes 196640 | tf_op jit(solution)/shard_map/ppermute | solution.py:38
  156.5 7.7 %collective-permute-done.26.refs_2_ = bf16[128,768]{1,0:T(8,128)(2,1)S(1)} collective-permute-done((bf16[128,768]{1,0:T(8,128)(2,1)S(1)}, bf16[128,768]{1,0:T(8,128)(2,1)S(1)}, u32[]{:S(2)}, u32[]{:S(2)}) %collective-permute-start.26) | collective-permute-done | bytes 196640 | tf_op jit(solution)/shard_map/ppermute | solution.py:38
  172.4 15.2 %collective-permute-done.33.refs_2_ = bf16[192,768]{1,0:T(8,128)(2,1)S(1)} collective-permute-done((bf16[192,768]{1,0:T(8,128)(2,1)S(1)}, bf16[192,768]{1,0:T(8,128)(2,1)S(1)}, u32[]{:S(2)}, u32[]{:S(2)}) %collective-permute-start.33) | collective-permute-done | bytes 294944 | tf_op jit(solution)/shard_map/ppermute | solution.py:38
  187.8 5.9 %collective-permute-start.41 = (bf16[192,768]{1,0:T(8,128)(2,1)S(1)}, bf16[192,768]{1,0:T(8,128)(2,1)S(1)}, u32[]{:S(2)}, u32[]{:S(2)}) collective-permute-start(bf16[192,768]{1,0:T(8,128)(2,1)S(1)} %feed_sums.1.refs_3_.refs_1_), channel_id=1, source_target_pairs={{0,1},{1,0},{2,3},{3,2},{4,5},{5,4},{6,7},{7,6},{8,9},{9,8},{10,11... | collective-permute-start | bytes 884744 | tf_op jit(solution)/shard_map/ppermute | solution.py:38
  195.9 2.4 collective-permute-start.39
  215.3 16.5 %collective-permute-done.49.refs_3_ = bf16[192,768]{1,0:T(8,128)(2,1)S(1)} collective-permute-done((bf16[192,768]{1,0:T(8,128)(2,1)S(1)}, bf16[192,768]{1,0:T(8,128)(2,1)S(1)}, u32[]{:S(2)}, u32[]{:S(2)}) %collective-permute-start.49) | collective-permute-done | bytes 294944 | tf_op jit(solution)/shard_map/ppermute | solution.py:38
  234.7 10.2 %collective-permute-done.43.refs_10_.refs_3_ = bf16[112,768]{1,0:T(8,128)(2,1)S(1)} collective-permute-done((bf16[112,768]{1,0:T(8,128)(2,1)}, bf16[112,768]{1,0:T(8,128)(2,1)S(1)}, u32[]{:S(2)}, u32[]{:S(2)}) %collective-permute-start.43) | collective-permute-done | bytes 172064 | tf_op jit(solution)/shard_map/ppermute | solution.py:38
  249.1 2.6 collective-permute-done.52.refs_6_
  252.7 5.4 %collective-permute-done.53.refs_7_ = bf16[192,768]{1,0:T(8,128)(2,1)S(1)} collective-permute-done((bf16[192,768]{1,0:T(8,128)(2,1)S(1)}, bf16[192,768]{1,0:T(8,128)(2,1)S(1)}, u32[]{:S(2)}, u32[]{:S(2)}) %collective-permute-start.53) | collective-permute-done | bytes 294944 | tf_op jit(solution)/shard_map/ppermute | solution.py:38
  260.2 4.2 %collective-permute-done.54.refs_8_ = bf16[192,768]{1,0:T(8,128)(2,1)S(1)} collective-permute-done((bf16[192,768]{1,0:T(8,128)(2,1)S(1)}, bf16[192,768]{1,0:T(8,128)(2,1)S(1)}, u32[]{:S(2)}, u32[]{:S(2)}) %collective-permute-start.54) | collective-permute-done | bytes 294944 | tf_op jit(solution)/shard_map/ppermute | solution.py:38
  264.4 3.5 %place_feed.1 = (f32[768,768]{1,0:T(8,128)}, f32[192,3072]{1,0:T(8,128)}) custom-call(s32[3]{0:T(128)S(1)} %pad_add_fusion.refs_0_, bf16[192,768]{1,0:T(8,128)(2,1)S(1)} %feed_sums.1.refs_3_.refs_1_, bf16[192,768]{1,0:T(8,128)(2,1)S(1)} %copy-done.31, bf16[192,768]{1,0:T(8,128)(2,1)S(1)} %collective-permute-done.49.refs_3_, ...), custom_call_target="tpu_custom_call" | custom-call | flops 1 | bytes 1200000 | tf_op jit(solution)/shard_map/place_feed/pallas_call | solution.py:521
  268.1 3.5 %collective-permute-done.47.refs_7_ = bf16[112,768]{1,0:T(8,128)(2,1)S(1)} collective-permute-done((bf16[112,768]{1,0:T(8,128)(2,1)S(1)}, bf16[112,768]{1,0:T(8,128)(2,1)S(1)}, u32[]{:S(2)}, u32[]{:S(2)}) %collective-permute-start.47) | collective-permute-done | bytes 172064 | tf_op jit(solution)/shard_map/ppermute | solution.py:38
  275.1 4.0 %place_last.1 = (f32[192,2304]{1,0:T(8,128)}, f32[192,768]{1,0:T(8,128)}) custom-call(s32[3]{0:T(128)S(1)} %pad_add_fusion.refs_0_, bf16[112,768]{1,0:T(8,128)(2,1)S(1)} %copy-done.21, bf16[112,768]{1,0:T(8,128)(2,1)S(1)} %collective-permute-done.42.refs_9_.refs_2_, bf16[112,768]{1,0:T(8,128)(2,1)S(1)} %collective-permute-done.43.refs_10_.refs_3_, ...), custom_call_target="tpu_custom_call" | custom-call | flops 1 | bytes 1200000 | tf_op jit(solution)/shard_map/place_last/pallas_call | solution.py:521
  (287 shorter events, 107.1 us)
Async XLA Ops:
  8.1 22.5 %collective-permute-start.3 = (bf16[192,576]{1,0:T(8,128)(2,1)S(1)}, bf16[192,576]{1,0:T(8,128)(2,1)S(1)}, u32[]{:S(2)}, u32[]{:S(2)}) collective-permute-start(bf16[192,576]{1,0:T(8,128)(2,1)S(1)} %get-tuple-element.76.refs_1_), channel_id=1, source_target_pairs={{0,8},{8,0},{16,24},{24,16},{1,9},{9,1},{17,25},{25,17},{2,10},{10... | collective-permute-start | bytes 663560 | tf_op jit(solution)/shard_map/ppermute | solution.py:38
  8.6 17.6 %collective-permute-start.4 = (bf16[192,576]{1,0:T(8,128)(2,1)S(1)}, bf16[192,576]{1,0:T(8,128)(2,1)S(1)}, u32[]{:S(2)}, u32[]{:S(2)}) collective-permute-start(bf16[192,576]{1,0:T(8,128)(2,1)S(1)} %get-tuple-element.76.refs_1_), channel_id=1, source_target_pairs={{0,16},{8,24},{16,0},{24,8},{1,17},{9,25},{17,1},{25,9},{2,18},{10... | collective-permute-start | bytes 663560 | tf_op jit(solution)/shard_map/ppermute | solution.py:38
  15.4 15.3 %collective-permute-start.1 = (bf16[192,768]{1,0:T(8,128)(2,1)S(1)}, bf16[192,768]{1,0:T(8,128)(2,1)S(1)}, u32[]{:S(2)}, u32[]{:S(2)}) collective-permute-start(bf16[192,768]{1,0:T(8,128)(2,1)S(1)} %get-tuple-element.75.refs_1_.refs_2_), channel_id=1, source_target_pairs={{0,16},{8,24},{16,0},{24,8},{1,17},{9,25},{17,1},{25,9},{2,18},{10... | collective-permute-start | bytes 884744 | tf_op jit(solution)/shard_map/ppermute | solution.py:38
  37.9 27.5 %collective-permute-start.15 = (bf16[768,768]{1,0:T(8,128)(2,1)S(1)}, bf16[768,768]{1,0:T(8,128)(2,1)S(1)}, u32[]{:S(2)}, u32[]{:S(2)}) collective-permute-start(bf16[768,768]{1,0:T(8,128)(2,1)S(1)} %pack.1.refs_1_), channel_id=1, source_target_pairs={{0,16},{8,24},{16,0},{24,8},{1,17},{9,25},{17,1},{25,9},{2,18},{10... | collective-permute-start | bytes 3538952 | tf_op jit(solution)/shard_map/ppermute | solution.py:38
  59.8 24.1 %collective-permute-start.14 = (bf16[768,768]{1,0:T(8,128)(2,1)S(1)}, bf16[768,768]{1,0:T(8,128)(2,1)}, u32[]{:S(2)}, u32[]{:S(2)}) collective-permute-start(bf16[768,768]{1,0:T(8,128)(2,1)S(1)} %pack.1.refs_1_), channel_id=1, source_target_pairs={{0,8},{8,0},{16,24},{24,16},{1,9},{9,1},{17,25},{25,17},{2,10},{10... | collective-permute-start | bytes 3538952 | tf_op jit(solution)/shard_map/ppermute | solution.py:38
  66.4 17.5 %collective-permute-start.16 = (bf16[768,768]{1,0:T(8,128)(2,1)}, bf16[768,768]{1,0:T(8,128)(2,1)}, u32[]{:S(2)}, u32[]{:S(2)}) collective-permute-start(bf16[768,768]{1,0:T(8,128)(2,1)} %gate.3.refs_3_), channel_id=1, source_target_pairs={{0,8},{8,0},{16,24},{24,16},{1,9},{9,1},{17,25},{25,17},{2,10},{10... | collective-permute-start | bytes 3538952 | tf_op jit(solution)/shard_map/ppermute | solution.py:38
  109.6 40.6 %collective-permute-start.30 = (bf16[1,4,192,768]{3,2,1,0:T(8,128)(2,1)S(1)}, bf16[1,4,192,768]{3,2,1,0:T(8,128)(2,1)S(1)}, u32[]{:S(2)}, u32[]{:S(2)}) collective-permute-start(bf16[1,4,192,768]{3,2,1,0:T(8,128)(2,1)S(1)} %get-tuple-element.100.refs_10_), channel_id=1, source_target_pairs={{0,16},{8,24},{16,0},{24,8},{1,17},{9,25},{17,1},{25,9},{2,18},{10... | collective-permute-start | bytes 3538952 | tf_op jit(solution)/shard_map/ppermute | solution.py:38
  129.1 13.2 %collective-permute-start.28 = (bf16[2,192,768]{2,1,0:T(8,128)(2,1)S(1)}, bf16[2,192,768]{2,1,0:T(8,128)(2,1)S(1)}, u32[]{:S(2)}, u32[]{:S(2)}) collective-permute-start(bf16[2,192,768]{2,1,0:T(8,128)(2,1)S(1)} %get-tuple-element.116), channel_id=1, source_target_pairs={{0,8},{8,0},{16,24},{24,16},{1,9},{9,1},{17,25},{25,17},{2,10},{10... | collective-permute-start | bytes 1769480 | tf_op jit(solution)/shard_map/ppermute | solution.py:38
  145.6 18.6 %collective-permute-start.29 = (bf16[2,208,768]{2,1,0:T(8,128)(2,1)S(1)}, bf16[2,208,768]{2,1,0:T(8,128)(2,1)S(1)}, u32[]{:S(2)}, u32[]{:S(2)}) collective-permute-start(bf16[2,208,768]{2,1,0:T(8,128)(2,1)S(1)} %get-tuple-element.119), channel_id=1, source_target_pairs={{0,8},{8,0},{16,24},{24,16},{1,9},{9,1},{17,25},{25,17},{2,10},{10... | collective-permute-start | bytes 1916936 | tf_op jit(solution)/shard_map/ppermute | solution.py:38
  147.0 17.2 %collective-permute-start.26 = (bf16[128,768]{1,0:T(8,128)(2,1)S(1)}, bf16[128,768]{1,0:T(8,128)(2,1)S(1)}, u32[]{:S(2)}, u32[]{:S(2)}) collective-permute-start(bf16[128,768]{1,0:T(8,128)(2,1)S(1)} %get-tuple-element.107), channel_id=1, source_target_pairs={{0,2},{1,3},{2,0},{3,1},{4,6},{5,7},{6,4},{7,5},{8,10},{9,11},{10,... | collective-permute-start | bytes 589832 | tf_op jit(solution)/shard_map/ppermute | solution.py:38
  148.2 18.6 %collective-permute-start.27 = (bf16[128,768]{1,0:T(8,128)(2,1)S(1)}, bf16[128,768]{1,0:T(8,128)(2,1)S(1)}, u32[]{:S(2)}, u32[]{:S(2)}) collective-permute-start(bf16[128,768]{1,0:T(8,128)(2,1)S(1)} %get-tuple-element.108), channel_id=1, source_target_pairs={{0,3},{1,2},{2,1},{3,0},{4,7},{5,6},{6,5},{7,4},{8,11},{9,10},{10,... | collective-permute-start | bytes 589832 | tf_op jit(solution)/shard_map/ppermute | solution.py:38
  150.2 19.4 %collective-permute-start.36 = (bf16[1,192,768]{2,1,0:T(8,128)(2,1)S(1)}, bf16[1,192,768]{2,1,0:T(8,128)(2,1)S(1)}, u32[]{:S(2)}, u32[]{:S(2)}) collective-permute-start(bf16[1,192,768]{2,1,0:T(8,128)(2,1)S(1)} %get-tuple-element.117.refs_10_), channel_id=1, source_target_pairs={{0,16},{8,24},{16,0},{24,8},{1,17},{9,25},{17,1},{25,9},{2,18},{10... | collective-permute-start | bytes 884744 | tf_op jit(solution)/shard_map/ppermute | solution.py:38
  156.5 15.9 %collective-permute-start.32 = (bf16[192,768]{1,0:T(8,128)(2,1)S(1)}, bf16[192,768]{1,0:T(8,128)(2,1)S(1)}, u32[]{:S(2)}, u32[]{:S(2)}) collective-permute-start(bf16[192,768]{1,0:T(8,128)(2,1)S(1)} %get-tuple-element.124), channel_id=1, source_target_pairs={{0,1},{1,0},{2,3},{3,2},{4,5},{5,4},{6,7},{7,6},{8,9},{9,8},{10,11... | collective-permute-start | bytes 884744 | tf_op jit(solution)/shard_map/ppermute | solution.py:38
  164.2 23.4 %collective-permute-start.33 = (bf16[192,768]{1,0:T(8,128)(2,1)S(1)}, bf16[192,768]{1,0:T(8,128)(2,1)S(1)}, u32[]{:S(2)}, u32[]{:S(2)}) collective-permute-start(bf16[192,768]{1,0:T(8,128)(2,1)S(1)} %get-tuple-element.125), channel_id=1, source_target_pairs={{0,2},{1,3},{2,0},{3,1},{4,6},{5,7},{6,4},{7,5},{8,10},{9,11},{10,... | collective-permute-start | bytes 884744 | tf_op jit(solution)/shard_map/ppermute | solution.py:38
  164.2 23.4 %collective-permute-start.34 = (bf16[192,768]{1,0:T(8,128)(2,1)S(1)}, bf16[192,768]{1,0:T(8,128)(2,1)S(1)}, u32[]{:S(2)}, u32[]{:S(2)}) collective-permute-start(bf16[192,768]{1,0:T(8,128)(2,1)S(1)} %get-tuple-element.126), channel_id=1, source_target_pairs={{0,3},{1,2},{2,1},{3,0},{4,7},{5,6},{6,5},{7,4},{8,11},{9,10},{10,... | collective-permute-start | bytes 884744 | tf_op jit(solution)/shard_map/ppermute | solution.py:38
  166.8 31.4 %collective-permute-start.31 = (bf16[1,208,768]{2,1,0:T(8,128)(2,1)S(1)}, bf16[1,208,768]{2,1,0:T(8,128)(2,1)S(1)}, u32[]{:S(2)}, u32[]{:S(2)}) collective-permute-start(bf16[1,208,768]{2,1,0:T(8,128)(2,1)S(1)} %get-tuple-element.123), channel_id=1, source_target_pairs={{0,16},{8,24},{16,0},{24,8},{1,17},{9,25},{17,1},{25,9},{2,18},{10... | collective-permute-start | bytes 958472 | tf_op jit(solution)/shard_map/ppermute | solution.py:38
  171.2 22.5 %collective-permute-start.37 = (bf16[96,768]{1,0:T(8,128)(2,1)S(1)}, bf16[96,768]{1,0:T(8,128)(2,1)S(1)}, u32[]{:S(2)}, u32[]{:S(2)}) collective-permute-start(bf16[96,768]{1,0:T(8,128)(2,1)S(1)} %get-tuple-element.131), channel_id=1, source_target_pairs={{0,4},{4,0},{1,5},{5,1},{2,6},{6,2},{3,7},{7,3},{8,12},{12,8},{9,1... | collective-permute-start | bytes 442376 | tf_op jit(solution)/shard_map/ppermute | solution.py:38
  187.8 21.6 %collective-permute-start.41 = (bf16[192,768]{1,0:T(8,128)(2,1)S(1)}, bf16[192,768]{1,0:T(8,128)(2,1)S(1)}, u32[]{:S(2)}, u32[]{:S(2)}) collective-permute-start(bf16[192,768]{1,0:T(8,128)(2,1)S(1)} %feed_sums.1.refs_3_.refs_1_), channel_id=1, source_target_pairs={{0,1},{1,0},{2,3},{3,2},{4,5},{5,4},{6,7},{7,6},{8,9},{9,8},{10,11... | collective-permute-start | bytes 884744 | tf_op jit(solution)/shard_map/ppermute | solution.py:38
  194.7 17.5 %collective-permute-start.18 = (bf16[128,768]{1,0:T(8,128)(2,1)S(1)}, bf16[128,768]{1,0:T(8,128)(2,1)S(1)}, u32[]{:S(2)}, u32[]{:S(2)}) collective-permute-start(bf16[128,768]{1,0:T(8,128)(2,1)S(1)} %copy-done.79), channel_id=1, source_target_pairs={{0,4},{4,0},{1,5},{5,1},{2,6},{6,2},{3,7},{7,3},{8,12},{12,8},{9,1... | collective-permute-start | bytes 589832 | tf_op jit(solution)/shard_map/ppermute | solution.py:38
  204.2 27.6 %collective-permute-start.49 = (bf16[192,768]{1,0:T(8,128)(2,1)S(1)}, bf16[192,768]{1,0:T(8,128)(2,1)S(1)}, u32[]{:S(2)}, u32[]{:S(2)}) collective-permute-start(bf16[192,768]{1,0:T(8,128)(2,1)S(1)} %feed_sums.1.refs_3_.refs_1_), channel_id=1, source_target_pairs={{0,2},{1,3},{2,0},{3,1},{4,6},{5,7},{6,4},{7,5},{8,10},{9,11},{10,... | collective-permute-start | bytes 884744 | tf_op jit(solution)/shard_map/ppermute | solution.py:38
  206.0 26.7 %collective-permute-start.50 = (bf16[192,768]{1,0:T(8,128)(2,1)S(1)}, bf16[192,768]{1,0:T(8,128)(2,1)S(1)}, u32[]{:S(2)}, u32[]{:S(2)}) collective-permute-start(bf16[192,768]{1,0:T(8,128)(2,1)S(1)} %feed_sums.1.refs_3_.refs_1_), channel_id=1, source_target_pairs={{0,3},{1,2},{2,1},{3,0},{4,7},{5,6},{6,5},{7,4},{8,11},{9,10},{10,... | collective-permute-start | bytes 884744 | tf_op jit(solution)/shard_map/ppermute | solution.py:38
  210.1 23.7 %collective-permute-start.44 = (bf16[112,768]{1,0:T(8,128)(2,1)}, bf16[112,768]{1,0:T(8,128)(2,1)S(1)}, u32[]{:S(2)}, u32[]{:S(2)}) collective-permute-start(bf16[112,768]{1,0:T(8,128)(2,1)} %gate.5.refs_1_), channel_id=1, source_target_pairs={{0,3},{1,2},{2,1},{3,0},{4,7},{5,6},{6,5},{7,4},{8,11},{9,10},{10,... | collective-permute-start | bytes 516104 | tf_op jit(solution)/shard_map/ppermute | solution.py:38
  212.0 33.0 %collective-permute-start.43 = (bf16[112,768]{1,0:T(8,128)(2,1)}, bf16[112,768]{1,0:T(8,128)(2,1)S(1)}, u32[]{:S(2)}, u32[]{:S(2)}) collective-permute-start(bf16[112,768]{1,0:T(8,128)(2,1)} %gate.5.refs_1_), channel_id=1, source_target_pairs={{0,2},{1,3},{2,0},{3,1},{4,6},{5,7},{6,4},{7,5},{8,10},{9,11},{10,... | collective-permute-start | bytes 516104 | tf_op jit(solution)/shard_map/ppermute | solution.py:38
  212.2 33.7 %collective-permute-start.42 = (bf16[112,768]{1,0:T(8,128)(2,1)}, bf16[112,768]{1,0:T(8,128)(2,1)S(1)}, u32[]{:S(2)}, u32[]{:S(2)}) collective-permute-start(bf16[112,768]{1,0:T(8,128)(2,1)} %gate.5.refs_1_), channel_id=1, source_target_pairs={{0,1},{1,0},{2,3},{3,2},{4,5},{5,4},{6,7},{7,6},{8,9},{9,8},{10,11... | collective-permute-start | bytes 516104 | tf_op jit(solution)/shard_map/ppermute | solution.py:38
  231.8 16.4 %collective-permute-start.51 = (bf16[192,768]{1,0:T(8,128)(2,1)S(1)}, bf16[192,768]{1,0:T(8,128)(2,1)S(1)}, u32[]{:S(2)}, u32[]{:S(2)}) collective-permute-start(bf16[192,768]{1,0:T(8,128)(2,1)S(1)} %feed_sums.1.refs_3_.refs_1_), channel_id=1, source_target_pairs={{0,4},{4,0},{1,5},{5,1},{2,6},{6,2},{3,7},{7,3},{8,12},{12,8},{9,1... | collective-permute-start | bytes 884744 | tf_op jit(solution)/shard_map/ppermute | solution.py:38
  232.7 35.2 %collective-permute-start.45 = (bf16[112,768]{1,0:T(8,128)(2,1)S(1)}, bf16[112,768]{1,0:T(8,128)(2,1)S(1)}, u32[]{:S(2)}, u32[]{:S(2)}) collective-permute-start(bf16[112,768]{1,0:T(8,128)(2,1)S(1)} %copy-done.21), channel_id=1, source_target_pairs={{0,4},{4,0},{1,5},{5,1},{2,6},{6,2},{3,7},{7,3},{8,12},{12,8},{9,1... | collective-permute-start | bytes 516104 | tf_op jit(solution)/shard_map/ppermute | solution.py:38
  233.8 17.9 %collective-permute-start.52 = (bf16[192,768]{1,0:T(8,128)(2,1)S(1)}, bf16[192,768]{1,0:T(8,128)(2,1)S(1)}, u32[]{:S(2)}, u32[]{:S(2)}) collective-permute-start(bf16[192,768]{1,0:T(8,128)(2,1)S(1)} %copy-done.31), channel_id=1, source_target_pairs={{0,4},{4,0},{1,5},{5,1},{2,6},{6,2},{3,7},{7,3},{8,12},{12,8},{9,1... | collective-permute-start | bytes 884744 | tf_op jit(solution)/shard_map/ppermute | solution.py:38
  245.0 13.1 %collective-permute-start.53 = (bf16[192,768]{1,0:T(8,128)(2,1)S(1)}, bf16[192,768]{1,0:T(8,128)(2,1)S(1)}, u32[]{:S(2)}, u32[]{:S(2)}) collective-permute-start(bf16[192,768]{1,0:T(8,128)(2,1)S(1)} %collective-permute-done.49.refs_3_), channel_id=1, source_target_pairs={{0,4},{4,0},{1,5},{5,1},{2,6},{6,2},{3,7},{7,3},{8,12},{12,8},{9,1... | collective-permute-start | bytes 884744 | tf_op jit(solution)/shard_map/ppermute | solution.py:38
  245.9 18.5 %collective-permute-start.54 = (bf16[192,768]{1,0:T(8,128)(2,1)S(1)}, bf16[192,768]{1,0:T(8,128)(2,1)S(1)}, u32[]{:S(2)}, u32[]{:S(2)}) collective-permute-start(bf16[192,768]{1,0:T(8,128)(2,1)S(1)} %collective-permute-done.50.refs_4_), channel_id=1, source_target_pairs={{0,4},{4,0},{1,5},{5,1},{2,6},{6,2},{3,7},{7,3},{8,12},{12,8},{9,1... | collective-permute-start | bytes 884744 | tf_op jit(solution)/shard_map/ppermute | solution.py:38
  248.2 19.9 %collective-permute-start.46 = (bf16[112,768]{1,0:T(8,128)(2,1)S(1)}, bf16[112,768]{1,0:T(8,128)(2,1)S(1)}, u32[]{:S(2)}, u32[]{:S(2)}) collective-permute-start(bf16[112,768]{1,0:T(8,128)(2,1)S(1)} %collective-permute-done.42.refs_9_.refs_2_), channel_id=1, source_target_pairs={{0,4},{4,0},{1,5},{5,1},{2,6},{6,2},{3,7},{7,3},{8,12},{12,8},{9,1... | collective-permute-start | bytes 516104 | tf_op jit(solution)/shard_map/ppermute | solution.py:38
  251.8 19.9 %collective-permute-start.47 = (bf16[112,768]{1,0:T(8,128)(2,1)S(1)}, bf16[112,768]{1,0:T(8,128)(2,1)S(1)}, u32[]{:S(2)}, u32[]{:S(2)}) collective-permute-start(bf16[112,768]{1,0:T(8,128)(2,1)S(1)} %collective-permute-done.43.refs_10_.refs_3_), channel_id=1, source_target_pairs={{0,4},{4,0},{1,5},{5,1},{2,6},{6,2},{3,7},{7,3},{8,12},{12,8},{9,1... | collective-permute-start | bytes 516104 | tf_op jit(solution)/shard_map/ppermute | solution.py:38
  258.1 15.4 %collective-permute-start.48 = (bf16[112,768]{1,0:T(8,128)(2,1)S(1)}, bf16[112,768]{1,0:T(8,128)(2,1)S(1)}, u32[]{:S(2)}, u32[]{:S(2)}) collective-permute-start(bf16[112,768]{1,0:T(8,128)(2,1)S(1)} %collective-permute-done.44.refs_11_.refs_4_), channel_id=1, source_target_pairs={{0,4},{4,0},{1,5},{5,1},{2,6},{6,2},{3,7},{7,3},{8,12},{12,8},{9,1... | collective-permute-start | bytes 516104 | tf_op jit(solution)/shard_map/ppermute | solution.py:38
  (103 other events, 735.9 us)

commit v3 on v2

--- a/solution.py
+++ b/solution.py
@@ -13,7 +13,6 @@
 SCALE = HD ** (-0.5)
 BF = jnp.bfloat16
 F32 = jnp.float32
-VMEM_LIMIT = 44 * 1024 * 1024
 
 
 def dot_nn(left_side, right_side):
@@ -103,14 +102,17 @@
     place_ref,
     counts_ref,
     grad_ref,
-    qkv_ref,
     w_out_ref,
     outcome_ref,
-    mine_ref,
     out_ref,
 ):
     out_ref[...] = w_out_ref[...]
-    width = grad_ref.shape[1]
+    valid = own_rows_valid(place_ref, counts_ref, seqs, grad_ref.shape[0])
+    outcome_ref[...] = jnp.where(valid, grad_ref[...], 0.0).astype(BF)
+
+
+def columns_kernel(seqs, place_ref, qkv_ref, mine_ref):
+    width = qkv_ref.shape[1] // 3
     size = width // seqs
     for part in range(3):
         chosen = qkv_ref[:, part * width : part * width + size]
@@ -118,8 +120,6 @@
             first = part * width + k * size
             chosen = jnp.where(place_ref[1] == k, qkv_ref[:, first : first + size], chosen)
         mine_ref[:, part * size : (part + 1) * size] = chosen
-    valid = own_rows_valid(place_ref, counts_ref, seqs, grad_ref.shape[0])
-    outcome_ref[...] = jnp.where(valid, grad_ref[...], 0.0).astype(BF)
 
 
 def first_norm_kernel(tokens_ref, gain_ref, shift_ref, normed_ref):
@@ -512,7 +512,7 @@
                     out[row : row + rows, column : column + size] = piece.astype(F32)
 
 
-def run(kernel, label, outs, scalars, remote, arrays, scratch=(), waits=(), in_hbm=False, cost=1.0):
+def run(kernel, label, outs, scalars, remote, arrays, scratch=(), waits=(), in_hbm=False, cost=1.0, mib=10):
     inputs = len(scalars) + len(remote) + len(arrays)
 
     def without_waits(*refs):
@@ -522,12 +522,12 @@
         without_waits,
         out_shape=tuple(outs),
         in_specs=[pl.BlockSpec(memory_space=pltpu.SMEM)] * len(scalars)
-        + [pl.BlockSpec(memory_space=pltpu.HBM)] * len(remote)
+        + [pl.BlockSpec(memory_space=pl.ANY)] * len(remote)
         + [pl.BlockSpec(memory_space=pltpu.VMEM)] * len(arrays)
-        + [pl.BlockSpec(memory_space=pltpu.HBM)] * len(waits),
-        out_specs=(pl.BlockSpec(memory_space=pltpu.HBM if in_hbm else pltpu.VMEM),) * len(outs),
+        + [pl.BlockSpec(memory_space=pl.ANY)] * len(waits),
+        out_specs=(pl.BlockSpec(memory_space=pl.ANY if in_hbm else pltpu.VMEM),) * len(outs),
         scratch_shapes=list(scratch),
-        compiler_params=pltpu.CompilerParams(vmem_limit_bytes=VMEM_LIMIT),
+        compiler_params=pltpu.CompilerParams(vmem_limit_bytes=mib * 1024 * 1024),
         cost_estimate=pl.CostEstimate(
             flops=1, bytes_accessed=int(cost * 1.2e6), transcendentals=0
         ),
@@ -546,8 +546,8 @@
     return pl.pallas_call(
         nothing,
         out_shape=shape(array.shape, array.dtype),
-        in_specs=[pl.BlockSpec(memory_space=pltpu.HBM)] * (1 + len(waits)),
-        out_specs=pl.BlockSpec(memory_space=pltpu.HBM),
+        in_specs=[pl.BlockSpec(memory_space=pl.ANY)] * (1 + len(waits)),
+        out_specs=pl.BlockSpec(memory_space=pl.ANY),
         input_output_aliases={0: 0},
         cost_estimate=pl.CostEstimate(flops=1, bytes_accessed=1, transcendentals=0),
         name="gate",
@@ -566,6 +566,7 @@
             [],
             [kept, arrived],
             waits=waits,
+            mib=14,
         )
         arrived = swap(sent, "fsdp", bit)
         bit *= 2
@@ -609,20 +610,25 @@
         [inputs, norm_gain, norm_bias],
     )
     normed1_pieces = from_all(normed1, "seq")
-    d_outcome, qkv_mine, out_mine = run(
+    (qkv_mine,) = run(
+        functools.partial(columns_kernel, seqs),
+        "columns",
+        [shape((own_rows, third), BF)],
+        [place],
+        [],
+        [w_qkv],
+        waits=[normed1],
+    )
+    qkv_pieces = doubled(qkv_mine, "fsdp")
+    d_outcome, out_mine = run(
         functools.partial(prepare_kernel, seqs),
         "prepare",
-        [
-            shape((rows, width), BF),
-            shape((own_rows, third), BF),
-            shape((own_rows, width), BF),
-        ],
+        [shape((rows, width), BF), shape((own_rows, width), BF)],
         [place, counts],
         [],
-        [grad_in, w_qkv, w_out],
-        waits=[normed1],
-    )
-    qkv_pieces = doubled(qkv_mine, "fsdp")
+        [grad_in, w_out],
+        waits=[qkv_pieces[owners // 2]],
+    )
     out_pieces = doubled(out_mine, "fsdp")
     outcome_pieces = from_all(d_outcome, "blk")
 
@@ -652,7 +658,8 @@
         qkv_pieces,
         [*normed1_pieces, qkv_shift],
         [dma((owners,))],
-        waits=[*outcome_pieces[1:], out_pieces[owners // 2]],
+        waits=outcome_pieces[1:],
+        mib=16,
     )
     packed = shape((parts * own_rows + hidden_rows, width), BF)
     if hidden_rows % 128 == 0:
@@ -664,7 +671,7 @@
             [w_up, w_down],
             [],
             [dma((owners + 1,))],
-            waits=[key_value],
+            waits=[key_value, out_pieces[owners // 2]],
             in_hbm=True,
         )
     else:
@@ -691,6 +698,7 @@
         [queries, *kv_blocks],
         waits=out_pieces[1:],
         cost=1.3,
+        mib=20,
     )
     att_pieces = sum_parts(att_out, "seq")
     weights = doubled(weights_mine, "fsdp", att_pieces[1:])
@@ -702,6 +710,7 @@
         out_pieces,
         [*att_pieces, inputs, vec_bias, norm_gain, norm_bias],
         [vmem((width, width), BF), dma((owners,))],
+        mib=12,
     )
 
     normed_pieces = from_all(normed2, "blk")
@@ -721,6 +730,7 @@
             dma((parts + 1, owners)),
         ],
         cost=2.3,
+        mib=24,
     )
     d_normed_pieces = sum_parts(rest[:blocks], "blk")
     chunk, up_chunk = hidden_rows // seqs, own_rows // seqs
@@ -733,6 +743,7 @@
         [],
         [*normed_pieces, *outcome_pieces, hidden, d_up],
         cost=1.3,
+        mib=24,
     )
     d_middle, d_branch, middle_sums, *d_heads = run(
         functools.partial(middle_kernel, owners, seqs, blocks),
@@ -744,11 +755,10 @@
         [*d_normed_pieces, middle, grad_in, norm_gain],
         [vmem((width, width), BF), dma((owners,))],
         waits=[sent],
+        mib=12,
     )
     d_att_pieces = sum_parts(d_heads, "seq")
-    kept, arrived, feed_sent = owner_sums(
-        kept, swap(gate(sent, [d_branch]), "fsdp", 1), place, "feed_step"
-    )
+    result_pieces = sum_parts(rest[blocks:], "blk")
     d_query, *d_kv = run(
         functools.partial(attend_back_kernel, blocks, heads, seqs, rows),
         "attend_back",
@@ -757,8 +767,11 @@
         [place, counts],
         [],
         [queries, log_total, *d_att_pieces, *kv_blocks],
-        waits=[feed_sent],
         cost=1.9,
+        mib=28,
+    )
+    kept, arrived, feed_sent = owner_sums(
+        kept, swap(gate(sent, d_att_pieces[1:]), "fsdp", 1), place, "feed_step", waits=[d_query]
     )
     out_sent, out_kept = run(
         functools.partial(out_grads_kernel, owners, seqs),
@@ -768,10 +781,8 @@
         [],
         [*att_pieces, d_branch],
         [vmem((seqs, rows, head_width), BF)],
-        waits=[d_query],
-    )
-    out_kept, out_arrived, out_step = owner_sums(
-        out_kept, swap(out_sent, "fsdp", 1), place, "out_step"
+        waits=[feed_sent],
+        mib=12,
     )
     blk_rows = own_rows // blocks
     d_projected, column_sums, first_sums, *d_normed1 = run(
@@ -786,6 +797,11 @@
         [],
         [],
         [d_query, *sum_parts(d_kv, "blk"), qkv_full, *normed1_pieces, norm_gain, norm_bias],
+        waits=[feed_sent, out_sent],
+        mib=16,
+    )
+    out_kept, out_arrived, out_step = owner_sums(
+        out_kept, swap(gate(out_sent, [column_sums]), "fsdp", 1), place, "out_step"
     )
     d_normed1_pieces = sum_parts(d_normed1, "seq")
     (grad_tokens,) = run(
@@ -813,6 +829,46 @@
         [place],
         [],
         [kept, arrived],
+        waits=[grad_tokens],
+        mib=12,
+    )
+
+    sent, last_kept = run(
+        functools.partial(last_grads_kernel, owners, seqs, blocks),
+        "last_grads",
+        [shape((owners // 2, own_rows + 16, width), BF)] * 2,
+        [place],
+        [],
+        [*normed1_pieces, d_projected, column_sums, first_sums, middle_sums, up_sums],
+        waits=[out_step],
+        mib=16,
+    )
+    last_kept, last_arrived, _ = owner_sums(
+        last_kept, swap(sent, "fsdp", 1), place, "last_step"
+    )
+    last_blocks = run(
+        functools.partial(block_kernel, blocks, 16),
+        "last_blocks",
+        [shape((blk_rows + 16, width), BF)] * blocks,
+        [place],
+        [],
+        [last_kept, last_arrived],
+    )
+    out_chunks = run(
+        functools.partial(out_chunks_kernel, blocks, seqs),
+        "out_chunks",
+        [shape((blk_rows, head_width), BF)] * seqs,
+        [place],
+        [],
+        sum_parts(out_blocks, "blk"),
+    )
+    (last_sums,) = run(
+        functools.partial(join_kernel, blocks, seqs),
+        "last_sums",
+        [shape((blk_rows + 16, width), BF)],
+        [],
+        [],
+        [*sum_parts(last_blocks, "blk"), *sum_parts(out_chunks, "seq")],
     )
     (feed_sums,) = run(
         add_kernel,
@@ -821,48 +877,11 @@
         [],
         [],
         sum_parts(feed_chunks, "seq"),
-    )
-
-    sent, last_kept = run(
-        functools.partial(last_grads_kernel, owners, seqs, blocks),
-        "last_grads",
-        [shape((owners // 2, own_rows + 16, width), BF)] * 2,
-        [place],
-        [],
-        [*normed1_pieces, d_projected, column_sums, first_sums, middle_sums, up_sums],
-        waits=[out_step],
-    )
-    last_kept, last_arrived, _ = owner_sums(
-        last_kept, swap(sent, "fsdp", 1), place, "last_step", waits=feed_chunks[:1]
-    )
-    last_blocks = run(
-        functools.partial(block_kernel, blocks, 16),
-        "last_blocks",
-        [shape((blk_rows + 16, width), BF)] * blocks,
-        [place],
-        [],
-        [last_kept, last_arrived],
-        waits=[feed_sums],
-    )
-    out_chunks = run(
-        functools.partial(out_chunks_kernel, blocks, seqs),
-        "out_chunks",
-        [shape((blk_rows, head_width), BF)] * seqs,
-        [place],
-        [],
-        sum_parts(out_blocks, "blk"),
-    )
-    (last_sums,) = run(
-        functools.partial(join_kernel, blocks, seqs),
-        "last_sums",
-        [shape((blk_rows + 16, width), BF)],
-        [],
-        [],
-        [*sum_parts(last_blocks, "blk"), *sum_parts(out_chunks, "seq")],
+        waits=[last_sums, *result_pieces[1:]],
     )
     feed_seq = from_all(feed_sums, "seq")
     last_seq = from_all(gate(last_sums, [feed_seq[1]]), "seq")
-    outcome = sum(one.astype(F32) for one in sum_parts(rest[blocks:], "blk"))
+    outcome = sum(one.astype(F32) for one in result_pieces)
     valid = lax.broadcasted_iota(jnp.int32, (rows, 1), 0) < counts[0, blk * seqs + seq]
     activations = jnp.where(valid, middle + outcome + biases[3], 0.0)
 
@@ -895,6 +914,7 @@
         [],
         [vmem((blocks, seqs, chunk_rows, width), BF), dma((blocks * seqs,))],
         waits=last_seq[1:],
+        mib=24,
     )
     grad_qkv, grad_w_out = run(
         functools.partial(
@@ -923,6 +943,7 @@
         [],
         [vmem((blocks, seqs, blk_rows + 16, width), BF), dma((blocks * seqs,))],
         waits=[grad_down],
+        mib=20,
     )
     small = tree_sum([one[blk_rows:] for one in last_seq])
     lines = small[:8, :own_rows]

time: 280 us -> 291 us (1.039)
  waiting for transfers between devices: 120 us -> 129 us
  starting transfers between devices: 70.6 us -> 65.7 us
  local copies, waits for them, and re-layouts: 34.5 us -> 38.8 us
    ppermute x55, waiting for transfers between devices: 120 us -> 129 us  [swap(): lax.ppermute(array, axis, [(i, i ^ bits) for i in range(lax.axis_size(axi...]
    ppermute x55, starting transfers between devices: 70.6 us -> 65.7 us  [swap(): lax.ppermute(array, axis, [(i, i ^ bits) for i in range(lax.axis_size(axi...]
    unnamed x160 -> x214, local copies, waits for them, and re-layouts: 31.2 us -> 35.5 us
    pallas_call x25 -> x26, Pallas kernels: 49 us -> 49.5 us  [run(): pl.pallas_call(without_waits, out_shape=tuple(outs), in_specs=[pl.BlockSp...]
  transfers between devices with their start and end apart: 55 -> 55, of which waited for: 24 -> 33; matrix products, arithmetic and copies ran while one was open for 2% -> 2% of each run, Pallas kernels for 11% -> 12%
where the time goes in v3:
time: 291 us; the launch traced here: 289 us
  waiting for transfers between devices  129 us (44%)
  starting transfers between devices  65.7 us (23%)
  Pallas kernels  49.6 us (17%)
  local copies, waits for them, and re-layouts  38.8 us (13%)
  other arithmetic  3.45 us (1%)
    ppermute x55, waiting for transfers between devices, swap(): lax.ppermute(array, axis, [(i, i ^ bits) for i in range(lax.axis_size(axi...  129 us
    ppermute x55, starting transfers between devices, swap(): lax.ppermute(array, axis, [(i, i ^ bits) for i in range(lax.axis_size(axi...  65.7 us
    pallas_call x26, Pallas kernels, run(): pl.pallas_call(without_waits, out_shape=tuple(outs), in_specs=[pl.BlockSp...  49.5 us
    unnamed x214, local copies, waits for them, and re-layouts  35.5 us
  transfers between devices with their start and end apart: 55, of which 33 were waited for; matrix products, arithmetic and copies ran while one was open for 2% of the time, Pallas kernels for 12%

profile of v3, /device:TPU:0, one launch (start us, length us, event | category | flops | bytes accessed | tf_op | source)
XLA Modules:
  0.0 288.8 jit_solution(6158790724436941141)
XLA Ops:
  5.5 3.0 %collective-permute-start = (bf16[192,576]{1,0:T(8,128)(2,1)S(1)}, bf16[192,576]{1,0:T(8,128)(2,1)S(1)}, u32[]{:S(2)}, u32[]{:S(2)}) collective-permute-start(bf16[192,576]{1,0:T(8,128)(2,1)S(1)} %columns.1.refs_1_), channel_id=1, source_target_pairs={{0,16},{8,24},{16,0},{24,8},{1,17},{9,25},{17,1},{25,9},{2,18},{10... | collective-permute-start | bytes 663560 | tf_op jit(solution)/shard_map/ppermute | solution.py:37
  10.1 2.6 collective-permute-start.7
  16.9 2.7 collective-permute-done.6.refs_6_.refs_5_.refs_2_
  21.8 5.4 %collective-permute-done.7.refs_7_.refs_6_.refs_3_ = bf16[128,768]{1,0:T(8,128)(2,1)S(1)} collective-permute-done((bf16[128,768]{1,0:T(8,128)(2,1)S(1)}, bf16[128,768]{1,0:T(8,128)(2,1)S(1)}, u32[]{:S(2)}, u32[]{:S(2)}) %collective-permute-start.7) | collective-permute-done | bytes 196640 | tf_op jit(solution)/shard_map/ppermute | solution.py:37
  28.7 2.7 project_in.1
  38.1 7.4 %collective-permute-done.10.refs_4_.refs_9_ = bf16[512,384]{1,0:T(8,128)(2,1)S(1)} collective-permute-done((bf16[512,384]{1,0:T(8,128)(2,1)S(1)}, bf16[512,384]{1,0:T(8,128)(2,1)S(1)}, u32[]{:S(2)}, u32[]{:S(2)}) %collective-permute-start.10) | collective-permute-done | bytes 393248 | tf_op jit(solution)/shard_map/ppermute | solution.py:37
  45.5 3.9 %attend.1 = (bf16[128,192]{1,0:T(8,128)(2,1)S(1)}, bf16[128,192]{1,0:T(8,128)(2,1)S(1)}, bf16[128,192]{1,0:T(8,128)(2,1)S(1)}, bf16[128,192]{1,0:T(8,128)(2,1)S(1)}, f32[3,512]{1,0:T(4,128)S(1)}) custom-call(s32[3]{0:T(128)S(1)} %pad_add_fusion.refs_0_, s32[1,8]{1,0:T(1,128)S(1)} %copy-done.92, bf16[512,192]{1,0:T(8,128)(2,1)S(1)} %get-tuple-element.76.refs_2_, ...), custom_call_target="tpu_custom_call" | custom-call | flops 1 | bytes 1560000 | tf_op jit(solution)/shard_map/attend/pallas_call | solution.py:521
  55.2 3.6 %collective-permute-done.12.refs_7_.refs_2_.refs_3_ = bf16[128,192]{1,0:T(8,128)(2,1)S(1)} collective-permute-done((bf16[128,192]{1,0:T(8,128)(2,1)S(1)}, bf16[128,192]{1,0:T(8,128)(2,1)S(1)}, u32[]{:S(2)}, u32[]{:S(2)}) %collective-permute-start.12) | collective-permute-done | bytes 49184 | tf_op jit(solution)/shard_map/ppermute | solution.py:37
  76.5 4.0 %collective-permute-done.17.refs_6_.refs_2_ = bf16[128,768]{1,0:T(8,128)(2,1)} collective-permute-done((bf16[128,768]{1,0:T(8,128)(2,1)}, bf16[128,768]{1,0:T(8,128)(2,1)}, u32[]{:S(2)}, u32[]{:S(2)}) %collective-permute-start.17) | collective-permute-done | bytes 196640 | tf_op jit(solution)/shard_map/ppermute | solution.py:37
  82.5 6.8 %hidden.1 = (bf16[256,1536]{1,0:T(8,128)(2,1)S(1)}, bf16[256,1536]{1,0:T(8,128)(2,1)S(1)}, f32[1,1536]{1,0:T(1,128)S(1)}, f32[128,768]{1,0:T(8,128)S(1)}, bf16[1...) custom-call(s32[3]{0:T(128)S(1)} %pad_add_fusion.refs_0_, ...), custom_call_target="tpu_custom_call" | custom-call | flops 1 | bytes 2760000 | tf_op jit(solution)/shard_map/hidden/pallas_call | solution.py:521
  91.5 3.8 %feed_grads.1 = (bf16[2,4,192,768]{3,2,1,0:T(8,128)(2,1)S(1)}, bf16[2,4,192,768]{3,2,1,0:T(8,128)(2,1)S(1)}) custom-call(s32[3]{0:T(128)S(1)} %pad_add_fusion.refs_0_, bf16[128,768]{1,0:T(8,128)(2,1)} %get-tuple-element.83.refs_5_.refs_1_, bf16[128,768]{1,0:T(8,128)(2,1)} %collective-permute-done.17.refs_6_.refs_2_, bf16[128,768]{1,0:T(8,128)(2,1)S(1)} %copy-done.49, ...), custom_call_target="tpu_custom_call" | custom-call | flops 1 | bytes 1560000 | tf_op jit(solution)/shard_map/feed_grads/pallas_call | solution.py:521
  105.2 3.2 %collective-permute-done.21.refs_6_.refs_2_ = bf16[128,192]{1,0:T(8,128)(2,1)S(1)} collective-permute-done((bf16[128,192]{1,0:T(8,128)(2,1)S(1)}, bf16[128,192]{1,0:T(8,128)(2,1)S(1)}, u32[]{:S(2)}, u32[]{:S(2)}) %collective-permute-start.21) | collective-permute-done | bytes 49184 | tf_op jit(solution)/shard_map/ppermute | solution.py:37
  112.7 5.6 %attend_back.1 = (bf16[512,192]{1,0:T(8,128)(2,1)S(1)}, f32[512,384]{1,0:T(8,128)S(1)}, bf16[512,384]{1,0:T(8,128)(2,1)S(1)}) custom-call(s32[3]{0:T(128)S(1)} %pad_add_fusion.refs_0_, s32[1,8]{1,0:T(1,128)S(1)} %copy-done.93, bf16[512,192]{1,0:T(8,128)(2,1)S(1)} %copy-done.43, f32[3,512]{1,0:T(4,128)S(1)} %copy-done.90, ...), custom_call_target="tpu_custom_call" | custom-call | flops 1 | bytes 2280000 | tf_op jit(solution)/shard_map/attend_back/pallas_call | solution.py:521
  125.5 4.4 %collective-permute-done.23.refs_2_ = bf16[512,384]{1,0:T(8,128)(2,1)S(1)} collective-permute-done((bf16[512,384]{1,0:T(8,128)(2,1)S(1)}, bf16[512,384]{1,0:T(8,128)(2,1)S(1)}, u32[]{:S(2)}, u32[]{:S(2)}) %collective-permute-start.23) | collective-permute-done | bytes 393248 | tf_op jit(solution)/shard_map/ppermute | solution.py:37
  139.3 2.6 last_grads.1
  147.8 5.2 %collective-permute-done.25.refs_1_ = bf16[128,768]{1,0:T(8,128)(2,1)S(1)} collective-permute-done((bf16[128,768]{1,0:T(8,128)(2,1)S(1)}, bf16[128,768]{1,0:T(8,128)(2,1)S(1)}, u32[]{:S(2)}, u32[]{:S(2)}) %collective-permute-start.25) | collective-permute-done | bytes 196640 | tf_op jit(solution)/shard_map/ppermute | solution.py:37
  154.5 6.1 %collective-permute-done.26.refs_2_ = bf16[128,768]{1,0:T(8,128)(2,1)S(1)} collective-permute-done((bf16[128,768]{1,0:T(8,128)(2,1)S(1)}, bf16[128,768]{1,0:T(8,128)(2,1)S(1)}, u32[]{:S(2)}, u32[]{:S(2)}) %collective-permute-start.26) | collective-permute-done | bytes 196640 | tf_op jit(solution)/shard_map/ppermute | solution.py:37
  161.8 9.7 %collective-permute-done.32.refs_2_ = bf16[1,192,768]{2,1,0:T(8,128)(2,1)S(1)} collective-permute-done((bf16[1,192,768]{2,1,0:T(8,128)(2,1)S(1)}, bf16[1,192,768]{2,1,0:T(8,128)(2,1)S(1)}, u32[]{:S(2)}, u32[]{:S(2)}) %collective-permute-start.32) | collective-permute-done | bytes 294944 | tf_op jit(solution)/shard_map/ppermute | solution.py:37
  180.9 14.6 %collective-permute-done.34.refs_3_ = bf16[96,192]{1,0:T(8,128)(2,1)S(1)} collective-permute-done((bf16[96,192]{1,0:T(8,128)(2,1)S(1)}, bf16[96,192]{1,0:T(8,128)(2,1)S(1)}, u32[]{:S(2)}, u32[]{:S(2)}) %collective-permute-start.34) | collective-permute-done | bytes 36896 | tf_op jit(solution)/shard_map/ppermute | solution.py:37
  195.5 3.2 %collective-permute-start.35 = (bf16[96,192]{1,0:T(8,128)(2,1)S(1)}, bf16[96,192]{1,0:T(8,128)(2,1)S(1)}, u32[]{:S(2)}, u32[]{:S(2)}) collective-permute-start(bf16[96,192]{1,0:T(8,128)(2,1)S(1)} %get-tuple-element.127), channel_id=1, source_target_pairs={{0,2},{1,3},{2,0},{3,1},{4,6},{5,7},{6,4},{7,5},{8,10},{9,11},{10,... | collective-permute-start | bytes 110600 | tf_op jit(solution)/shard_map/ppermute | solution.py:37
  198.7 7.8 %collective-permute-done.35.refs_4_ = bf16[96,192]{1,0:T(8,128)(2,1)S(1)} collective-permute-done((bf16[96,192]{1,0:T(8,128)(2,1)S(1)}, bf16[96,192]{1,0:T(8,128)(2,1)S(1)}, u32[]{:S(2)}, u32[]{:S(2)}) %collective-permute-start.35) | collective-permute-done | bytes 36896 | tf_op jit(solution)/shard_map/ppermute | solution.py:37
  209.9 2.5 collective-permute-done.36.refs_5_
  213.0 4.9 %collective-permute-done.31.refs_1_ = bf16[112,768]{1,0:T(8,128)(2,1)S(1)} collective-permute-done((bf16[112,768]{1,0:T(8,128)(2,1)S(1)}, bf16[112,768]{1,0:T(8,128)(2,1)S(1)}, u32[]{:S(2)}, u32[]{:S(2)}) %collective-permute-start.31) | collective-permute-done | bytes 172064 | tf_op jit(solution)/shard_map/ppermute | solution.py:37
  223.9 6.4 %collective-permute-done.41.refs_1_.refs_2_ = bf16[192,768]{1,0:T(8,128)(2,1)S(1)} collective-permute-done((bf16[192,768]{1,0:T(8,128)(2,1)S(1)}, bf16[192,768]{1,0:T(8,128)(2,1)S(1)}, u32[]{:S(2)}, u32[]{:S(2)}) %collective-permute-start.41) | collective-permute-done | bytes 294944 | tf_op jit(solution)/shard_map/ppermute | solution.py:37
  231.1 7.2 %collective-permute-start.44 = (bf16[112,768]{1,0:T(8,128)(2,1)}, bf16[112,768]{1,0:T(8,128)(2,1)S(1)}, u32[]{:S(2)}, u32[]{:S(2)}) collective-permute-start(bf16[112,768]{1,0:T(8,128)(2,1)} %gate.7.refs_1_), channel_id=1, source_target_pairs={{0,3},{1,2},{2,1},{3,0},{4,7},{5,6},{6,5},{7,4},{8,11},{9,10},{10,... | collective-permute-start | bytes 516104 | tf_op jit(solution)/shard_map/ppermute | solution.py:37
  239.7 7.7 %collective-permute-done.49.refs_3_ = bf16[192,768]{1,0:T(8,128)(2,1)S(1)} collective-permute-done((bf16[192,768]{1,0:T(8,128)(2,1)S(1)}, bf16[192,768]{1,0:T(8,128)(2,1)S(1)}, u32[]{:S(2)}, u32[]{:S(2)}) %collective-permute-start.49) | collective-permute-done | bytes 294944 | tf_op jit(solution)/shard_map/ppermute | solution.py:37
  250.1 8.0 %collective-permute-done.43.refs_10_.refs_3_ = bf16[112,768]{1,0:T(8,128)(2,1)S(1)} collective-permute-done((bf16[112,768]{1,0:T(8,128)(2,1)}, bf16[112,768]{1,0:T(8,128)(2,1)S(1)}, u32[]{:S(2)}, u32[]{:S(2)}) %collective-permute-start.43) | collective-permute-done | bytes 172064 | tf_op jit(solution)/shard_map/ppermute | solution.py:37
  263.4 4.7 %collective-permute-done.53.refs_7_ = bf16[192,768]{1,0:T(8,128)(2,1)S(1)} collective-permute-done((bf16[192,768]{1,0:T(8,128)(2,1)S(1)}, bf16[192,768]{1,0:T(8,128)(2,1)S(1)}, u32[]{:S(2)}, u32[]{:S(2)}) %collective-permute-start.53) | collective-permute-done | bytes 294944 | tf_op jit(solution)/shard_map/ppermute | solution.py:37
  269.8 4.5 %collective-permute-done.54.refs_8_ = bf16[192,768]{1,0:T(8,128)(2,1)S(1)} collective-permute-done((bf16[192,768]{1,0:T(8,128)(2,1)S(1)}, bf16[192,768]{1,0:T(8,128)(2,1)S(1)}, u32[]{:S(2)}, u32[]{:S(2)}) %collective-permute-start.54) | collective-permute-done | bytes 294944 | tf_op jit(solution)/shard_map/ppermute | solution.py:37
  274.3 3.5 %place_feed.1 = (f32[768,768]{1,0:T(8,128)}, f32[192,3072]{1,0:T(8,128)}) custom-call(s32[3]{0:T(128)S(1)} %pad_add_fusion.refs_0_, bf16[192,768]{1,0:T(8,128)(2,1)S(1)} %feed_sums.1.refs_1_, bf16[192,768]{1,0:T(8,128)(2,1)S(1)} %copy-done.33, bf16[192,768]{1,0:T(8,128)(2,1)S(1)} %collective-permute-done.49.refs_3_, ...), custom_call_target="tpu_custom_call" | custom-call | flops 1 | bytes 1200000 | tf_op jit(solution)/shard_map/place_feed/pallas_call | solution.py:521
  278.0 3.0 %collective-permute-done.47.refs_7_ = bf16[112,768]{1,0:T(8,128)(2,1)S(1)} collective-permute-done((bf16[112,768]{1,0:T(8,128)(2,1)S(1)}, bf16[112,768]{1,0:T(8,128)(2,1)S(1)}, u32[]{:S(2)}, u32[]{:S(2)}) %collective-permute-start.47) | collective-permute-done | bytes 172064 | tf_op jit(solution)/shard_map/ppermute | solution.py:37
  284.6 4.0 %place_last.1 = (f32[192,2304]{1,0:T(8,128)}, f32[192,768]{1,0:T(8,128)}) custom-call(s32[3]{0:T(128)S(1)} %pad_add_fusion.refs_0_, bf16[112,768]{1,0:T(8,128)(2,1)S(1)} %copy-done.9, bf16[112,768]{1,0:T(8,128)(2,1)S(1)} %collective-permute-done.42.refs_9_.refs_2_, bf16[112,768]{1,0:T(8,128)(2,1)S(1)} %collective-permute-done.43.refs_10_.refs_3_, ...), custom_call_target="tpu_custom_call" | custom-call | flops 1 | bytes 1200000 | tf_op jit(solution)/shard_map/place_last/pallas_call | solution.py:521
  (343 shorter events, 122.3 us)
Async XLA Ops:
  8.5 18.9 %collective-permute-start.4 = (bf16[192,576]{1,0:T(8,128)(2,1)S(1)}, bf16[192,576]{1,0:T(8,128)(2,1)}, u32[]{:S(2)}, u32[]{:S(2)}) collective-permute-start(bf16[192,576]{1,0:T(8,128)(2,1)S(1)} %columns.1.refs_1_), channel_id=1, source_target_pairs={{0,8},{8,0},{16,24},{24,16},{1,9},{9,1},{17,25},{25,17},{2,10},{10... | collective-permute-start | bytes 663560 | tf_op jit(solution)/shard_map/ppermute | solution.py:37
  8.5 11.1 %collective-permute-start.6 = (bf16[128,768]{1,0:T(8,128)(2,1)S(1)}, bf16[128,768]{1,0:T(8,128)(2,1)S(1)}, u32[]{:S(2)}, u32[]{:S(2)}) collective-permute-start(bf16[128,768]{1,0:T(8,128)(2,1)S(1)} %first_norm.1.refs_2_.refs_5_.refs_4_.refs_1_), channel_id=1, source_target_pairs={{0,1},{1,0},{2,3},{3,2},{4,5},{5,4},{6,7},{7,6},{8,9},{9,8},{10,11... | collective-permute-start | bytes 589832 | tf_op jit(solution)/shard_map/ppermute | solution.py:37
  10.1 17.1 %collective-permute-start.7 = (bf16[128,768]{1,0:T(8,128)(2,1)S(1)}, bf16[128,768]{1,0:T(8,128)(2,1)S(1)}, u32[]{:S(2)}, u32[]{:S(2)}) collective-permute-start(bf16[128,768]{1,0:T(8,128)(2,1)S(1)} %first_norm.1.refs_2_.refs_5_.refs_4_.refs_1_), channel_id=1, source_target_pairs={{0,2},{1,3},{2,0},{3,1},{4,6},{5,7},{6,4},{7,5},{8,10},{9,11},{10,... | collective-permute-start | bytes 589832 | tf_op jit(solution)/shard_map/ppermute | solution.py:37
  12.7 14.7 %collective-permute-start.8 = (bf16[128,768]{1,0:T(8,128)(2,1)S(1)}, bf16[128,768]{1,0:T(8,128)(2,1)S(1)}, u32[]{:S(2)}, u32[]{:S(2)}) collective-permute-start(bf16[128,768]{1,0:T(8,128)(2,1)S(1)} %first_norm.1.refs_2_.refs_5_.refs_4_.refs_1_), channel_id=1, source_target_pairs={{0,3},{1,2},{2,1},{3,0},{4,7},{5,6},{6,5},{7,4},{8,11},{9,10},{10,... | collective-permute-start | bytes 589832 | tf_op jit(solution)/shard_map/ppermute | solution.py:37
  15.1 16.4 %collective-permute-start.2 = (bf16[192,768]{1,0:T(8,128)(2,1)S(1)}, bf16[192,768]{1,0:T(8,128)(2,1)S(1)}, u32[]{:S(2)}, u32[]{:S(2)}) collective-permute-start(bf16[192,768]{1,0:T(8,128)(2,1)S(1)} %get-tuple-element.74.refs_1_.refs_2_), channel_id=1, source_target_pairs={{0,16},{8,24},{16,0},{24,8},{1,17},{9,25},{17,1},{25,9},{2,18},{10... | collective-permute-start | bytes 884744 | tf_op jit(solution)/shard_map/ppermute | solution.py:37
  34.0 28.1 %collective-permute-start.15 = (bf16[768,768]{1,0:T(8,128)(2,1)S(1)}, bf16[768,768]{1,0:T(8,128)(2,1)S(1)}, u32[]{:S(2)}, u32[]{:S(2)}) collective-permute-start(bf16[768,768]{1,0:T(8,128)(2,1)S(1)} %pack.1.refs_1_), channel_id=1, source_target_pairs={{0,16},{8,24},{16,0},{24,8},{1,17},{9,25},{17,1},{25,9},{2,18},{10... | collective-permute-start | bytes 3538952 | tf_op jit(solution)/shard_map/ppermute | solution.py:37
  54.9 25.7 %collective-permute-start.14 = (bf16[768,768]{1,0:T(8,128)(2,1)S(1)}, bf16[768,768]{1,0:T(8,128)(2,1)}, u32[]{:S(2)}, u32[]{:S(2)}) collective-permute-start(bf16[768,768]{1,0:T(8,128)(2,1)S(1)} %pack.1.refs_1_), channel_id=1, source_target_pairs={{0,8},{8,0},{16,24},{24,16},{1,9},{9,1},{17,25},{25,17},{2,10},{10... | collective-permute-start | bytes 3538952 | tf_op jit(solution)/shard_map/ppermute | solution.py:37
  63.1 17.5 %collective-permute-start.16 = (bf16[768,768]{1,0:T(8,128)(2,1)}, bf16[768,768]{1,0:T(8,128)(2,1)}, u32[]{:S(2)}, u32[]{:S(2)}) collective-permute-start(bf16[768,768]{1,0:T(8,128)(2,1)} %gate.4.refs_3_), channel_id=1, source_target_pairs={{0,8},{8,0},{16,24},{24,16},{1,9},{9,1},{17,25},{25,17},{2,10},{10... | collective-permute-start | bytes 3538952 | tf_op jit(solution)/shard_map/ppermute | solution.py:37
  118.3 11.6 %collective-permute-start.23 = (bf16[512,384]{1,0:T(8,128)(2,1)S(1)}, bf16[512,384]{1,0:T(8,128)(2,1)S(1)}, u32[]{:S(2)}, u32[]{:S(2)}) collective-permute-start(bf16[512,384]{1,0:T(8,128)(2,1)S(1)} %get-tuple-element.98), channel_id=1, source_target_pairs={{0,4},{4,0},{1,5},{5,1},{2,6},{6,2},{3,7},{7,3},{8,12},{12,8},{9,1... | collective-permute-start | bytes 1179656 | tf_op jit(solution)/shard_map/ppermute | solution.py:37
  136.3 38.4 %collective-permute-start.37 = (bf16[1,4,192,768]{3,2,1,0:T(8,128)(2,1)S(1)}, bf16[1,4,192,768]{3,2,1,0:T(8,128)(2,1)S(1)}, u32[]{:S(2)}, u32[]{:S(2)}) collective-permute-start(bf16[1,4,192,768]{3,2,1,0:T(8,128)(2,1)S(1)} %get-tuple-element.101.refs_6_.refs_10_), channel_id=1, source_target_pairs={{0,16},{8,24},{16,0},{24,8},{1,17},{9,25},{17,1},{25,9},{2,18},{10... | collective-permute-start | bytes 3538952 | tf_op jit(solution)/shard_map/ppermute | solution.py:37
  142.1 29.3 %collective-permute-start.32 = (bf16[1,192,768]{2,1,0:T(8,128)(2,1)S(1)}, bf16[1,192,768]{2,1,0:T(8,128)(2,1)S(1)}, u32[]{:S(2)}, u32[]{:S(2)}) collective-permute-start(bf16[1,192,768]{2,1,0:T(8,128)(2,1)S(1)} %get-tuple-element.115.refs_10_), channel_id=1, source_target_pairs={{0,16},{8,24},{16,0},{24,8},{1,17},{9,25},{17,1},{25,9},{2,18},{10... | collective-permute-start | bytes 884744 | tf_op jit(solution)/shard_map/ppermute | solution.py:37
  143.5 17.1 %collective-permute-start.26 = (bf16[128,768]{1,0:T(8,128)(2,1)S(1)}, bf16[128,768]{1,0:T(8,128)(2,1)S(1)}, u32[]{:S(2)}, u32[]{:S(2)}) collective-permute-start(bf16[128,768]{1,0:T(8,128)(2,1)S(1)} %copy-done.104), channel_id=1, source_target_pairs={{0,2},{1,3},{2,0},{3,1},{4,6},{5,7},{6,4},{7,5},{8,10},{9,11},{10,... | collective-permute-start | bytes 589832 | tf_op jit(solution)/shard_map/ppermute | solution.py:37
  145.6 15.0 %collective-permute-start.27 = (bf16[128,768]{1,0:T(8,128)(2,1)S(1)}, bf16[128,768]{1,0:T(8,128)(2,1)S(1)}, u32[]{:S(2)}, u32[]{:S(2)}) collective-permute-start(bf16[128,768]{1,0:T(8,128)(2,1)S(1)} %copy-done.102), channel_id=1, source_target_pairs={{0,3},{1,2},{2,1},{3,0},{4,7},{5,6},{6,5},{7,4},{8,11},{9,10},{10,... | collective-permute-start | bytes 589832 | tf_op jit(solution)/shard_map/ppermute | solution.py:37
  153.0 55.7 %collective-permute-start.30 = (bf16[1,208,768]{2,1,0:T(8,128)(2,1)S(1)}, bf16[1,208,768]{2,1,0:T(8,128)(2,1)S(1)}, u32[]{:S(2)}, u32[]{:S(2)}) collective-permute-start(bf16[1,208,768]{2,1,0:T(8,128)(2,1)S(1)} %get-tuple-element.119), channel_id=1, source_target_pairs={{0,16},{8,24},{16,0},{24,8},{1,17},{9,25},{17,1},{25,9},{2,18},{10... | collective-permute-start | bytes 958472 | tf_op jit(solution)/shard_map/ppermute | solution.py:37
  175.5 42.4 %collective-permute-start.38 = (bf16[192,768]{1,0:T(8,128)(2,1)S(1)}, bf16[192,768]{1,0:T(8,128)(2,1)S(1)}, u32[]{:S(2)}, u32[]{:S(2)}) collective-permute-start(bf16[192,768]{1,0:T(8,128)(2,1)S(1)} %get-tuple-element.131), channel_id=1, source_target_pairs={{0,1},{1,0},{2,3},{3,2},{4,5},{5,4},{6,7},{7,6},{8,9},{9,8},{10,11... | collective-permute-start | bytes 884744 | tf_op jit(solution)/shard_map/ppermute | solution.py:37
  176.4 41.5 %collective-permute-start.39 = (bf16[192,768]{1,0:T(8,128)(2,1)S(1)}, bf16[192,768]{1,0:T(8,128)(2,1)S(1)}, u32[]{:S(2)}, u32[]{:S(2)}) collective-permute-start(bf16[192,768]{1,0:T(8,128)(2,1)S(1)} %get-tuple-element.132), channel_id=1, source_target_pairs={{0,2},{1,3},{2,0},{3,1},{4,6},{5,7},{6,4},{7,5},{8,10},{9,11},{10,... | collective-permute-start | bytes 884744 | tf_op jit(solution)/shard_map/ppermute | solution.py:37
  178.5 39.5 %collective-permute-start.40 = (bf16[192,768]{1,0:T(8,128)(2,1)S(1)}, bf16[192,768]{1,0:T(8,128)(2,1)S(1)}, u32[]{:S(2)}, u32[]{:S(2)}) collective-permute-start(bf16[192,768]{1,0:T(8,128)(2,1)S(1)} %get-tuple-element.133), channel_id=1, source_target_pairs={{0,3},{1,2},{2,1},{3,0},{4,7},{5,6},{6,5},{7,4},{8,11},{9,10},{10,... | collective-permute-start | bytes 884744 | tf_op jit(solution)/shard_map/ppermute | solution.py:37
  180.9 14.6 %collective-permute-start.34 = (bf16[96,192]{1,0:T(8,128)(2,1)S(1)}, bf16[96,192]{1,0:T(8,128)(2,1)S(1)}, u32[]{:S(2)}, u32[]{:S(2)}) collective-permute-start(bf16[96,192]{1,0:T(8,128)(2,1)S(1)} %get-tuple-element.126), channel_id=1, source_target_pairs={{0,1},{1,0},{2,3},{3,2},{4,5},{5,4},{6,7},{7,6},{8,9},{9,8},{10,11... | collective-permute-start | bytes 110600 | tf_op jit(solution)/shard_map/ppermute | solution.py:37
  195.5 11.0 %collective-permute-start.35 = (bf16[96,192]{1,0:T(8,128)(2,1)S(1)}, bf16[96,192]{1,0:T(8,128)(2,1)S(1)}, u32[]{:S(2)}, u32[]{:S(2)}) collective-permute-start(bf16[96,192]{1,0:T(8,128)(2,1)S(1)} %get-tuple-element.127), channel_id=1, source_target_pairs={{0,2},{1,3},{2,0},{3,1},{4,6},{5,7},{6,4},{7,5},{8,10},{9,11},{10,... | collective-permute-start | bytes 110600 | tf_op jit(solution)/shard_map/ppermute | solution.py:37
  218.1 12.2 %collective-permute-start.41 = (bf16[192,768]{1,0:T(8,128)(2,1)S(1)}, bf16[192,768]{1,0:T(8,128)(2,1)S(1)}, u32[]{:S(2)}, u32[]{:S(2)}) collective-permute-start(bf16[192,768]{1,0:T(8,128)(2,1)S(1)} %feed_sums.1.refs_1_), channel_id=1, source_target_pairs={{0,1},{1,0},{2,3},{3,2},{4,5},{5,4},{6,7},{7,6},{8,9},{9,8},{10,11... | collective-permute-start | bytes 884744 | tf_op jit(solution)/shard_map/ppermute | solution.py:37
  219.1 28.4 %collective-permute-start.49 = (bf16[192,768]{1,0:T(8,128)(2,1)S(1)}, bf16[192,768]{1,0:T(8,128)(2,1)S(1)}, u32[]{:S(2)}, u32[]{:S(2)}) collective-permute-start(bf16[192,768]{1,0:T(8,128)(2,1)S(1)} %feed_sums.1.refs_1_), channel_id=1, source_target_pairs={{0,2},{1,3},{2,0},{3,1},{4,6},{5,7},{6,4},{7,5},{8,10},{9,11},{10,... | collective-permute-start | bytes 884744 | tf_op jit(solution)/shard_map/ppermute | solution.py:37
  221.6 26.5 %collective-permute-start.50 = (bf16[192,768]{1,0:T(8,128)(2,1)S(1)}, bf16[192,768]{1,0:T(8,128)(2,1)S(1)}, u32[]{:S(2)}, u32[]{:S(2)}) collective-permute-start(bf16[192,768]{1,0:T(8,128)(2,1)S(1)} %feed_sums.1.refs_1_), channel_id=1, source_target_pairs={{0,3},{1,2},{2,1},{3,0},{4,7},{5,6},{6,5},{7,4},{8,11},{9,10},{10,... | collective-permute-start | bytes 884744 | tf_op jit(solution)/shard_map/ppermute | solution.py:37
  231.1 18.4 %collective-permute-start.44 = (bf16[112,768]{1,0:T(8,128)(2,1)}, bf16[112,768]{1,0:T(8,128)(2,1)S(1)}, u32[]{:S(2)}, u32[]{:S(2)}) collective-permute-start(bf16[112,768]{1,0:T(8,128)(2,1)} %gate.7.refs_1_), channel_id=1, source_target_pairs={{0,3},{1,2},{2,1},{3,0},{4,7},{5,6},{6,5},{7,4},{8,11},{9,10},{10,... | collective-permute-start | bytes 516104 | tf_op jit(solution)/shard_map/ppermute | solution.py:37
  238.2 19.8 %collective-permute-start.43 = (bf16[112,768]{1,0:T(8,128)(2,1)}, bf16[112,768]{1,0:T(8,128)(2,1)S(1)}, u32[]{:S(2)}, u32[]{:S(2)}) collective-permute-start(bf16[112,768]{1,0:T(8,128)(2,1)} %gate.7.refs_1_), channel_id=1, source_target_pairs={{0,2},{1,3},{2,0},{3,1},{4,6},{5,7},{6,4},{7,5},{8,10},{9,11},{10,... | collective-permute-start | bytes 516104 | tf_op jit(solution)/shard_map/ppermute | solution.py:37
  238.2 20.4 %collective-permute-start.42 = (bf16[112,768]{1,0:T(8,128)(2,1)}, bf16[112,768]{1,0:T(8,128)(2,1)S(1)}, u32[]{:S(2)}, u32[]{:S(2)}) collective-permute-start(bf16[112,768]{1,0:T(8,128)(2,1)} %gate.7.refs_1_), channel_id=1, source_target_pairs={{0,1},{1,0},{2,3},{3,2},{4,5},{5,4},{6,7},{7,6},{8,9},{9,8},{10,11... | collective-permute-start | bytes 516104 | tf_op jit(solution)/shard_map/ppermute | solution.py:37
  247.5 13.9 %collective-permute-start.51 = (bf16[192,768]{1,0:T(8,128)(2,1)S(1)}, bf16[192,768]{1,0:T(8,128)(2,1)S(1)}, u32[]{:S(2)}, u32[]{:S(2)}) collective-permute-start(bf16[192,768]{1,0:T(8,128)(2,1)S(1)} %feed_sums.1.refs_1_), channel_id=1, source_target_pairs={{0,4},{4,0},{1,5},{5,1},{2,6},{6,2},{3,7},{7,3},{8,12},{12,8},{9,1... | collective-permute-start | bytes 884744 | tf_op jit(solution)/shard_map/ppermute | solution.py:37
  248.1 29.8 %collective-permute-start.45 = (bf16[112,768]{1,0:T(8,128)(2,1)S(1)}, bf16[112,768]{1,0:T(8,128)(2,1)S(1)}, u32[]{:S(2)}, u32[]{:S(2)}) collective-permute-start(bf16[112,768]{1,0:T(8,128)(2,1)S(1)} %copy-done.9), channel_id=1, source_target_pairs={{0,4},{4,0},{1,5},{5,1},{2,6},{6,2},{3,7},{7,3},{8,12},{12,8},{9,1... | collective-permute-start | bytes 516104 | tf_op jit(solution)/shard_map/ppermute | solution.py:37
  249.5 12.4 %collective-permute-start.52 = (bf16[192,768]{1,0:T(8,128)(2,1)S(1)}, bf16[192,768]{1,0:T(8,128)(2,1)S(1)}, u32[]{:S(2)}, u32[]{:S(2)}) collective-permute-start(bf16[192,768]{1,0:T(8,128)(2,1)S(1)} %copy-done.33), channel_id=1, source_target_pairs={{0,4},{4,0},{1,5},{5,1},{2,6},{6,2},{3,7},{7,3},{8,12},{12,8},{9,1... | collective-permute-start | bytes 884744 | tf_op jit(solution)/shard_map/ppermute | solution.py:37
  258.7 15.7 %collective-permute-start.54 = (bf16[192,768]{1,0:T(8,128)(2,1)S(1)}, bf16[192,768]{1,0:T(8,128)(2,1)S(1)}, u32[]{:S(2)}, u32[]{:S(2)}) collective-permute-start(bf16[192,768]{1,0:T(8,128)(2,1)S(1)} %collective-permute-done.50.refs_4_), channel_id=1, source_target_pairs={{0,4},{4,0},{1,5},{5,1},{2,6},{6,2},{3,7},{7,3},{8,12},{12,8},{9,1... | collective-permute-start | bytes 884744 | tf_op jit(solution)/shard_map/ppermute | solution.py:37
  261.3 16.7 %collective-permute-start.46 = (bf16[112,768]{1,0:T(8,128)(2,1)S(1)}, bf16[112,768]{1,0:T(8,128)(2,1)S(1)}, u32[]{:S(2)}, u32[]{:S(2)}) collective-permute-start(bf16[112,768]{1,0:T(8,128)(2,1)S(1)} %collective-permute-done.42.refs_9_.refs_2_), channel_id=1, source_target_pairs={{0,4},{4,0},{1,5},{5,1},{2,6},{6,2},{3,7},{7,3},{8,12},{12,8},{9,1... | collective-permute-start | bytes 516104 | tf_op jit(solution)/shard_map/ppermute | solution.py:37
  261.9 19.1 %collective-permute-start.47 = (bf16[112,768]{1,0:T(8,128)(2,1)S(1)}, bf16[112,768]{1,0:T(8,128)(2,1)S(1)}, u32[]{:S(2)}, u32[]{:S(2)}) collective-permute-start(bf16[112,768]{1,0:T(8,128)(2,1)S(1)} %collective-permute-done.43.refs_10_.refs_3_), channel_id=1, source_target_pairs={{0,4},{4,0},{1,5},{5,1},{2,6},{6,2},{3,7},{7,3},{8,12},{12,8},{9,1... | collective-permute-start | bytes 516104 | tf_op jit(solution)/shard_map/ppermute | solution.py:37
  268.0 14.9 %collective-permute-start.48 = (bf16[112,768]{1,0:T(8,128)(2,1)S(1)}, bf16[112,768]{1,0:T(8,128)(2,1)S(1)}, u32[]{:S(2)}, u32[]{:S(2)}) collective-permute-start(bf16[112,768]{1,0:T(8,128)(2,1)S(1)} %collective-permute-done.44.refs_11_.refs_4_), channel_id=1, source_target_pairs={{0,4},{4,0},{1,5},{5,1},{2,6},{6,2},{3,7},{7,3},{8,12},{12,8},{9,1... | collective-permute-start | bytes 516104 | tf_op jit(solution)/shard_map/ppermute | solution.py:37
  (130 other events, 732.0 us)

commit v4 on v3

--- a/solution.py
+++ b/solution.py
@@ -345,37 +345,35 @@
             ref[i] = (kept_ref[index].astype(F32) + arrived_ref[index].astype(F32)).astype(BF)
 
 
-def chunk_kernel(seqs, place_ref, kept_ref, arrived_ref, *out_refs):
+def chunk_kernel(seqs, blocks, place_ref, kept_ref, arrived_ref, *refs):
+    in_refs, out_refs = refs[:blocks], refs[blocks:]
+    out_grads = sum(ref[...].astype(F32) for ref in in_refs)
+    count, width = out_grads.shape
+    size = width // seqs
+    rows = out_refs[0].shape[0]
     for j in range(seqs):
         index = place_ref[1] ^ j
         total = kept_ref[0, index].astype(F32) + arrived_ref[0, index].astype(F32)
-        out_refs[j][...] = total.astype(BF)
-
-
-def add_kernel(*refs):
-    refs[-1][...] = sum(ref[...].astype(F32) for ref in refs[:-1]).astype(BF)
-
-
-def out_chunks_kernel(blocks, seqs, place_ref, *refs):
-    total = sum(ref[...].astype(F32) for ref in refs[:blocks])
-    size = total.shape[1] // seqs
-    for j in range(seqs):
-        chosen = total[:, :size]
+        out_refs[j][:, :width] = total.astype(BF)
+        chosen = out_grads[:, :size]
         for k in range(1, seqs):
-            columns = total[:, k * size : (k + 1) * size]
-            chosen = jnp.where(place_ref[1] ^ j == k, columns, chosen)
-        refs[blocks + j][...] = chosen.astype(BF)
-
-
-def join_kernel(blocks, seqs, *refs):
-    in_refs, part_refs, out_ref = refs[:blocks], refs[blocks : blocks + seqs], refs[-1]
+            chosen = jnp.where(index == k, out_grads[:, k * size : (k + 1) * size], chosen)
+        out_refs[j][0:count, width:] = chosen.astype(BF)
+        if count < rows:
+            out_refs[j][count:, width:] = jnp.zeros((rows - count, size), BF)
+
+
+def sums_kernel(seqs, blocks, *refs):
+    part_refs, in_refs, (feed_ref, last_ref) = refs[:seqs], refs[seqs:-2], refs[-2:]
+    width = feed_ref.shape[1]
+    total = sum(ref[...].astype(F32) for ref in part_refs)
+    feed_ref[...] = total[:, :width].astype(BF)
     terms = [ref[...].astype(F32) for ref in in_refs]
     while len(terms) > 1:
         terms = [terms[i] + terms[i + 1] for i in range(0, len(terms), 2)]
-    out_ref[...] = terms[0].astype(BF)
-    total = sum(ref[...].astype(F32) for ref in part_refs)
-    size, columns = total.shape
-    out_ref[0:size, 3 * columns :] = total.astype(BF)
+    last_ref[...] = terms[0].astype(BF)
+    size = last_ref.shape[0] - 16
+    last_ref[0:size, 3 * (width // seqs) :] = total[:size, width:].astype(BF)
 
 
 def project_back_kernel(blocks, seqs, *refs):
@@ -512,7 +510,7 @@
                     out[row : row + rows, column : column + size] = piece.astype(F32)
 
 
-def run(kernel, label, outs, scalars, remote, arrays, scratch=(), waits=(), in_hbm=False, cost=1.0, mib=10):
+def run(kernel, label, outs, scalars, remote, arrays, scratch=(), waits=(), cost=1.0, mib=10):
     inputs = len(scalars) + len(remote) + len(arrays)
 
     def without_waits(*refs):
@@ -522,10 +520,10 @@
         without_waits,
         out_shape=tuple(outs),
         in_specs=[pl.BlockSpec(memory_space=pltpu.SMEM)] * len(scalars)
-        + [pl.BlockSpec(memory_space=pl.ANY)] * len(remote)
+        + [pl.BlockSpec(memory_space=pltpu.VMEM)] * len(remote)
         + [pl.BlockSpec(memory_space=pltpu.VMEM)] * len(arrays)
-        + [pl.BlockSpec(memory_space=pl.ANY)] * len(waits),
-        out_specs=(pl.BlockSpec(memory_space=pl.ANY if in_hbm else pltpu.VMEM),) * len(outs),
+        + [pl.BlockSpec(memory_space=pltpu.VMEM)] * len(waits),
+        out_specs=(pl.BlockSpec(memory_space=pltpu.VMEM),) * len(outs),
         scratch_shapes=list(scratch),
         compiler_params=pltpu.CompilerParams(vmem_limit_bytes=mib * 1024 * 1024),
         cost_estimate=pl.CostEstimate(
@@ -539,19 +537,15 @@
     return jax.ShapeDtypeStruct(tuple(dims), kind)
 
 
+def copy_kernel(from_ref, to_ref):
+    to_ref[...] = from_ref[...]
+
+
 def gate(array, waits):
-    def nothing(*refs):
-        pass
-
-    return pl.pallas_call(
-        nothing,
-        out_shape=shape(array.shape, array.dtype),
-        in_specs=[pl.BlockSpec(memory_space=pl.ANY)] * (1 + len(waits)),
-        out_specs=pl.BlockSpec(memory_space=pl.ANY),
-        input_output_aliases={0: 0},
-        cost_estimate=pl.CostEstimate(flops=1, bytes_accessed=1, transcendentals=0),
-        name="gate",
-    )(array, *waits)
+    (result,) = run(
+        copy_kernel, "gate", [shape(array.shape, array.dtype)], [], [], [array], waits=waits
+    )
+    return result
 
 
 def owner_sums(kept, arrived, place, label, waits=()):
@@ -672,7 +666,6 @@
             [],
             [dma((owners + 1,))],
             waits=[key_value, out_pieces[owners // 2]],
-            in_hbm=True,
         )
     else:
         columns = [
@@ -811,6 +804,7 @@
         [],
         [],
         [*d_normed1_pieces, inputs, d_middle, norm_gain],
+        waits=[arrived],
     )
 
     out_blocks = run(
@@ -820,15 +814,14 @@
         [place],
         [],
         [out_kept, out_arrived],
-        waits=[grad_tokens],
     )
     feed_chunks = run(
-        functools.partial(chunk_kernel, seqs),
+        functools.partial(chunk_kernel, seqs, blocks),
         "feed_chunks",
-        [shape((chunk_rows, width), BF)] * seqs,
-        [place],
-        [],
-        [kept, arrived],
+        [shape((chunk_rows, width + head_width), BF)] * seqs,
+        [place],
+        [],
+        [kept, arrived, *sum_parts(out_blocks, "blk")],
         waits=[grad_tokens],
         mib=12,
     )
@@ -854,30 +847,14 @@
         [],
         [last_kept, last_arrived],
     )
-    out_chunks = run(
-        functools.partial(out_chunks_kernel, blocks, seqs),
-        "out_chunks",
-        [shape((blk_rows, head_width), BF)] * seqs,
-        [place],
-        [],
-        sum_parts(out_blocks, "blk"),
-    )
-    (last_sums,) = run(
-        functools.partial(join_kernel, blocks, seqs),
-        "last_sums",
-        [shape((blk_rows + 16, width), BF)],
-        [],
-        [],
-        [*sum_parts(last_blocks, "blk"), *sum_parts(out_chunks, "seq")],
-    )
-    (feed_sums,) = run(
-        add_kernel,
-        "feed_sums",
-        [shape((chunk_rows, width), BF)],
-        [],
-        [],
-        sum_parts(feed_chunks, "seq"),
-        waits=[last_sums, *result_pieces[1:]],
+    feed_sums, last_sums = run(
+        functools.partial(sums_kernel, seqs, blocks),
+        "sums",
+        [shape((chunk_rows, width), BF), shape((blk_rows + 16, width), BF)],
+        [],
+        [],
+        [*sum_parts(feed_chunks, "seq"), *sum_parts(last_blocks, "blk")],
+        waits=result_pieces[1:],
     )
     feed_seq = from_all(feed_sums, "seq")
     last_seq = from_all(gate(last_sums, [feed_seq[1]]), "seq")

time: 291 us -> 281 us (0.966)
  local copies, waits for them, and re-layouts: 38.8 us -> 16.6 us
  waiting for transfers between devices: 129 us -> 143 us
    unnamed x214 -> x112, local copies, waits for them, and re-layouts: 35.5 us -> 13.4 us
    ppermute x55 -> x52, waiting for transfers between devices: 129 us -> 143 us  [swap(): lax.ppermute(array, axis, [(i, i ^ bits) for i in range(lax.axis_size(axi...]
    ppermute x55 -> x52, starting transfers between devices: 65.7 us -> 65.1 us  [swap(): lax.ppermute(array, axis, [(i, i ^ bits) for i in range(lax.axis_size(axi...]
    pallas_call x26 -> x28, Pallas kernels: 49.5 us -> 49.7 us  [run(): pl.pallas_call(without_waits, out_shape=tuple(outs), in_specs=[pl.BlockSp...]
  transfers between devices with their start and end apart: 55 -> 52, of which waited for: 33 -> 31; matrix products, arithmetic and copies ran while one was open for 2% -> 2% of each run, Pallas kernels for 12% -> 12%
where the time goes in v4:
time: 281 us; the launch traced here: 279 us
  waiting for transfers between devices  143 us (51%)
  starting transfers between devices  65.1 us (23%)
  Pallas kernels  49.7 us (18%)
  local copies, waits for them, and re-layouts  16.6 us (6%)
  other arithmetic  3.44 us (1%)
    ppermute x52, waiting for transfers between devices, swap(): lax.ppermute(array, axis, [(i, i ^ bits) for i in range(lax.axis_size(axi...  143 us
    ppermute x52, starting transfers between devices, swap(): lax.ppermute(array, axis, [(i, i ^ bits) for i in range(lax.axis_size(axi...  65.1 us
    pallas_call x28, Pallas kernels, run(): pl.pallas_call(without_waits, out_shape=tuple(outs), in_specs=[pl.BlockSp...  49.7 us
    unnamed x112, local copies, waits for them, and re-layouts  13.4 us
  transfers between devices with their start and end apart: 52, of which 31 were waited for; matrix products, arithmetic and copies ran while one was open for 2% of the time, Pallas kernels for 12%

profile of v4, /device:TPU:0, one launch (start us, length us, event | category | flops | bytes accessed | tf_op | source)
XLA Modules:
  0.0 279.0 jit_solution(9766346744853594801)
XLA Ops:
  5.5 3.0 %collective-permute-start = (bf16[192,576]{1,0:T(8,128)(2,1)S(1)}, bf16[192,576]{1,0:T(8,128)(2,1)S(1)}, u32[]{:S(2)}, u32[]{:S(2)}) collective-permute-start(bf16[192,576]{1,0:T(8,128)(2,1)S(1)} %columns.1.refs_1_), channel_id=1, source_target_pairs={{0,16},{8,24},{16,0},{24,8},{1,17},{9,25},{17,1},{25,9},{2,18},{10... | collective-permute-start | bytes 663560 | tf_op jit(solution)/shard_map/ppermute | solution.py:37
  10.1 2.6 collective-permute-start.7
  16.9 2.7 collective-permute-done.6.refs_6_.refs_5_.refs_2_
  21.8 5.4 %collective-permute-done.7.refs_7_.refs_6_.refs_3_ = bf16[128,768]{1,0:T(8,128)(2,1)S(1)} collective-permute-done((bf16[128,768]{1,0:T(8,128)(2,1)S(1)}, bf16[128,768]{1,0:T(8,128)(2,1)S(1)}, u32[]{:S(2)}, u32[]{:S(2)}) %collective-permute-start.7) | collective-permute-done | bytes 196640 | tf_op jit(solution)/shard_map/ppermute | solution.py:37
  28.7 2.8 project_in.1
  39.4 7.4 %collective-permute-done.10.refs_4_.refs_9_ = bf16[512,384]{1,0:T(8,128)(2,1)S(1)} collective-permute-done((bf16[512,384]{1,0:T(8,128)(2,1)S(1)}, bf16[512,384]{1,0:T(8,128)(2,1)S(1)}, u32[]{:S(2)}, u32[]{:S(2)}) %collective-permute-start.10) | collective-permute-done | bytes 393248 | tf_op jit(solution)/shard_map/ppermute | solution.py:37
  46.8 3.9 %attend.1 = (bf16[128,192]{1,0:T(8,128)(2,1)S(1)}, bf16[128,192]{1,0:T(8,128)(2,1)S(1)}, bf16[128,192]{1,0:T(8,128)(2,1)S(1)}, bf16[128,192]{1,0:T(8,128)(2,1)S(1)}, f32[3,512]{1,0:T(4,128)S(1)}) custom-call(s32[3]{0:T(128)S(1)} %pad_add_fusion.refs_0_, s32[1,8]{1,0:T(1,128)S(1)} %copy-done.54, bf16[512,192]{1,0:T(8,128)(2,1)S(1)} %get-tuple-element.74.refs_2_, ...), custom_call_target="tpu_custom_call" | custom-call | flops 1 | bytes 1560000 | tf_op jit(solution)/shard_map/attend/pallas_call | solution.py:519
  55.4 3.6 %collective-permute-done.12.refs_7_.refs_2_.refs_3_ = bf16[128,192]{1,0:T(8,128)(2,1)S(1)} collective-permute-done((bf16[128,192]{1,0:T(8,128)(2,1)S(1)}, bf16[128,192]{1,0:T(8,128)(2,1)S(1)}, u32[]{:S(2)}, u32[]{:S(2)}) %collective-permute-start.12) | collective-permute-done | bytes 49184 | tf_op jit(solution)/shard_map/ppermute | solution.py:37
  60.0 3.4 %collective-permute-done.15.refs_0_ = bf16[768,768]{1,0:T(8,128)(2,1)S(1)} collective-permute-done((bf16[768,768]{1,0:T(8,128)(2,1)S(1)}, bf16[768,768]{1,0:T(8,128)(2,1)S(1)}, u32[]{:S(2)}, u32[]{:S(2)}) %collective-permute-start.15) | collective-permute-done | bytes 1179680 | tf_op jit(solution)/shard_map/ppermute | solution.py:37
  70.1 4.1 %collective-permute-done.17.refs_6_.refs_2_ = bf16[128,768]{1,0:T(8,128)(2,1)} collective-permute-done((bf16[128,768]{1,0:T(8,128)(2,1)}, bf16[128,768]{1,0:T(8,128)(2,1)}, u32[]{:S(2)}, u32[]{:S(2)}) %collective-permute-start.17) | collective-permute-done | bytes 196640 | tf_op jit(solution)/shard_map/ppermute | solution.py:37
  76.1 6.7 %hidden.1 = (bf16[256,1536]{1,0:T(8,128)(2,1)S(1)}, bf16[256,1536]{1,0:T(8,128)(2,1)S(1)}, f32[1,1536]{1,0:T(1,128)S(1)}, f32[128,768]{1,0:T(8,128)S(1)}, bf16[1...) custom-call(s32[3]{0:T(128)S(1)} %pad_add_fusion.refs_0_, ...), custom_call_target="tpu_custom_call" | custom-call | flops 1 | bytes 2760000 | tf_op jit(solution)/shard_map/hidden/pallas_call | solution.py:519
  85.0 3.9 %feed_grads.1 = (bf16[2,4,192,768]{3,2,1,0:T(8,128)(2,1)S(1)}, bf16[2,4,192,768]{3,2,1,0:T(8,128)(2,1)S(1)}) custom-call(s32[3]{0:T(128)S(1)} %pad_add_fusion.refs_0_, bf16[128,768]{1,0:T(8,128)(2,1)} %get-tuple-element.81.refs_5_.refs_1_, bf16[128,768]{1,0:T(8,128)(2,1)} %collective-permute-done.17.refs_6_.refs_2_, bf16[128,768]{1,0:T(8,128)(2,1)S(1)} %copy-done.33, ...), custom_call_target="tpu_custom_call" | custom-call | flops 1 | bytes 1560000 | tf_op jit(solution)/shard_map/feed_grads/pallas_call | solution.py:519
  96.9 3.3 %collective-permute-done.21.refs_6_.refs_2_ = bf16[128,192]{1,0:T(8,128)(2,1)S(1)} collective-permute-done((bf16[128,192]{1,0:T(8,128)(2,1)S(1)}, bf16[128,192]{1,0:T(8,128)(2,1)S(1)}, u32[]{:S(2)}, u32[]{:S(2)}) %collective-permute-start.21) | collective-permute-done | bytes 49184 | tf_op jit(solution)/shard_map/ppermute | solution.py:37
  101.4 5.7 %attend_back.1 = (bf16[512,192]{1,0:T(8,128)(2,1)S(1)}, f32[512,384]{1,0:T(8,128)S(1)}, bf16[512,384]{1,0:T(8,128)(2,1)S(1)}) custom-call(s32[3]{0:T(128)S(1)} %pad_add_fusion.refs_0_, s32[1,8]{1,0:T(1,128)S(1)} %copy-done.55, bf16[512,192]{1,0:T(8,128)(2,1)S(1)} %copy-done.28, f32[3,512]{1,0:T(4,128)S(1)} %copy-done.52, ...), custom_call_target="tpu_custom_call" | custom-call | flops 1 | bytes 2280000 | tf_op jit(solution)/shard_map/attend_back/pallas_call | solution.py:519
  111.6 7.0 %collective-permute-done.23.refs_2_ = bf16[512,384]{1,0:T(8,128)(2,1)S(1)} collective-permute-done((bf16[512,384]{1,0:T(8,128)(2,1)S(1)}, bf16[512,384]{1,0:T(8,128)(2,1)S(1)}, u32[]{:S(2)}, u32[]{:S(2)}) %collective-permute-start.23) | collective-permute-done | bytes 393248 | tf_op jit(solution)/shard_map/ppermute | solution.py:37
  123.0 2.7 last_grads.1
  128.8 26.2 %collective-permute-done.30.refs_2_ = bf16[1,192,768]{2,1,0:T(8,128)(2,1)S(1)} collective-permute-done((bf16[1,192,768]{2,1,0:T(8,128)(2,1)S(1)}, bf16[1,192,768]{2,1,0:T(8,128)(2,1)S(1)}, u32[]{:S(2)}, u32[]{:S(2)}) %collective-permute-start.30) | collective-permute-done | bytes 294944 | tf_op jit(solution)/shard_map/ppermute | solution.py:37
  160.4 3.0 %collective-permute-done.27.refs_3_ = bf16[128,768]{1,0:T(8,128)(2,1)S(1)} collective-permute-done((bf16[128,768]{1,0:T(8,128)(2,1)S(1)}, bf16[128,768]{1,0:T(8,128)(2,1)S(1)}, u32[]{:S(2)}, u32[]{:S(2)}) %collective-permute-start.27) | collective-permute-done | bytes 196640 | tf_op jit(solution)/shard_map/ppermute | solution.py:37
  166.9 3.4 %collective-permute-start.32 = (bf16[192,960]{1,0:T(8,128)(2,1)S(1)}, bf16[192,960]{1,0:T(8,128)(2,1)S(1)}, u32[]{:S(2)}, u32[]{:S(2)}) collective-permute-start(bf16[192,960]{1,0:T(8,128)(2,1)S(1)} %get-tuple-element.115), channel_id=1, source_target_pairs={{0,1},{1,0},{2,3},{3,2},{4,5},{5,4},{6,7},{7,6},{8,9},{9,8},{10,11... | collective-permute-start | bytes 1105928 | tf_op jit(solution)/shard_map/ppermute | solution.py:37
  175.4 4.1 %collective-permute-done.18.refs_6_ = bf16[128,768]{1,0:T(8,128)(2,1)S(1)} collective-permute-done((bf16[128,768]{1,0:T(8,128)(2,1)S(1)}, bf16[128,768]{1,0:T(8,128)(2,1)S(1)}, u32[]{:S(2)}, u32[]{:S(2)}) %collective-permute-start.18) | collective-permute-done | bytes 196640 | tf_op jit(solution)/shard_map/ppermute | solution.py:37
  179.5 5.8 %collective-permute-done.32.refs_1_ = bf16[192,960]{1,0:T(8,128)(2,1)S(1)} collective-permute-done((bf16[192,960]{1,0:T(8,128)(2,1)S(1)}, bf16[192,960]{1,0:T(8,128)(2,1)S(1)}, u32[]{:S(2)}, u32[]{:S(2)}) %collective-permute-start.32) | collective-permute-done | bytes 368672 | tf_op jit(solution)/shard_map/ppermute | solution.py:37
  185.3 14.7 %collective-permute-done.33.refs_2_ = bf16[192,960]{1,0:T(8,128)(2,1)S(1)} collective-permute-done((bf16[192,960]{1,0:T(8,128)(2,1)S(1)}, bf16[192,960]{1,0:T(8,128)(2,1)S(1)}, u32[]{:S(2)}, u32[]{:S(2)}) %collective-permute-start.33) | collective-permute-done | bytes 368672 | tf_op jit(solution)/shard_map/ppermute | solution.py:37
  200.4 6.5 %collective-permute-start.38 = (bf16[192,768]{1,0:T(8,128)(2,1)S(1)}, bf16[192,768]{1,0:T(8,128)(2,1)S(1)}, u32[]{:S(2)}, u32[]{:S(2)}) collective-permute-start(bf16[192,768]{1,0:T(8,128)(2,1)S(1)} %get-tuple-element.129.refs_1_), channel_id=1, source_target_pairs={{0,1},{1,0},{2,3},{3,2},{4,5},{5,4},{6,7},{7,6},{8,9},{9,8},{10,11... | collective-permute-start | bytes 884744 | tf_op jit(solution)/shard_map/ppermute | solution.py:37
  210.7 5.1 %collective-permute-done.38.refs_1_.refs_2_ = bf16[192,768]{1,0:T(8,128)(2,1)S(1)} collective-permute-done((bf16[192,768]{1,0:T(8,128)(2,1)S(1)}, bf16[192,768]{1,0:T(8,128)(2,1)S(1)}, u32[]{:S(2)}, u32[]{:S(2)}) %collective-permute-start.38) | collective-permute-done | bytes 294944 | tf_op jit(solution)/shard_map/ppermute | solution.py:37
  215.8 3.7 %collective-permute-start.41 = (bf16[112,768]{1,0:T(8,128)(2,1)S(1)}, bf16[112,768]{1,0:T(8,128)(2,1)S(1)}, u32[]{:S(2)}, u32[]{:S(2)}) collective-permute-start(bf16[112,768]{1,0:T(8,128)(2,1)S(1)} %gate.7.refs_1_), channel_id=1, source_target_pairs={{0,3},{1,2},{2,1},{3,0},{4,7},{5,6},{6,5},{7,4},{8,11},{9,10},{10,... | collective-permute-start | bytes 516104 | tf_op jit(solution)/shard_map/ppermute | solution.py:37
  221.1 16.6 %collective-permute-done.46.refs_3_ = bf16[192,768]{1,0:T(8,128)(2,1)S(1)} collective-permute-done((bf16[192,768]{1,0:T(8,128)(2,1)S(1)}, bf16[192,768]{1,0:T(8,128)(2,1)S(1)}, u32[]{:S(2)}, u32[]{:S(2)}) %collective-permute-start.46) | collective-permute-done | bytes 294944 | tf_op jit(solution)/shard_map/ppermute | solution.py:37
  241.2 7.3 %collective-permute-done.40.refs_10_.refs_3_ = bf16[112,768]{1,0:T(8,128)(2,1)S(1)} collective-permute-done((bf16[112,768]{1,0:T(8,128)(2,1)S(1)}, bf16[112,768]{1,0:T(8,128)(2,1)S(1)}, u32[]{:S(2)}, u32[]{:S(2)}) %collective-permute-start.40) | collective-permute-done | bytes 172064 | tf_op jit(solution)/shard_map/ppermute | solution.py:37
  253.8 4.7 %collective-permute-done.50.refs_7_ = bf16[192,768]{1,0:T(8,128)(2,1)S(1)} collective-permute-done((bf16[192,768]{1,0:T(8,128)(2,1)S(1)}, bf16[192,768]{1,0:T(8,128)(2,1)S(1)}, u32[]{:S(2)}, u32[]{:S(2)}) %collective-permute-start.50) | collective-permute-done | bytes 294944 | tf_op jit(solution)/shard_map/ppermute | solution.py:37
  261.1 3.7 %collective-permute-done.51.refs_8_ = bf16[192,768]{1,0:T(8,128)(2,1)S(1)} collective-permute-done((bf16[192,768]{1,0:T(8,128)(2,1)S(1)}, bf16[192,768]{1,0:T(8,128)(2,1)S(1)}, u32[]{:S(2)}, u32[]{:S(2)}) %collective-permute-start.51) | collective-permute-done | bytes 294944 | tf_op jit(solution)/shard_map/ppermute | solution.py:37
  264.8 3.5 %place_feed.1 = (f32[768,768]{1,0:T(8,128)}, f32[192,3072]{1,0:T(8,128)}) custom-call(s32[3]{0:T(128)S(1)} %pad_add_fusion.refs_0_, bf16[192,768]{1,0:T(8,128)(2,1)S(1)} %get-tuple-element.129.refs_1_, bf16[192,768]{1,0:T(8,128)(2,1)S(1)} %collective-permute-done.38.refs_1_.refs_2_, bf16[192,768]{1,0:T(8,128)(2,1)S(1)} %collective-permute-done.46.refs_3_, ...), custom_call_target="tpu_custom_call" | custom-call | flops 1 | bytes 1200000 | tf_op jit(solution)/shard_map/place_feed/pallas_call | solution.py:519
  268.5 2.8 %collective-permute-done.44.refs_7_ = bf16[112,768]{1,0:T(8,128)(2,1)S(1)} collective-permute-done((bf16[112,768]{1,0:T(8,128)(2,1)S(1)}, bf16[112,768]{1,0:T(8,128)(2,1)S(1)}, u32[]{:S(2)}, u32[]{:S(2)}) %collective-permute-start.44) | collective-permute-done | bytes 172064 | tf_op jit(solution)/shard_map/ppermute | solution.py:37
  274.8 4.0 %place_last.1 = (f32[192,2304]{1,0:T(8,128)}, f32[192,768]{1,0:T(8,128)}) custom-call(s32[3]{0:T(128)S(1)} %pad_add_fusion.refs_0_, bf16[112,768]{1,0:T(8,128)(2,1)S(1)} %gate.7.refs_1_, bf16[112,768]{1,0:T(8,128)(2,1)S(1)} %collective-permute-done.39.refs_9_.refs_2_, bf16[112,768]{1,0:T(8,128)(2,1)S(1)} %collective-permute-done.40.refs_10_.refs_3_, ...), custom_call_target="tpu_custom_call" | custom-call | flops 1 | bytes 1200000 | tf_op jit(solution)/shard_map/place_last/pallas_call | solution.py:519
  (233 shorter events, 94.3 us)
Async XLA Ops:
  8.5 18.9 %collective-permute-start.4 = (bf16[192,576]{1,0:T(8,128)(2,1)S(1)}, bf16[192,576]{1,0:T(8,128)(2,1)S(1)}, u32[]{:S(2)}, u32[]{:S(2)}) collective-permute-start(bf16[192,576]{1,0:T(8,128)(2,1)S(1)} %columns.1.refs_1_), channel_id=1, source_target_pairs={{0,8},{8,0},{16,24},{24,16},{1,9},{9,1},{17,25},{25,17},{2,10},{10... | collective-permute-start | bytes 663560 | tf_op jit(solution)/shard_map/ppermute | solution.py:37
  8.5 11.1 %collective-permute-start.6 = (bf16[128,768]{1,0:T(8,128)(2,1)S(1)}, bf16[128,768]{1,0:T(8,128)(2,1)S(1)}, u32[]{:S(2)}, u32[]{:S(2)}) collective-permute-start(bf16[128,768]{1,0:T(8,128)(2,1)S(1)} %first_norm.1.refs_2_.refs_5_.refs_4_.refs_1_), channel_id=1, source_target_pairs={{0,1},{1,0},{2,3},{3,2},{4,5},{5,4},{6,7},{7,6},{8,9},{9,8},{10,11... | collective-permute-start | bytes 589832 | tf_op jit(solution)/shard_map/ppermute | solution.py:37
  10.1 17.1 %collective-permute-start.7 = (bf16[128,768]{1,0:T(8,128)(2,1)S(1)}, bf16[128,768]{1,0:T(8,128)(2,1)S(1)}, u32[]{:S(2)}, u32[]{:S(2)}) collective-permute-start(bf16[128,768]{1,0:T(8,128)(2,1)S(1)} %first_norm.1.refs_2_.refs_5_.refs_4_.refs_1_), channel_id=1, source_target_pairs={{0,2},{1,3},{2,0},{3,1},{4,6},{5,7},{6,4},{7,5},{8,10},{9,11},{10,... | collective-permute-start | bytes 589832 | tf_op jit(solution)/shard_map/ppermute | solution.py:37
  12.7 14.7 %collective-permute-start.8 = (bf16[128,768]{1,0:T(8,128)(2,1)S(1)}, bf16[128,768]{1,0:T(8,128)(2,1)S(1)}, u32[]{:S(2)}, u32[]{:S(2)}) collective-permute-start(bf16[128,768]{1,0:T(8,128)(2,1)S(1)} %first_norm.1.refs_2_.refs_5_.refs_4_.refs_1_), channel_id=1, source_target_pairs={{0,3},{1,2},{2,1},{3,0},{4,7},{5,6},{6,5},{7,4},{8,11},{9,10},{10,... | collective-permute-start | bytes 589832 | tf_op jit(solution)/shard_map/ppermute | solution.py:37
  15.1 16.4 %collective-permute-start.2 = (bf16[192,768]{1,0:T(8,128)(2,1)S(1)}, bf16[192,768]{1,0:T(8,128)(2,1)S(1)}, u32[]{:S(2)}, u32[]{:S(2)}) collective-permute-start(bf16[192,768]{1,0:T(8,128)(2,1)S(1)} %get-tuple-element.72.refs_1_.refs_2_), channel_id=1, source_target_pairs={{0,16},{8,24},{16,0},{24,8},{1,17},{9,25},{17,1},{25,9},{2,18},{10... | collective-permute-start | bytes 884744 | tf_op jit(solution)/shard_map/ppermute | solution.py:37
  35.4 28.1 %collective-permute-start.15 = (bf16[768,768]{1,0:T(8,128)(2,1)S(1)}, bf16[768,768]{1,0:T(8,128)(2,1)S(1)}, u32[]{:S(2)}, u32[]{:S(2)}) collective-permute-start(bf16[768,768]{1,0:T(8,128)(2,1)S(1)} %pack.1.refs_1_), channel_id=1, source_target_pairs={{0,16},{8,24},{16,0},{24,8},{1,17},{9,25},{17,1},{25,9},{2,18},{10... | collective-permute-start | bytes 3538952 | tf_op jit(solution)/shard_map/ppermute | solution.py:37
  35.9 10.9 %collective-permute-start.10 = (bf16[512,384]{1,0:T(8,128)(2,1)S(1)}, bf16[512,384]{1,0:T(8,128)(2,1)S(1)}, u32[]{:S(2)}, u32[]{:S(2)}) collective-permute-start(bf16[512,384]{1,0:T(8,128)(2,1)S(1)} %get-tuple-element.75.refs_3_.refs_8_), channel_id=1, source_target_pairs={{0,4},{4,0},{1,5},{5,1},{2,6},{6,2},{3,7},{7,3},{8,12},{12,8},{9,1... | collective-permute-start | bytes 1179656 | tf_op jit(solution)/shard_map/ppermute | solution.py:37
  55.3 18.9 %collective-permute-start.14 = (bf16[768,768]{1,0:T(8,128)(2,1)S(1)}, bf16[768,768]{1,0:T(8,128)(2,1)}, u32[]{:S(2)}, u32[]{:S(2)}) collective-permute-start(bf16[768,768]{1,0:T(8,128)(2,1)S(1)} %pack.1.refs_1_), channel_id=1, source_target_pairs={{0,8},{8,0},{16,24},{24,16},{1,9},{9,1},{17,25},{25,17},{2,10},{10... | collective-permute-start | bytes 3538952 | tf_op jit(solution)/shard_map/ppermute | solution.py:37
  107.0 11.6 %collective-permute-start.23 = (bf16[512,384]{1,0:T(8,128)(2,1)S(1)}, bf16[512,384]{1,0:T(8,128)(2,1)S(1)}, u32[]{:S(2)}, u32[]{:S(2)}) collective-permute-start(bf16[512,384]{1,0:T(8,128)(2,1)S(1)} %get-tuple-element.96), channel_id=1, source_target_pairs={{0,4},{4,0},{1,5},{5,1},{2,6},{6,2},{3,7},{7,3},{8,12},{12,8},{9,1... | collective-permute-start | bytes 1179656 | tf_op jit(solution)/shard_map/ppermute | solution.py:37
  120.3 43.1 %collective-permute-start.28 = (bf16[1,4,192,768]{3,2,1,0:T(8,128)(2,1)S(1)}, bf16[1,4,192,768]{3,2,1,0:T(8,128)(2,1)S(1)}, u32[]{:S(2)}, u32[]{:S(2)}) collective-permute-start(bf16[1,4,192,768]{3,2,1,0:T(8,128)(2,1)S(1)} %get-tuple-element.99.refs_6_.refs_10_), channel_id=1, source_target_pairs={{0,16},{8,24},{16,0},{24,8},{1,17},{9,25},{17,1},{25,9},{2,18},{10... | collective-permute-start | bytes 3538952 | tf_op jit(solution)/shard_map/ppermute | solution.py:37
  125.7 31.9 %collective-permute-start.35 = (bf16[2,208,768]{2,1,0:T(8,128)(2,1)S(1)}, bf16[2,208,768]{2,1,0:T(8,128)(2,1)S(1)}, u32[]{:S(2)}, u32[]{:S(2)}) collective-permute-start(bf16[2,208,768]{2,1,0:T(8,128)(2,1)S(1)} %get-tuple-element.123), channel_id=1, source_target_pairs={{0,8},{8,0},{16,24},{24,16},{1,9},{9,1},{17,25},{25,17},{2,10},{10... | collective-permute-start | bytes 1916936 | tf_op jit(solution)/shard_map/ppermute | solution.py:37
  125.9 29.2 %collective-permute-start.30 = (bf16[1,192,768]{2,1,0:T(8,128)(2,1)S(1)}, bf16[1,192,768]{2,1,0:T(8,128)(2,1)S(1)}, u32[]{:S(2)}, u32[]{:S(2)}) collective-permute-start(bf16[1,192,768]{2,1,0:T(8,128)(2,1)S(1)} %get-tuple-element.111.refs_10_), channel_id=1, source_target_pairs={{0,16},{8,24},{16,0},{24,8},{1,17},{9,25},{17,1},{25,9},{2,18},{10... | collective-permute-start | bytes 884744 | tf_op jit(solution)/shard_map/ppermute | solution.py:37
  126.3 33.5 %collective-permute-start.25 = (bf16[128,768]{1,0:T(8,128)(2,1)S(1)}, bf16[128,768]{1,0:T(8,128)(2,1)S(1)}, u32[]{:S(2)}, u32[]{:S(2)}) collective-permute-start(bf16[128,768]{1,0:T(8,128)(2,1)S(1)} %get-tuple-element.103), channel_id=1, source_target_pairs={{0,1},{1,0},{2,3},{3,2},{4,5},{5,4},{6,7},{7,6},{8,9},{9,8},{10,11... | collective-permute-start | bytes 589832 | tf_op jit(solution)/shard_map/ppermute | solution.py:37
  127.4 33.1 %collective-permute-start.26 = (bf16[128,768]{1,0:T(8,128)(2,1)S(1)}, bf16[128,768]{1,0:T(8,128)(2,1)S(1)}, u32[]{:S(2)}, u32[]{:S(2)}) collective-permute-start(bf16[128,768]{1,0:T(8,128)(2,1)S(1)} %get-tuple-element.104), channel_id=1, source_target_pairs={{0,2},{1,3},{2,0},{3,1},{4,6},{5,7},{6,4},{7,5},{8,10},{9,11},{10,... | collective-permute-start | bytes 589832 | tf_op jit(solution)/shard_map/ppermute | solution.py:37
  159.8 14.3 %collective-permute-start.36 = (bf16[1,208,768]{2,1,0:T(8,128)(2,1)S(1)}, bf16[1,208,768]{2,1,0:T(8,128)(2,1)S(1)}, u32[]{:S(2)}, u32[]{:S(2)}) collective-permute-start(bf16[1,208,768]{2,1,0:T(8,128)(2,1)S(1)} %get-tuple-element.125), channel_id=1, source_target_pairs={{0,16},{8,24},{16,0},{24,8},{1,17},{9,25},{17,1},{25,9},{2,18},{10... | collective-permute-start | bytes 958472 | tf_op jit(solution)/shard_map/ppermute | solution.py:37
  166.9 18.4 %collective-permute-start.32 = (bf16[192,960]{1,0:T(8,128)(2,1)S(1)}, bf16[192,960]{1,0:T(8,128)(2,1)S(1)}, u32[]{:S(2)}, u32[]{:S(2)}) collective-permute-start(bf16[192,960]{1,0:T(8,128)(2,1)S(1)} %get-tuple-element.115), channel_id=1, source_target_pairs={{0,1},{1,0},{2,3},{3,2},{4,5},{5,4},{6,7},{7,6},{8,9},{9,8},{10,11... | collective-permute-start | bytes 1105928 | tf_op jit(solution)/shard_map/ppermute | solution.py:37
  170.2 29.8 %collective-permute-start.33 = (bf16[192,960]{1,0:T(8,128)(2,1)S(1)}, bf16[192,960]{1,0:T(8,128)(2,1)S(1)}, u32[]{:S(2)}, u32[]{:S(2)}) collective-permute-start(bf16[192,960]{1,0:T(8,128)(2,1)S(1)} %get-tuple-element.116), channel_id=1, source_target_pairs={{0,2},{1,3},{2,0},{3,1},{4,6},{5,7},{6,4},{7,5},{8,10},{9,11},{10,... | collective-permute-start | bytes 1105928 | tf_op jit(solution)/shard_map/ppermute | solution.py:37
  171.0 29.0 %collective-permute-start.34 = (bf16[192,960]{1,0:T(8,128)(2,1)S(1)}, bf16[192,960]{1,0:T(8,128)(2,1)S(1)}, u32[]{:S(2)}, u32[]{:S(2)}) collective-permute-start(bf16[192,960]{1,0:T(8,128)(2,1)S(1)} %get-tuple-element.117), channel_id=1, source_target_pairs={{0,3},{1,2},{2,1},{3,0},{4,7},{5,6},{6,5},{7,4},{8,11},{9,10},{10,... | collective-permute-start | bytes 1105928 | tf_op jit(solution)/shard_map/ppermute | solution.py:37
  174.8 25.3 %collective-permute-start.37 = (bf16[112,768]{1,0:T(8,128)(2,1)S(1)}, bf16[112,768]{1,0:T(8,128)(2,1)S(1)}, u32[]{:S(2)}, u32[]{:S(2)}) collective-permute-start(bf16[112,768]{1,0:T(8,128)(2,1)S(1)} %get-tuple-element.127), channel_id=1, source_target_pairs={{0,4},{4,0},{1,5},{5,1},{2,6},{6,2},{3,7},{7,3},{8,12},{12,8},{9,1... | collective-permute-start | bytes 516104 | tf_op jit(solution)/shard_map/ppermute | solution.py:37
  200.4 15.4 %collective-permute-start.38 = (bf16[192,768]{1,0:T(8,128)(2,1)S(1)}, bf16[192,768]{1,0:T(8,128)(2,1)S(1)}, u32[]{:S(2)}, u32[]{:S(2)}) collective-permute-start(bf16[192,768]{1,0:T(8,128)(2,1)S(1)} %get-tuple-element.129.refs_1_), channel_id=1, source_target_pairs={{0,1},{1,0},{2,3},{3,2},{4,5},{5,4},{6,7},{7,6},{8,9},{9,8},{10,11... | collective-permute-start | bytes 884744 | tf_op jit(solution)/shard_map/ppermute | solution.py:37
  207.6 30.2 %collective-permute-start.46 = (bf16[192,768]{1,0:T(8,128)(2,1)S(1)}, bf16[192,768]{1,0:T(8,128)(2,1)S(1)}, u32[]{:S(2)}, u32[]{:S(2)}) collective-permute-start(bf16[192,768]{1,0:T(8,128)(2,1)S(1)} %get-tuple-element.129.refs_1_), channel_id=1, source_target_pairs={{0,2},{1,3},{2,0},{3,1},{4,6},{5,7},{6,4},{7,5},{8,10},{9,11},{10,... | collective-permute-start | bytes 884744 | tf_op jit(solution)/shard_map/ppermute | solution.py:37
  208.5 30.7 %collective-permute-start.47 = (bf16[192,768]{1,0:T(8,128)(2,1)S(1)}, bf16[192,768]{1,0:T(8,128)(2,1)S(1)}, u32[]{:S(2)}, u32[]{:S(2)}) collective-permute-start(bf16[192,768]{1,0:T(8,128)(2,1)S(1)} %get-tuple-element.129.refs_1_), channel_id=1, source_target_pairs={{0,3},{1,2},{2,1},{3,0},{4,7},{5,6},{6,5},{7,4},{8,11},{9,10},{10,... | collective-permute-start | bytes 884744 | tf_op jit(solution)/shard_map/ppermute | solution.py:37
  215.8 23.9 %collective-permute-start.41 = (bf16[112,768]{1,0:T(8,128)(2,1)S(1)}, bf16[112,768]{1,0:T(8,128)(2,1)S(1)}, u32[]{:S(2)}, u32[]{:S(2)}) collective-permute-start(bf16[112,768]{1,0:T(8,128)(2,1)S(1)} %gate.7.refs_1_), channel_id=1, source_target_pairs={{0,3},{1,2},{2,1},{3,0},{4,7},{5,6},{6,5},{7,4},{8,11},{9,10},{10,... | collective-permute-start | bytes 516104 | tf_op jit(solution)/shard_map/ppermute | solution.py:37
  219.5 29.0 %collective-permute-start.40 = (bf16[112,768]{1,0:T(8,128)(2,1)S(1)}, bf16[112,768]{1,0:T(8,128)(2,1)S(1)}, u32[]{:S(2)}, u32[]{:S(2)}) collective-permute-start(bf16[112,768]{1,0:T(8,128)(2,1)S(1)} %gate.7.refs_1_), channel_id=1, source_target_pairs={{0,2},{1,3},{2,0},{3,1},{4,6},{5,7},{6,4},{7,5},{8,10},{9,11},{10,... | collective-permute-start | bytes 516104 | tf_op jit(solution)/shard_map/ppermute | solution.py:37
  219.5 30.4 %collective-permute-start.39 = (bf16[112,768]{1,0:T(8,128)(2,1)S(1)}, bf16[112,768]{1,0:T(8,128)(2,1)S(1)}, u32[]{:S(2)}, u32[]{:S(2)}) collective-permute-start(bf16[112,768]{1,0:T(8,128)(2,1)S(1)} %gate.7.refs_1_), channel_id=1, source_target_pairs={{0,1},{1,0},{2,3},{3,2},{4,5},{5,4},{6,7},{7,6},{8,9},{9,8},{10,11... | collective-permute-start | bytes 516104 | tf_op jit(solution)/shard_map/ppermute | solution.py:37
  237.7 14.0 %collective-permute-start.48 = (bf16[192,768]{1,0:T(8,128)(2,1)S(1)}, bf16[192,768]{1,0:T(8,128)(2,1)S(1)}, u32[]{:S(2)}, u32[]{:S(2)}) collective-permute-start(bf16[192,768]{1,0:T(8,128)(2,1)S(1)} %get-tuple-element.129.refs_1_), channel_id=1, source_target_pairs={{0,4},{4,0},{1,5},{5,1},{2,6},{6,2},{3,7},{7,3},{8,12},{12,8},{9,1... | collective-permute-start | bytes 884744 | tf_op jit(solution)/shard_map/ppermute | solution.py:37
  239.2 29.1 %collective-permute-start.42 = (bf16[112,768]{1,0:T(8,128)(2,1)S(1)}, bf16[112,768]{1,0:T(8,128)(2,1)S(1)}, u32[]{:S(2)}, u32[]{:S(2)}) collective-permute-start(bf16[112,768]{1,0:T(8,128)(2,1)S(1)} %gate.7.refs_1_), channel_id=1, source_target_pairs={{0,4},{4,0},{1,5},{5,1},{2,6},{6,2},{3,7},{7,3},{8,12},{12,8},{9,1... | collective-permute-start | bytes 516104 | tf_op jit(solution)/shard_map/ppermute | solution.py:37
  239.8 13.5 %collective-permute-start.49 = (bf16[192,768]{1,0:T(8,128)(2,1)S(1)}, bf16[192,768]{1,0:T(8,128)(2,1)S(1)}, u32[]{:S(2)}, u32[]{:S(2)}) collective-permute-start(bf16[192,768]{1,0:T(8,128)(2,1)S(1)} %collective-permute-done.38.refs_1_.refs_2_), channel_id=1, source_target_pairs={{0,4},{4,0},{1,5},{5,1},{2,6},{6,2},{3,7},{7,3},{8,12},{12,8},{9,1... | collective-permute-start | bytes 884744 | tf_op jit(solution)/shard_map/ppermute | solution.py:37
  250.0 14.8 %collective-permute-start.51 = (bf16[192,768]{1,0:T(8,128)(2,1)S(1)}, bf16[192,768]{1,0:T(8,128)(2,1)S(1)}, u32[]{:S(2)}, u32[]{:S(2)}) collective-permute-start(bf16[192,768]{1,0:T(8,128)(2,1)S(1)} %collective-permute-done.47.refs_4_), channel_id=1, source_target_pairs={{0,4},{4,0},{1,5},{5,1},{2,6},{6,2},{3,7},{7,3},{8,12},{12,8},{9,1... | collective-permute-start | bytes 884744 | tf_op jit(solution)/shard_map/ppermute | solution.py:37
  251.8 16.7 %collective-permute-start.43 = (bf16[112,768]{1,0:T(8,128)(2,1)S(1)}, bf16[112,768]{1,0:T(8,128)(2,1)S(1)}, u32[]{:S(2)}, u32[]{:S(2)}) collective-permute-start(bf16[112,768]{1,0:T(8,128)(2,1)S(1)} %collective-permute-done.39.refs_9_.refs_2_), channel_id=1, source_target_pairs={{0,4},{4,0},{1,5},{5,1},{2,6},{6,2},{3,7},{7,3},{8,12},{12,8},{9,1... | collective-permute-start | bytes 516104 | tf_op jit(solution)/shard_map/ppermute | solution.py:37
  253.2 18.1 %collective-permute-start.44 = (bf16[112,768]{1,0:T(8,128)(2,1)S(1)}, bf16[112,768]{1,0:T(8,128)(2,1)S(1)}, u32[]{:S(2)}, u32[]{:S(2)}) collective-permute-start(bf16[112,768]{1,0:T(8,128)(2,1)S(1)} %collective-permute-done.40.refs_10_.refs_3_), channel_id=1, source_target_pairs={{0,4},{4,0},{1,5},{5,1},{2,6},{6,2},{3,7},{7,3},{8,12},{12,8},{9,1... | collective-permute-start | bytes 516104 | tf_op jit(solution)/shard_map/ppermute | solution.py:37
  258.5 14.7 %collective-permute-start.45 = (bf16[112,768]{1,0:T(8,128)(2,1)S(1)}, bf16[112,768]{1,0:T(8,128)(2,1)S(1)}, u32[]{:S(2)}, u32[]{:S(2)}) collective-permute-start(bf16[112,768]{1,0:T(8,128)(2,1)S(1)} %collective-permute-done.41.refs_11_.refs_4_), channel_id=1, source_target_pairs={{0,4},{4,0},{1,5},{5,1},{2,6},{6,2},{3,7},{7,3},{8,12},{12,8},{9,1... | collective-permute-start | bytes 516104 | tf_op jit(solution)/shard_map/ppermute | solution.py:37
  (76 other events, 571.2 us)

commit v5 on v4

--- a/solution.py
+++ b/solution.py
@@ -364,16 +364,16 @@
 
 
 def sums_kernel(seqs, blocks, *refs):
-    part_refs, in_refs, (feed_ref, last_ref) = refs[:seqs], refs[seqs:-2], refs[-2:]
-    width = feed_ref.shape[1]
+    part_refs, in_refs, out_ref = refs[:seqs], refs[seqs:-1], refs[-1]
+    width = out_ref.shape[1]
     total = sum(ref[...].astype(F32) for ref in part_refs)
-    feed_ref[...] = total[:, :width].astype(BF)
+    base, size = total.shape[0], in_refs[0].shape[0] - 16
+    out_ref[0:base, :] = total[:, :width].astype(BF)
     terms = [ref[...].astype(F32) for ref in in_refs]
     while len(terms) > 1:
         terms = [terms[i] + terms[i + 1] for i in range(0, len(terms), 2)]
-    last_ref[...] = terms[0].astype(BF)
-    size = last_ref.shape[0] - 16
-    last_ref[0:size, 3 * (width // seqs) :] = total[:size, width:].astype(BF)
+    out_ref[base:, :] = terms[0].astype(BF)
+    out_ref[base : base + size, 3 * (width // seqs) :] = total[:size, width:].astype(BF)
 
 
 def project_back_kernel(blocks, seqs, *refs):
@@ -793,9 +793,6 @@
         waits=[feed_sent, out_sent],
         mib=16,
     )
-    out_kept, out_arrived, out_step = owner_sums(
-        out_kept, swap(gate(out_sent, [column_sums]), "fsdp", 1), place, "out_step"
-    )
     d_normed1_pieces = sum_parts(d_normed1, "seq")
     (grad_tokens,) = run(
         functools.partial(first_back_kernel, seqs),
@@ -807,6 +804,9 @@
         waits=[arrived],
     )
 
+    out_kept, out_arrived, out_step = owner_sums(
+        out_kept, swap(gate(out_sent, [column_sums]), "fsdp", 1), place, "out_step", waits=[grad_tokens]
+    )
     out_blocks = run(
         functools.partial(block_kernel, blocks, 0),
         "out_blocks",
@@ -833,7 +833,6 @@
         [place],
         [],
         [*normed1_pieces, d_projected, column_sums, first_sums, middle_sums, up_sums],
-        waits=[out_step],
         mib=16,
     )
     last_kept, last_arrived, _ = owner_sums(
@@ -847,24 +846,23 @@
         [],
         [last_kept, last_arrived],
     )
-    feed_sums, last_sums = run(
+    (all_sums,) = run(
         functools.partial(sums_kernel, seqs, blocks),
         "sums",
-        [shape((chunk_rows, width), BF), shape((blk_rows + 16, width), BF)],
+        [shape((chunk_rows + blk_rows + 16, width), BF)],
         [],
         [],
         [*sum_parts(feed_chunks, "seq"), *sum_parts(last_blocks, "blk")],
         waits=result_pieces[1:],
     )
-    feed_seq = from_all(feed_sums, "seq")
-    last_seq = from_all(gate(last_sums, [feed_seq[1]]), "seq")
+    sums_seq = from_all(all_sums, "seq")
     outcome = sum(one.astype(F32) for one in result_pieces)
     valid = lax.broadcasted_iota(jnp.int32, (rows, 1), 0) < counts[0, blk * seqs + seq]
     activations = jnp.where(valid, middle + outcome + biases[3], 0.0)
 
-    feed_all = [from_all(one, "blk") for one in feed_seq]
-    last_all = [from_all(one, "blk") for one in last_seq]
-    grad_down, grad_up = run(
+    sums_all = [from_all(one, "blk") for one in sums_seq]
+    base = chunk_rows
+    grad_down, grad_up, grad_qkv, grad_w_out = run(
         functools.partial(
             place_kernel,
             seqs,
@@ -882,26 +880,9 @@
                     )
                     for i in range(owners)
                 ],
-            ],
-        ),
-        "place_feed",
-        [shape((blocks * hidden_rows, width), F32), shape((own_rows, blocks * hidden_width), F32)],
-        [place],
-        [feed_all[k][m] for m in range(blocks) for k in range(seqs)],
-        [],
-        [vmem((blocks, seqs, chunk_rows, width), BF), dma((blocks * seqs,))],
-        waits=last_seq[1:],
-        mib=24,
-    )
-    grad_qkv, grad_w_out = run(
-        functools.partial(
-            place_kernel,
-            seqs,
-            blocks,
-            [
                 lambda b, k: [
                     (
-                        0,
+                        base,
                         blk_rows,
                         i * head_width,
                         head_width,
@@ -910,19 +891,23 @@
                     )
                     for i in range(3)
                 ],
-                lambda b, k: [(0, blk_rows, third, head_width, b * blk_rows, k * head_width)],
+                lambda b, k: [(base, blk_rows, third, head_width, b * blk_rows, k * head_width)],
             ],
         ),
-        "place_last",
-        [shape((own_rows, 3 * width), F32), shape((own_rows, width), F32)],
-        [place],
-        [last_all[k][m] for m in range(blocks) for k in range(seqs)],
-        [],
-        [vmem((blocks, seqs, blk_rows + 16, width), BF), dma((blocks * seqs,))],
-        waits=[grad_down],
-        mib=20,
-    )
-    small = tree_sum([one[blk_rows:] for one in last_seq])
+        "place",
+        [
+            shape((blocks * hidden_rows, width), F32),
+            shape((own_rows, blocks * hidden_width), F32),
+            shape((own_rows, 3 * width), F32),
+            shape((own_rows, width), F32),
+        ],
+        [place],
+        [sums_all[k][m] for m in range(blocks) for k in range(seqs)],
+        [],
+        [vmem((blocks, seqs, base + blk_rows + 16, width), BF), dma((blocks * seqs,))],
+        mib=36,
+    )
+    small = tree_sum([one[base + blk_rows :] for one in sums_seq])
     lines = small[:8, :own_rows]
     return (
         activations[None],

time: 281 us -> 280 us (level)
  waiting for transfers between devices: 143 us -> 152 us
  starting transfers between devices: 65.1 us -> 58.5 us
    ppermute x52 -> x45, waiting for transfers between devices: 143 us -> 152 us  [swap(): lax.ppermute(array, axis, [(i, i ^ bits) for i in range(lax.axis_size(axi...]
    ppermute x52 -> x45, starting transfers between devices: 65.1 us -> 58.5 us  [swap(): lax.ppermute(array, axis, [(i, i ^ bits) for i in range(lax.axis_size(axi...]
    pallas_call x28 -> x26, Pallas kernels: 49.7 us -> 49.8 us  [run(): pl.pallas_call(without_waits, out_shape=tuple(outs), in_specs=[pl.BlockSp...]
  transfers between devices with their start and end apart: 52 -> 45, of which waited for: 31 -> 30; matrix products, arithmetic and copies ran while one was open for 2% -> 2% of each run, Pallas kernels for 12% -> 11%
where the time goes in v5:
time: 280 us
  waiting for transfers between devices  152 us (54%)
  starting transfers between devices  58.5 us (21%)
  Pallas kernels  49.8 us (18%)
  local copies, waits for them, and re-layouts  15 us (5%)
  other arithmetic  3.45 us (1%)
    ppermute x45, waiting for transfers between devices, swap(): lax.ppermute(array, axis, [(i, i ^ bits) for i in range(lax.axis_size(axi...  152 us
    ppermute x45, starting transfers between devices, swap(): lax.ppermute(array, axis, [(i, i ^ bits) for i in range(lax.axis_size(axi...  58.5 us
    pallas_call x26, Pallas kernels, run(): pl.pallas_call(without_waits, out_shape=tuple(outs), in_specs=[pl.BlockSp...  49.8 us
    unnamed x112, local copies, waits for them, and re-layouts  11.7 us
  transfers between devices with their start and end apart: 45, of which 30 were waited for; matrix products, arithmetic and copies ran while one was open for 2% of the time, Pallas kernels for 11%

profile of v5, /device:TPU:0, one launch (start us, length us, event | category | flops | bytes accessed | tf_op | source)
XLA Modules:
  0.0 279.9 jit_solution(15482772286376631643)
XLA Ops:
  5.5 3.0 %collective-permute-start = (bf16[192,576]{1,0:T(8,128)(2,1)S(1)}, bf16[192,576]{1,0:T(8,128)(2,1)S(1)}, u32[]{:S(2)}, u32[]{:S(2)}) collective-permute-start(bf16[192,576]{1,0:T(8,128)(2,1)S(1)} %columns.1.refs_1_), channel_id=1, source_target_pairs={{0,16},{8,24},{16,0},{24,8},{1,17},{9,25},{17,1},{25,9},{2,18},{10... | collective-permute-start | bytes 663560 | tf_op jit(solution)/shard_map/ppermute | solution.py:37
  10.1 2.6 collective-permute-start.7
  16.9 2.7 collective-permute-done.6.refs_6_.refs_5_.refs_2_
  21.8 5.4 %collective-permute-done.7.refs_7_.refs_6_.refs_3_ = bf16[128,768]{1,0:T(8,128)(2,1)S(1)} collective-permute-done((bf16[128,768]{1,0:T(8,128)(2,1)S(1)}, bf16[128,768]{1,0:T(8,128)(2,1)S(1)}, u32[]{:S(2)}, u32[]{:S(2)}) %collective-permute-start.7) | collective-permute-done | bytes 196640 | tf_op jit(solution)/shard_map/ppermute | solution.py:37
  28.7 2.8 project_in.1
  39.4 7.4 %collective-permute-done.10.refs_4_.refs_9_ = bf16[512,384]{1,0:T(8,128)(2,1)S(1)} collective-permute-done((bf16[512,384]{1,0:T(8,128)(2,1)S(1)}, bf16[512,384]{1,0:T(8,128)(2,1)S(1)}, u32[]{:S(2)}, u32[]{:S(2)}) %collective-permute-start.10) | collective-permute-done | bytes 393248 | tf_op jit(solution)/shard_map/ppermute | solution.py:37
  46.8 3.9 %attend.1 = (bf16[128,192]{1,0:T(8,128)(2,1)S(1)}, bf16[128,192]{1,0:T(8,128)(2,1)S(1)}, bf16[128,192]{1,0:T(8,128)(2,1)S(1)}, bf16[128,192]{1,0:T(8,128)(2,1)S(1)}, f32[3,512]{1,0:T(4,128)S(1)}) custom-call(s32[3]{0:T(128)S(1)} %pad_add_fusion.refs_0_, s32[1,8]{1,0:T(1,128)S(1)} %copy-done.54, bf16[512,192]{1,0:T(8,128)(2,1)S(1)} %get-tuple-element.72.refs_2_, ...), custom_call_target="tpu_custom_call" | custom-call | flops 1 | bytes 1560000 | tf_op jit(solution)/shard_map/attend/pallas_call | solution.py:519
  55.4 3.6 %collective-permute-done.12.refs_7_.refs_2_.refs_3_ = bf16[128,192]{1,0:T(8,128)(2,1)S(1)} collective-permute-done((bf16[128,192]{1,0:T(8,128)(2,1)S(1)}, bf16[128,192]{1,0:T(8,128)(2,1)S(1)}, u32[]{:S(2)}, u32[]{:S(2)}) %collective-permute-start.12) | collective-permute-done | bytes 49184 | tf_op jit(solution)/shard_map/ppermute | solution.py:37
  60.0 3.4 %collective-permute-done.15.refs_0_ = bf16[768,768]{1,0:T(8,128)(2,1)S(1)} collective-permute-done((bf16[768,768]{1,0:T(8,128)(2,1)S(1)}, bf16[768,768]{1,0:T(8,128)(2,1)S(1)}, u32[]{:S(2)}, u32[]{:S(2)}) %collective-permute-start.15) | collective-permute-done | bytes 1179680 | tf_op jit(solution)/shard_map/ppermute | solution.py:37
  63.7 2.1 project_out.1
  70.1 4.1 %collective-permute-done.17.refs_6_.refs_2_ = bf16[128,768]{1,0:T(8,128)(2,1)} collective-permute-done((bf16[128,768]{1,0:T(8,128)(2,1)}, bf16[128,768]{1,0:T(8,128)(2,1)}, u32[]{:S(2)}, u32[]{:S(2)}) %collective-permute-start.17) | collective-permute-done | bytes 196640 | tf_op jit(solution)/shard_map/ppermute | solution.py:37
  76.0 7.4 %hidden.1 = (bf16[256,1536]{1,0:T(8,128)(2,1)S(1)}, bf16[256,1536]{1,0:T(8,128)(2,1)S(1)}, f32[1,1536]{1,0:T(1,128)S(1)}, f32[128,768]{1,0:T(8,128)S(1)}, bf16[1...) custom-call(s32[3]{0:T(128)S(1)} %pad_add_fusion.refs_0_, ...), custom_call_target="tpu_custom_call" | custom-call | flops 1 | bytes 2760000 | tf_op jit(solution)/shard_map/hidden/pallas_call | solution.py:519
  85.7 3.8 %feed_grads.1 = (bf16[2,4,192,768]{3,2,1,0:T(8,128)(2,1)S(1)}, bf16[2,4,192,768]{3,2,1,0:T(8,128)(2,1)S(1)}) custom-call(s32[3]{0:T(128)S(1)} %pad_add_fusion.refs_0_, bf16[128,768]{1,0:T(8,128)(2,1)} %get-tuple-element.79.refs_5_.refs_1_, bf16[128,768]{1,0:T(8,128)(2,1)} %collective-permute-done.17.refs_6_.refs_2_, bf16[128,768]{1,0:T(8,128)(2,1)S(1)} %copy-done.33, ...), custom_call_target="tpu_custom_call" | custom-call | flops 1 | bytes 1560000 | tf_op jit(solution)/shard_map/feed_grads/pallas_call | solution.py:519
  97.5 3.3 %collective-permute-done.21.refs_6_.refs_2_ = bf16[128,192]{1,0:T(8,128)(2,1)S(1)} collective-permute-done((bf16[128,192]{1,0:T(8,128)(2,1)S(1)}, bf16[128,192]{1,0:T(8,128)(2,1)S(1)}, u32[]{:S(2)}, u32[]{:S(2)}) %collective-permute-start.21) | collective-permute-done | bytes 49184 | tf_op jit(solution)/shard_map/ppermute | solution.py:37
  102.0 5.7 %attend_back.1 = (bf16[512,192]{1,0:T(8,128)(2,1)S(1)}, f32[512,384]{1,0:T(8,128)S(1)}, bf16[512,384]{1,0:T(8,128)(2,1)S(1)}) custom-call(s32[3]{0:T(128)S(1)} %pad_add_fusion.refs_0_, s32[1,8]{1,0:T(1,128)S(1)} %copy-done.55, bf16[512,192]{1,0:T(8,128)(2,1)S(1)} %copy-done.28, f32[3,512]{1,0:T(4,128)S(1)} %copy-done.52, ...), custom_call_target="tpu_custom_call" | custom-call | flops 1 | bytes 2280000 | tf_op jit(solution)/shard_map/attend_back/pallas_call | solution.py:519
  112.8 7.9 %collective-permute-done.23.refs_2_ = bf16[512,384]{1,0:T(8,128)(2,1)S(1)} collective-permute-done((bf16[512,384]{1,0:T(8,128)(2,1)S(1)}, bf16[512,384]{1,0:T(8,128)(2,1)S(1)}, u32[]{:S(2)}, u32[]{:S(2)}) %collective-permute-start.23) | collective-permute-done | bytes 393248 | tf_op jit(solution)/shard_map/ppermute | solution.py:37
  123.5 2.7 last_grads.1
  131.6 11.7 %collective-permute-done.26.refs_2_ = bf16[128,768]{1,0:T(8,128)(2,1)S(1)} collective-permute-done((bf16[128,768]{1,0:T(8,128)(2,1)S(1)}, bf16[128,768]{1,0:T(8,128)(2,1)S(1)}, u32[]{:S(2)}, u32[]{:S(2)}) %collective-permute-start.26) | collective-permute-done | bytes 196640 | tf_op jit(solution)/shard_map/ppermute | solution.py:37
  147.8 6.5 %collective-permute-done.30.refs_2_ = bf16[1,192,768]{2,1,0:T(8,128)(2,1)S(1)} collective-permute-done((bf16[1,192,768]{2,1,0:T(8,128)(2,1)S(1)}, bf16[1,192,768]{2,1,0:T(8,128)(2,1)S(1)}, u32[]{:S(2)}, u32[]{:S(2)}) %collective-permute-start.30) | collective-permute-done | bytes 294944 | tf_op jit(solution)/shard_map/ppermute | solution.py:37
  160.1 2.0 feed_chunks.1
  162.1 4.8 %collective-permute-start.32 = (bf16[192,960]{1,0:T(8,128)(2,1)}, bf16[192,960]{1,0:T(8,128)(2,1)S(1)}, u32[]{:S(2)}, u32[]{:S(2)}) collective-permute-start(bf16[192,960]{1,0:T(8,128)(2,1)} %get-tuple-element.113), channel_id=1, source_target_pairs={{0,1},{1,0},{2,3},{3,2},{4,5},{5,4},{6,7},{7,6},{8,9},{9,8},{10,11... | collective-permute-start | bytes 1105928 | tf_op jit(solution)/shard_map/ppermute | solution.py:37
  172.6 2.7 collective-permute-done.18.refs_6_
  177.2 3.4 %collective-permute-done.32.refs_1_ = bf16[192,960]{1,0:T(8,128)(2,1)S(1)} collective-permute-done((bf16[192,960]{1,0:T(8,128)(2,1)}, bf16[192,960]{1,0:T(8,128)(2,1)S(1)}, u32[]{:S(2)}, u32[]{:S(2)}) %collective-permute-start.32) | collective-permute-done | bytes 368672 | tf_op jit(solution)/shard_map/ppermute | solution.py:37
  180.6 21.1 %collective-permute-done.33.refs_2_ = bf16[192,960]{1,0:T(8,128)(2,1)S(1)} collective-permute-done((bf16[192,960]{1,0:T(8,128)(2,1)S(1)}, bf16[192,960]{1,0:T(8,128)(2,1)S(1)}, u32[]{:S(2)}, u32[]{:S(2)}) %collective-permute-start.33) | collective-permute-done | bytes 368672 | tf_op jit(solution)/shard_map/ppermute | solution.py:37
  202.0 2.4 collective-permute-start.40
  204.5 4.7 %collective-permute-start.39 = (bf16[304,768]{1,0:T(8,128)(2,1)S(1)}, bf16[304,768]{1,0:T(8,128)(2,1)S(1)}, u32[]{:S(2)}, u32[]{:S(2)}) collective-permute-start(bf16[304,768]{1,0:T(8,128)(2,1)S(1)} %sums.1.refs_1_), channel_id=1, source_target_pairs={{0,2},{1,3},{2,0},{3,1},{4,6},{5,7},{6,4},{7,5},{8,10},{9,11},{10,... | collective-permute-start | bytes 1400840 | tf_op jit(solution)/shard_map/ppermute | solution.py:37
  212.4 4.3 %collective-permute-done.40.refs_4_ = bf16[304,768]{1,0:T(8,128)(2,1)S(1)} collective-permute-done((bf16[304,768]{1,0:T(8,128)(2,1)S(1)}, bf16[304,768]{1,0:T(8,128)(2,1)S(1)}, u32[]{:S(2)}, u32[]{:S(2)}) %collective-permute-start.40) | collective-permute-done | bytes 466976 | tf_op jit(solution)/shard_map/ppermute | solution.py:37
  216.7 24.7 %collective-permute-done.39.refs_3_ = bf16[304,768]{1,0:T(8,128)(2,1)S(1)} collective-permute-done((bf16[304,768]{1,0:T(8,128)(2,1)S(1)}, bf16[304,768]{1,0:T(8,128)(2,1)S(1)}, u32[]{:S(2)}, u32[]{:S(2)}) %collective-permute-start.39) | collective-permute-done | bytes 466976 | tf_op jit(solution)/shard_map/ppermute | solution.py:37
  247.3 8.3 %collective-permute-done.42.refs_6_ = bf16[304,768]{1,0:T(8,128)(2,1)S(1)} collective-permute-done((bf16[304,768]{1,0:T(8,128)(2,1)S(1)}, bf16[304,768]{1,0:T(8,128)(2,1)S(1)}, u32[]{:S(2)}, u32[]{:S(2)}) %collective-permute-start.42) | collective-permute-done | bytes 466976 | tf_op jit(solution)/shard_map/ppermute | solution.py:37
  255.6 10.0 %collective-permute-done.43.refs_7_ = bf16[304,768]{1,0:T(8,128)(2,1)S(1)} collective-permute-done((bf16[304,768]{1,0:T(8,128)(2,1)S(1)}, bf16[304,768]{1,0:T(8,128)(2,1)S(1)}, u32[]{:S(2)}, u32[]{:S(2)}) %collective-permute-start.43) | collective-permute-done | bytes 466976 | tf_op jit(solution)/shard_map/ppermute | solution.py:37
  265.6 7.8 %collective-permute-done.44.refs_8_ = bf16[304,768]{1,0:T(8,128)(2,1)S(1)} collective-permute-done((bf16[304,768]{1,0:T(8,128)(2,1)S(1)}, bf16[304,768]{1,0:T(8,128)(2,1)S(1)}, u32[]{:S(2)}, u32[]{:S(2)}) %collective-permute-start.44) | collective-permute-done | bytes 466976 | tf_op jit(solution)/shard_map/ppermute | solution.py:37
  273.5 6.3 %place.1 = (f32[768,768]{1,0:T(8,128)}, f32[192,3072]{1,0:T(8,128)}, f32[192,2304]{1,0:T(8,128)}, f32[192,768]{1,0:T(8,128)}) custom-call(s32[3]{0:T(128)S(1)} %pad_add_fusion.refs_0_, bf16[304,768]{1,0:T(8,128)(2,1)S(1)} %sums.1.refs_1_, bf16[304,768]{1,0:T(8,128)(2,1)S(1)} %collective-permute-done.38.refs_2_, ...), custom_call_target="tpu_custom_call" | custom-call | flops 1 | bytes 1200000 | tf_op jit(solution)/shard_map/place/pallas_call | solution.py:519
  (217 shorter events, 85.9 us)
Async XLA Ops:
  5.5 9.0 %collective-permute-start = (bf16[192,576]{1,0:T(8,128)(2,1)S(1)}, bf16[192,576]{1,0:T(8,128)(2,1)S(1)}, u32[]{:S(2)}, u32[]{:S(2)}) collective-permute-start(bf16[192,576]{1,0:T(8,128)(2,1)S(1)} %columns.1.refs_1_), channel_id=1, source_target_pairs={{0,16},{8,24},{16,0},{24,8},{1,17},{9,25},{17,1},{25,9},{2,18},{10... | collective-permute-start | bytes 663560 | tf_op jit(solution)/shard_map/ppermute | solution.py:37
  8.5 18.9 %collective-permute-start.4 = (bf16[192,576]{1,0:T(8,128)(2,1)S(1)}, bf16[192,576]{1,0:T(8,128)(2,1)S(1)}, u32[]{:S(2)}, u32[]{:S(2)}) collective-permute-start(bf16[192,576]{1,0:T(8,128)(2,1)S(1)} %columns.1.refs_1_), channel_id=1, source_target_pairs={{0,8},{8,0},{16,24},{24,16},{1,9},{9,1},{17,25},{25,17},{2,10},{10... | collective-permute-start | bytes 663560 | tf_op jit(solution)/shard_map/ppermute | solution.py:37
  8.5 11.1 %collective-permute-start.6 = (bf16[128,768]{1,0:T(8,128)(2,1)S(1)}, bf16[128,768]{1,0:T(8,128)(2,1)S(1)}, u32[]{:S(2)}, u32[]{:S(2)}) collective-permute-start(bf16[128,768]{1,0:T(8,128)(2,1)S(1)} %first_norm.1.refs_2_.refs_5_.refs_4_.refs_1_), channel_id=1, source_target_pairs={{0,1},{1,0},{2,3},{3,2},{4,5},{5,4},{6,7},{7,6},{8,9},{9,8},{10,11... | collective-permute-start | bytes 589832 | tf_op jit(solution)/shard_map/ppermute | solution.py:37
  10.1 17.1 %collective-permute-start.7 = (bf16[128,768]{1,0:T(8,128)(2,1)S(1)}, bf16[128,768]{1,0:T(8,128)(2,1)S(1)}, u32[]{:S(2)}, u32[]{:S(2)}) collective-permute-start(bf16[128,768]{1,0:T(8,128)(2,1)S(1)} %first_norm.1.refs_2_.refs_5_.refs_4_.refs_1_), channel_id=1, source_target_pairs={{0,2},{1,3},{2,0},{3,1},{4,6},{5,7},{6,4},{7,5},{8,10},{9,11},{10,... | collective-permute-start | bytes 589832 | tf_op jit(solution)/shard_map/ppermute | solution.py:37
  12.7 14.7 %collective-permute-start.8 = (bf16[128,768]{1,0:T(8,128)(2,1)S(1)}, bf16[128,768]{1,0:T(8,128)(2,1)S(1)}, u32[]{:S(2)}, u32[]{:S(2)}) collective-permute-start(bf16[128,768]{1,0:T(8,128)(2,1)S(1)} %first_norm.1.refs_2_.refs_5_.refs_4_.refs_1_), channel_id=1, source_target_pairs={{0,3},{1,2},{2,1},{3,0},{4,7},{5,6},{6,5},{7,4},{8,11},{9,10},{10,... | collective-permute-start | bytes 589832 | tf_op jit(solution)/shard_map/ppermute | solution.py:37
  15.1 16.4 %collective-permute-start.2 = (bf16[192,768]{1,0:T(8,128)(2,1)S(1)}, bf16[192,768]{1,0:T(8,128)(2,1)S(1)}, u32[]{:S(2)}, u32[]{:S(2)}) collective-permute-start(bf16[192,768]{1,0:T(8,128)(2,1)S(1)} %get-tuple-element.70.refs_1_.refs_2_), channel_id=1, source_target_pairs={{0,16},{8,24},{16,0},{24,8},{1,17},{9,25},{17,1},{25,9},{2,18},{10... | collective-permute-start | bytes 884744 | tf_op jit(solution)/shard_map/ppermute | solution.py:37
  19.6 7.8 %collective-permute-start.9 = (bf16[128,768]{1,0:T(8,128)(2,1)S(1)}, bf16[128,768]{1,0:T(8,128)(2,1)S(1)}, u32[]{:S(2)}, u32[]{:S(2)}) collective-permute-start(bf16[128,768]{1,0:T(8,128)(2,1)S(1)} %get-tuple-element.71.refs_7_.refs_3_), channel_id=1, source_target_pairs={{0,4},{4,0},{1,5},{5,1},{2,6},{6,2},{3,7},{7,3},{8,12},{12,8},{9,1... | collective-permute-start | bytes 589832 | tf_op jit(solution)/shard_map/ppermute | solution.py:37
  35.4 28.1 %collective-permute-start.15 = (bf16[768,768]{1,0:T(8,128)(2,1)S(1)}, bf16[768,768]{1,0:T(8,128)(2,1)S(1)}, u32[]{:S(2)}, u32[]{:S(2)}) collective-permute-start(bf16[768,768]{1,0:T(8,128)(2,1)S(1)} %pack.1.refs_1_), channel_id=1, source_target_pairs={{0,16},{8,24},{16,0},{24,8},{1,17},{9,25},{17,1},{25,9},{2,18},{10... | collective-permute-start | bytes 3538952 | tf_op jit(solution)/shard_map/ppermute | solution.py:37
  35.9 10.9 %collective-permute-start.10 = (bf16[512,384]{1,0:T(8,128)(2,1)S(1)}, bf16[512,384]{1,0:T(8,128)(2,1)S(1)}, u32[]{:S(2)}, u32[]{:S(2)}) collective-permute-start(bf16[512,384]{1,0:T(8,128)(2,1)S(1)} %get-tuple-element.73.refs_3_.refs_8_), channel_id=1, source_target_pairs={{0,4},{4,0},{1,5},{5,1},{2,6},{6,2},{3,7},{7,3},{8,12},{12,8},{9,1... | collective-permute-start | bytes 1179656 | tf_op jit(solution)/shard_map/ppermute | solution.py:37
  55.3 18.9 %collective-permute-start.14 = (bf16[768,768]{1,0:T(8,128)(2,1)S(1)}, bf16[768,768]{1,0:T(8,128)(2,1)}, u32[]{:S(2)}, u32[]{:S(2)}) collective-permute-start(bf16[768,768]{1,0:T(8,128)(2,1)S(1)} %pack.1.refs_1_), channel_id=1, source_target_pairs={{0,8},{8,0},{16,24},{24,16},{1,9},{9,1},{17,25},{25,17},{2,10},{10... | collective-permute-start | bytes 3538952 | tf_op jit(solution)/shard_map/ppermute | solution.py:37
  63.5 10.6 %collective-permute-start.16 = (bf16[768,768]{1,0:T(8,128)(2,1)S(1)}, bf16[768,768]{1,0:T(8,128)(2,1)}, u32[]{:S(2)}, u32[]{:S(2)}) collective-permute-start(bf16[768,768]{1,0:T(8,128)(2,1)S(1)} %gate.3.refs_3_), channel_id=1, source_target_pairs={{0,8},{8,0},{16,24},{24,16},{1,9},{9,1},{17,25},{25,17},{2,10},{10... | collective-permute-start | bytes 3538952 | tf_op jit(solution)/shard_map/ppermute | solution.py:37
  66.6 7.6 %collective-permute-start.17 = (bf16[128,768]{1,0:T(8,128)(2,1)}, bf16[128,768]{1,0:T(8,128)(2,1)}, u32[]{:S(2)}, u32[]{:S(2)}) collective-permute-start(bf16[128,768]{1,0:T(8,128)(2,1)} %get-tuple-element.79.refs_5_.refs_1_), channel_id=1, source_target_pairs={{0,4},{4,0},{1,5},{5,1},{2,6},{6,2},{3,7},{7,3},{8,12},{12,8},{9,1... | collective-permute-start | bytes 589832 | tf_op jit(solution)/shard_map/ppermute | solution.py:37
  84.2 6.5 %collective-permute-start.19 = (bf16[128,768]{1,0:T(8,128)(2,1)S(1)}, bf16[128,768]{1,0:T(8,128)(2,1)S(1)}, u32[]{:S(2)}, u32[]{:S(2)}) collective-permute-start(bf16[128,768]{1,0:T(8,128)(2,1)S(1)} %get-tuple-element.84), channel_id=1, source_target_pairs={{0,4},{4,0},{1,5},{5,1},{2,6},{6,2},{3,7},{7,3},{8,12},{12,8},{9,1... | collective-permute-start | bytes 589832 | tf_op jit(solution)/shard_map/ppermute | solution.py:37
  108.9 34.4 %collective-permute-start.28 = (bf16[1,4,192,768]{3,2,1,0:T(8,128)(2,1)S(1)}, bf16[1,4,192,768]{3,2,1,0:T(8,128)(2,1)S(1)}, u32[]{:S(2)}, u32[]{:S(2)}) collective-permute-start(bf16[1,4,192,768]{3,2,1,0:T(8,128)(2,1)S(1)} %get-tuple-element.97.refs_6_.refs_10_), channel_id=1, source_target_pairs={{0,16},{8,24},{16,0},{24,8},{1,17},{9,25},{17,1},{25,9},{2,18},{10... | collective-permute-start | bytes 3538952 | tf_op jit(solution)/shard_map/ppermute | solution.py:37
  109.5 11.2 %collective-permute-start.23 = (bf16[512,384]{1,0:T(8,128)(2,1)S(1)}, bf16[512,384]{1,0:T(8,128)(2,1)S(1)}, u32[]{:S(2)}, u32[]{:S(2)}) collective-permute-start(bf16[512,384]{1,0:T(8,128)(2,1)S(1)} %get-tuple-element.94), channel_id=1, source_target_pairs={{0,4},{4,0},{1,5},{5,1},{2,6},{6,2},{3,7},{7,3},{8,12},{12,8},{9,1... | collective-permute-start | bytes 1179656 | tf_op jit(solution)/shard_map/ppermute | solution.py:37
  122.4 22.1 %collective-permute-start.29 = (bf16[2,192,768]{2,1,0:T(8,128)(2,1)S(1)}, bf16[2,192,768]{2,1,0:T(8,128)(2,1)S(1)}, u32[]{:S(2)}, u32[]{:S(2)}) collective-permute-start(bf16[2,192,768]{2,1,0:T(8,128)(2,1)S(1)} %gate.5), channel_id=1, source_target_pairs={{0,8},{8,0},{16,24},{24,16},{1,9},{9,1},{17,25},{25,17},{2,10},{10... | collective-permute-start | bytes 1769480 | tf_op jit(solution)/shard_map/ppermute | solution.py:37
  122.4 7.3 %collective-permute-start.25 = (bf16[128,768]{1,0:T(8,128)(2,1)S(1)}, bf16[128,768]{1,0:T(8,128)(2,1)S(1)}, u32[]{:S(2)}, u32[]{:S(2)}) collective-permute-start(bf16[128,768]{1,0:T(8,128)(2,1)S(1)} %get-tuple-element.101), channel_id=1, source_target_pairs={{0,1},{1,0},{2,3},{3,2},{4,5},{5,4},{6,7},{7,6},{8,9},{9,8},{10,11... | collective-permute-start | bytes 589832 | tf_op jit(solution)/shard_map/ppermute | solution.py:37
  126.1 30.3 %collective-permute-start.35 = (bf16[2,208,768]{2,1,0:T(8,128)(2,1)S(1)}, bf16[2,208,768]{2,1,0:T(8,128)(2,1)S(1)}, u32[]{:S(2)}, u32[]{:S(2)}) collective-permute-start(bf16[2,208,768]{2,1,0:T(8,128)(2,1)S(1)} %get-tuple-element.121), channel_id=1, source_target_pairs={{0,8},{8,0},{16,24},{24,16},{1,9},{9,1},{17,25},{25,17},{2,10},{10... | collective-permute-start | bytes 1916936 | tf_op jit(solution)/shard_map/ppermute | solution.py:37
  126.3 17.0 %collective-permute-start.26 = (bf16[128,768]{1,0:T(8,128)(2,1)S(1)}, bf16[128,768]{1,0:T(8,128)(2,1)S(1)}, u32[]{:S(2)}, u32[]{:S(2)}) collective-permute-start(bf16[128,768]{1,0:T(8,128)(2,1)S(1)} %get-tuple-element.102), channel_id=1, source_target_pairs={{0,2},{1,3},{2,0},{3,1},{4,6},{5,7},{6,4},{7,5},{8,10},{9,11},{10,... | collective-permute-start | bytes 589832 | tf_op jit(solution)/shard_map/ppermute | solution.py:37
  129.7 13.6 %collective-permute-start.27 = (bf16[128,768]{1,0:T(8,128)(2,1)S(1)}, bf16[128,768]{1,0:T(8,128)(2,1)S(1)}, u32[]{:S(2)}, u32[]{:S(2)}) collective-permute-start(bf16[128,768]{1,0:T(8,128)(2,1)S(1)} %get-tuple-element.103), channel_id=1, source_target_pairs={{0,3},{1,2},{2,1},{3,0},{4,7},{5,6},{6,5},{7,4},{8,11},{9,10},{10,... | collective-permute-start | bytes 589832 | tf_op jit(solution)/shard_map/ppermute | solution.py:37
  146.2 8.0 %collective-permute-start.30 = (bf16[1,192,768]{2,1,0:T(8,128)(2,1)S(1)}, bf16[1,192,768]{2,1,0:T(8,128)(2,1)S(1)}, u32[]{:S(2)}, u32[]{:S(2)}) collective-permute-start(bf16[1,192,768]{2,1,0:T(8,128)(2,1)S(1)} %get-tuple-element.109), channel_id=1, source_target_pairs={{0,16},{8,24},{16,0},{24,8},{1,17},{9,25},{17,1},{25,9},{2,18},{10... | collective-permute-start | bytes 884744 | tf_op jit(solution)/shard_map/ppermute | solution.py:37
  157.1 13.6 %collective-permute-start.36 = (bf16[1,208,768]{2,1,0:T(8,128)(2,1)S(1)}, bf16[1,208,768]{2,1,0:T(8,128)(2,1)S(1)}, u32[]{:S(2)}, u32[]{:S(2)}) collective-permute-start(bf16[1,208,768]{2,1,0:T(8,128)(2,1)S(1)} %get-tuple-element.123), channel_id=1, source_target_pairs={{0,16},{8,24},{16,0},{24,8},{1,17},{9,25},{17,1},{25,9},{2,18},{10... | collective-permute-start | bytes 958472 | tf_op jit(solution)/shard_map/ppermute | solution.py:37
  162.1 18.5 %collective-permute-start.32 = (bf16[192,960]{1,0:T(8,128)(2,1)}, bf16[192,960]{1,0:T(8,128)(2,1)S(1)}, u32[]{:S(2)}, u32[]{:S(2)}) collective-permute-start(bf16[192,960]{1,0:T(8,128)(2,1)} %get-tuple-element.113), channel_id=1, source_target_pairs={{0,1},{1,0},{2,3},{3,2},{4,5},{5,4},{6,7},{7,6},{8,9},{9,8},{10,11... | collective-permute-start | bytes 1105928 | tf_op jit(solution)/shard_map/ppermute | solution.py:37
  166.9 34.8 %collective-permute-start.33 = (bf16[192,960]{1,0:T(8,128)(2,1)S(1)}, bf16[192,960]{1,0:T(8,128)(2,1)S(1)}, u32[]{:S(2)}, u32[]{:S(2)}) collective-permute-start(bf16[192,960]{1,0:T(8,128)(2,1)S(1)} %get-tuple-element.114), channel_id=1, source_target_pairs={{0,2},{1,3},{2,0},{3,1},{4,6},{5,7},{6,4},{7,5},{8,10},{9,11},{10,... | collective-permute-start | bytes 1105928 | tf_op jit(solution)/shard_map/ppermute | solution.py:37
  167.8 33.9 %collective-permute-start.34 = (bf16[192,960]{1,0:T(8,128)(2,1)S(1)}, bf16[192,960]{1,0:T(8,128)(2,1)S(1)}, u32[]{:S(2)}, u32[]{:S(2)}) collective-permute-start(bf16[192,960]{1,0:T(8,128)(2,1)S(1)} %get-tuple-element.115), channel_id=1, source_target_pairs={{0,3},{1,2},{2,1},{3,0},{4,7},{5,6},{6,5},{7,4},{8,11},{9,10},{10,... | collective-permute-start | bytes 1105928 | tf_op jit(solution)/shard_map/ppermute | solution.py:37
  202.0 14.7 %collective-permute-start.40 = (bf16[304,768]{1,0:T(8,128)(2,1)S(1)}, bf16[304,768]{1,0:T(8,128)(2,1)S(1)}, u32[]{:S(2)}, u32[]{:S(2)}) collective-permute-start(bf16[304,768]{1,0:T(8,128)(2,1)S(1)} %sums.1.refs_1_), channel_id=1, source_target_pairs={{0,3},{1,2},{2,1},{3,0},{4,7},{5,6},{6,5},{7,4},{8,11},{9,10},{10,... | collective-permute-start | bytes 1400840 | tf_op jit(solution)/shard_map/ppermute | solution.py:37
  204.5 36.9 %collective-permute-start.39 = (bf16[304,768]{1,0:T(8,128)(2,1)S(1)}, bf16[304,768]{1,0:T(8,128)(2,1)S(1)}, u32[]{:S(2)}, u32[]{:S(2)}) collective-permute-start(bf16[304,768]{1,0:T(8,128)(2,1)S(1)} %sums.1.refs_1_), channel_id=1, source_target_pairs={{0,2},{1,3},{2,0},{3,1},{4,6},{5,7},{6,4},{7,5},{8,10},{9,11},{10,... | collective-permute-start | bytes 1400840 | tf_op jit(solution)/shard_map/ppermute | solution.py:37
  209.1 32.3 %collective-permute-start.38 = (bf16[304,768]{1,0:T(8,128)(2,1)S(1)}, bf16[304,768]{1,0:T(8,128)(2,1)S(1)}, u32[]{:S(2)}, u32[]{:S(2)}) collective-permute-start(bf16[304,768]{1,0:T(8,128)(2,1)S(1)} %sums.1.refs_1_), channel_id=1, source_target_pairs={{0,1},{1,0},{2,3},{3,2},{4,5},{5,4},{6,7},{7,6},{8,9},{9,8},{10,11... | collective-permute-start | bytes 1400840 | tf_op jit(solution)/shard_map/ppermute | solution.py:37
  210.9 36.4 %collective-permute-start.41 = (bf16[304,768]{1,0:T(8,128)(2,1)S(1)}, bf16[304,768]{1,0:T(8,128)(2,1)S(1)}, u32[]{:S(2)}, u32[]{:S(2)}) collective-permute-start(bf16[304,768]{1,0:T(8,128)(2,1)S(1)} %sums.1.refs_1_), channel_id=1, source_target_pairs={{0,4},{4,0},{1,5},{5,1},{2,6},{6,2},{3,7},{7,3},{8,12},{12,8},{9,1... | collective-permute-start | bytes 1400840 | tf_op jit(solution)/shard_map/ppermute | solution.py:37
  242.0 13.6 %collective-permute-start.42 = (bf16[304,768]{1,0:T(8,128)(2,1)S(1)}, bf16[304,768]{1,0:T(8,128)(2,1)S(1)}, u32[]{:S(2)}, u32[]{:S(2)}) collective-permute-start(bf16[304,768]{1,0:T(8,128)(2,1)S(1)} %collective-permute-done.38.refs_2_), channel_id=1, source_target_pairs={{0,4},{4,0},{1,5},{5,1},{2,6},{6,2},{3,7},{7,3},{8,12},{12,8},{9,1... | collective-permute-start | bytes 1400840 | tf_op jit(solution)/shard_map/ppermute | solution.py:37
  243.5 22.1 %collective-permute-start.43 = (bf16[304,768]{1,0:T(8,128)(2,1)S(1)}, bf16[304,768]{1,0:T(8,128)(2,1)S(1)}, u32[]{:S(2)}, u32[]{:S(2)}) collective-permute-start(bf16[304,768]{1,0:T(8,128)(2,1)S(1)} %collective-permute-done.39.refs_3_), channel_id=1, source_target_pairs={{0,4},{4,0},{1,5},{5,1},{2,6},{6,2},{3,7},{7,3},{8,12},{12,8},{9,1... | collective-permute-start | bytes 1400840 | tf_op jit(solution)/shard_map/ppermute | solution.py:37
  244.0 29.4 %collective-permute-start.44 = (bf16[304,768]{1,0:T(8,128)(2,1)S(1)}, bf16[304,768]{1,0:T(8,128)(2,1)S(1)}, u32[]{:S(2)}, u32[]{:S(2)}) collective-permute-start(bf16[304,768]{1,0:T(8,128)(2,1)S(1)} %collective-permute-done.40.refs_4_), channel_id=1, source_target_pairs={{0,4},{4,0},{1,5},{5,1},{2,6},{6,2},{3,7},{7,3},{8,12},{12,8},{9,1... | collective-permute-start | bytes 1400840 | tf_op jit(solution)/shard_map/ppermute | solution.py:37
  (69 other events, 505.9 us)
